TPU v7x, 128 devices: a whole 4x4x4 slice. The times are simulated.
128 devices in a mesh: section: 4 (over z_lo, core), seq: 32 (over z_hi, y, x).
Axes of the slice: x: 4, y: 4, z: 4 (z_hi: 2, z_lo: 2; z = z_hi * 2 + z_lo), core: 2. Of those that a mesh axis runs over, the one named last changes fastest.
Arguments:
- tokens: bfloat16 [4, 1024, 6144], P('section', 'seq'), may hold values from -6 to 6
- mod_shift: float32 [4, 6144], P('section'), may hold values from -0.5 to 0.5
- mod_scale: float32 [4, 6144], P('section'), may hold values from -0.5 to 0.5
- mod_gate: float32 [4, 6144], P('section'), may hold values from 0.5 to 1.5
- w_query: bfloat16 [4, 6144, 4096], P('section', None, 'seq'), may hold values from -1 to 1
- w_key: bfloat16 [4, 6144, 4096], P('section', None, 'seq'), may hold values from -0.078125 to 0.078125
- w_value: bfloat16 [4, 6144, 4096], P('section', None, 'seq'), may hold values from -0.078125 to 0.078125
- w_out: bfloat16 [4, 4096, 6144], P('section', 'seq'), may hold values from -0.09375 to 0.09375
- stale_keys: bfloat16 [4, 13312, 4096], P('section', 'seq'), may hold values from -410 to 410
- stale_values: bfloat16 [4, 13312, 4096], P('section', 'seq'), may hold values from -6 to 6
- patch_index: int32 [4], P('section'), may hold values from 0 to 12
Outputs:
- forwarded: bfloat16 [4, 1024, 6144], P('section', 'seq')
All inputs are finite; a program needn't handle non-finite values.
Results may differ from a plain program's by a relative error of at most 0.011.
Values may be sent and summed in bfloat16 or wider, within the bound.
No kernel may reach another device: no remote copies, remote signals or barrier semaphores. Data moves between devices by JAX's collectives and lax.ppermute only.
A program may use at most 192 MiB of HBM per device.

v0:
```python
import jax
import jax.numpy as jnp
from jax import lax
from jax.sharding import PartitionSpec as P

HD = 128


def from_behind(value, axis, steps):
    count = lax.axis_size(axis)
    pairs = [(source, (source + steps) % count) for source in range(count)]
    return lax.ppermute(value, axis, pairs)


def body(
    tokens,
    mod_shift,
    mod_scale,
    mod_gate,
    w_query,
    w_key,
    w_value,
    w_out,
    stale_keys,
    stale_values,
    patch_index,
):
    inputs = tokens[0].astype(jnp.float32)
    meansq = jnp.mean(inputs * inputs, axis=-1, keepdims=True)
    normed = (inputs * lax.rsqrt(meansq + 1e-06) * (1.0 + mod_scale[0]) + mod_shift[0]).astype(
        jnp.bfloat16
    )
    local = w_query.shape[2]
    w_joint = jnp.concatenate((w_query[0], w_key[0], w_value[0]), axis=1)
    joint = jnp.dot(
        lax.all_gather(normed, "seq", axis=0, tiled=True),
        w_joint,
        preferred_element_type=jnp.float32,
    ).astype(jnp.bfloat16)
    query = joint[:, :local]
    keyed = joint[:, local : 2 * local]
    valued = joint[:, 2 * local :]
    keys_all = lax.all_to_all(stale_keys[0], "seq", split_axis=1, concat_axis=0, tiled=True)
    values_all = lax.all_to_all(stale_values[0], "seq", split_axis=1, concat_axis=0, tiled=True)
    patch = joint.shape[0]
    total = keys_all.shape[0]
    offset = patch_index[0] * patch
    anchor = jnp.zeros((), jnp.int32)
    keys_all = lax.dynamic_update_slice(keys_all, keyed, (offset, anchor))
    values_all = lax.dynamic_update_slice(values_all, valued, (offset, anchor))
    count_heads = local // HD
    query_heads = query.reshape(patch, count_heads, HD)
    key_heads = keys_all.reshape(total, count_heads, HD)
    value_heads = values_all.reshape(total, count_heads, HD)
    scores = jnp.einsum(
        "qhd,khd->hqk", query_heads, key_heads, preferred_element_type=jnp.float32
    ) / jnp.sqrt(jnp.float32(HD))
    probs = jax.nn.softmax(scores, axis=-1).astype(jnp.bfloat16)
    attended = jnp.einsum(
        "hqk,khd->qhd", probs, value_heads, preferred_element_type=jnp.float32
    ).astype(jnp.bfloat16)
    attended = attended.reshape(patch, local)
    projected = lax.psum_scatter(
        jnp.dot(attended, w_out[0], preferred_element_type=jnp.float32).astype(jnp.bfloat16),
        "seq",
        scatter_dimension=0,
        tiled=True,
    ).astype(jnp.float32)
    updated = (inputs + mod_gate[0] * projected).astype(jnp.bfloat16)
    return from_behind(updated[None], "section", 1)


def solution(mesh):
    placed = (
        P("section", "seq", None),
        P("section", None),
        P("section", None),
        P("section", None),
        P("section", None, "seq"),
        P("section", None, "seq"),
        P("section", None, "seq"),
        P("section", "seq", None),
        P("section", "seq", None),
        P("section", "seq", None),
        P("section"),
    )
    return jax.shard_map(
        body, mesh=mesh, in_specs=placed, out_specs=P("section", "seq", None), check_vma=False
    )
```

profile of v0, /device:TPU:2, one launch (start us, length us, event | category | flops | bytes accessed | tf_op | source)
XLA Modules:
  0.0 546.7 jit_solution(15673029558657225153)
XLA Ops:
  6.5 0.0 copy-start
  6.5 0.0 all-gather.2.cloned.1.call-start
  6.5 1.3 fusion.14
  7.8 0.8 broadcast_add_fusion
  8.6 1.9 fusion.17
  10.6 0.0 all-gather.2.cloned.1.call-update
  10.6 2.9 copy.17
  13.5 3.0 copy.15
  16.5 11.0 %all-to-all-start.1 = ((bf16[416,32,128]{2,0,1:T(8,128)(2,1)}), bf16[416,32,128]{2,0,1:T(8,128)(2,1)}, u32[]{:S(2)}, u32[]{:S(2)}) async-start(bf16[416,32,128]{2,0,1:T(8,128)(2,1)} %copy.15), calls=%async_computation.1 | async-start | bytes 6815744 | tf_op jit(solution)/shard_map/all_to_all | solution.py:43
  27.5 2.9 copy.16
  30.4 3.1 copy.14
  33.5 40.4 %all-to-all-done.1 = bf16[416,32,128]{2,0,1:T(8,128)(2,1)} async-done(((bf16[416,32,128]{2,0,1:T(8,128)(2,1)}), bf16[416,32,128]{2,0,1:T(8,128)(2,1)}, u32[]{:S(2)}, u32[]{:S(2)}) %all-to-all-start.1) | async-done | bytes 3407904 | tf_op jit(solution)/shard_map/all_to_all | solution.py:43
  73.8 6.6 %all-to-all-start = ((bf16[416,32,128]{2,0,1:T(8,128)(2,1)}), bf16[416,32,128]{2,0,1:T(8,128)(2,1)}, u32[]{:S(2)}, u32[]{:S(2)}) async-start(bf16[416,32,128]{2,0,1:T(8,128)(2,1)} %copy.14), calls=%async_computation | async-start | bytes 6815744 | tf_op jit(solution)/shard_map/all_to_all | solution.py:44
  80.4 0.2 reduce-scatter.2.cloned.1.call-start
  81.3 120.9 %all-gather.2.cloned.1.call-done = bf16[1024,6144]{1,0:T(8,128)(2,1)} async-done(((bf16[32,6144]{1,0:T(8,128)(2,1)}), bf16[1024,6144]{1,0:T(8,128)(2,1)}) %all-gather.2.cloned.1.call-update) | async-done | bytes 12582928 | tf_op jit(solution)/shard_map/all_gather | solution.py:36
  202.2 11.0 %fusion.9 = bf16[1024,384]{1,0:T(8,128)(2,1)S(1)} fusion(bf16[1024,6144]{1,0:T(8,128)(2,1)} %all-gather.2.cloned.1.call-done, bf16[6144,128]{1,0:T(8,128)(2,1)} %bitcast.47, bf16[6144,128]{1,0:T(8,128)(2,1)} %bitcast.48, bf16[6144,128]{1,0:T(8,128)(2,1)} %bitcast.49), kind=kOutput, calls=%fused_computation.13 | convolution fusion | flops 4846387200 | bytes 18087936 | tf_op jit(solution)/shard_map/dot_general | solution.py:35
  213.1 0.0 all-to-all-done
  213.1 0.8 slice_dynamic-update-slice_fusion
  214.0 21.0 %multiply_reduce_fusion = (f32[1024]{0:T(1024)S(1)}, f32[1024,13312]{1,0:T(8,128)}) fusion(bf16[13312,128]{1,0:T(8,128)(2,1)} %get-tuple-element.5, bf16[1024,384]{1,0:T(8,128)(2,1)S(1)} %fusion.9), kind=kOutput, calls=%fused_computation.2 | convolution fusion | flops 3516922880 | bytes 58200064 | tf_op jit(solution)/shard_map/qhd,khd->hqk/dot_general | solution.py:55
  234.9 17.8 %fusion = f32[1024]{0:T(1024)S(1)} fusion(f32[1024,13312]{1,0:T(8,128)} %get-tuple-element.8, f32[1024]{0:T(1024)S(1)} %get-tuple-element.7), kind=kLoop, calls=%fused_computation.3 | loop fusion | flops 40893440 | bytes 54534144 | tf_op jit(solution)/shard_map/reduce_sum | solution.py:58
  252.8 0.0 copy-done
  252.8 29.3 %convolution_convert_fusion = bf16[1024,6144]{1,0:T(8,128)(2,1)} fusion(bf16[1,128,6144]{2,1,0:T(8,128)(2,1)S(1)} %copy-done, bf16[13312,128]{1,0:T(8,128)(2,1)} %get-tuple-element.6, f32[1024,13312]{1,0:T(8,128)} %get-tuple-element.8, f32[1024]{0:T(1024)S(1)} %fusion, f32[1024]{0:T(1024)S(1)} %get-tuple-element.7), kind=kOutput, calls=%fused_computation.5 | convolution fusion | flops 5161222144 | bytes 72097792 | tf_op jit(solution)/shard_map/dot_general | solution.py:64
  282.1 0.0 copy-start.1
  282.1 0.0 copy-start.2
  282.1 0.0 copy-start.3
  282.1 0.0 reduce-scatter.2.cloned.1.call-update
  282.1 248.7 %reduce-scatter.2.cloned.1.call-done = bf16[32,6144]{1,0:T(8,128)(2,1)} async-done(((bf16[1024,6144]{1,0:T(8,128)(2,1)}), bf16[32,6144]{1,0:T(8,128)(2,1)}) %reduce-scatter.2.cloned.1.call-update) | async-done | bytes 393232 | tf_op jit(solution)/shard_map/reduce_scatter | solution.py:63
  530.7 0.0 copy-done.2
  530.7 0.0 copy-done.3
  530.7 1.1 fusion.19
  531.9 0.1 collective-permute-start
  531.9 7.2 %collective-permute-done = bf16[1,32,6144]{2,1,0:T(8,128)(2,1)S(1)} collective-permute-done((bf16[1,32,6144]{2,1,0:T(8,128)(2,1)S(1)}, bf16[1,32,6144]{2,1,0:T(8,128)(2,1)S(1)}, u32[]{:S(2)}, u32[]{:S(2)}) %collective-permute-start) | collective-permute-done | bytes 393248 | tf_op jit(solution)/shard_map/ppermute | solution.py:12
  539.1 0.7 copy.22
  539.9 0.0 copy-done.1
  (1 shorter events, 0.0 us)
Async XLA Ops:
  6.5 246.2 %copy-start = (bf16[1,128,6144]{2,1,0:T(8,128)(2,1)S(1)}, bf16[1,128,6144]{2,1,0:T(8,128)(2,1)}, u32[]{:S(2)}) copy-start(bf16[1,128,6144]{2,1,0:T(8,128)(2,1)} %param.18) | copy-start | bytes 4718596
  6.5 195.6 %all-gather.2.cloned.1.call-start = ((), (), s32[]{:S(2)}) async-start(), calls=%async_computation.3 | async-start | bytes 12976128 | tf_op jit(solution)/shard_map/all_gather | solution.py:36
  16.5 57.3 %all-to-all-start.1 = ((bf16[416,32,128]{2,0,1:T(8,128)(2,1)}), bf16[416,32,128]{2,0,1:T(8,128)(2,1)}, u32[]{:S(2)}, u32[]{:S(2)}) async-start(bf16[416,32,128]{2,0,1:T(8,128)(2,1)} %copy.15), calls=%async_computation.1 | async-start | bytes 6815744 | tf_op jit(solution)/shard_map/all_to_all | solution.py:43
  73.8 139.3 %all-to-all-start = ((bf16[416,32,128]{2,0,1:T(8,128)(2,1)}), bf16[416,32,128]{2,0,1:T(8,128)(2,1)}, u32[]{:S(2)}, u32[]{:S(2)}) async-start(bf16[416,32,128]{2,0,1:T(8,128)(2,1)} %copy.14), calls=%async_computation | async-start | bytes 6815744 | tf_op jit(solution)/shard_map/all_to_all | solution.py:44
  80.4 450.3 %reduce-scatter.2.cloned.1.call-start = ((), (), s32[]{:S(2)}) async-start(), calls=%async_computation.4 | async-start | bytes 12976128 | tf_op jit(solution)/shard_map/reduce_scatter | solution.py:63
  282.1 257.8 %copy-start.1 = (bf16[1,128,6144]{2,1,0:T(8,128)(2,1)S(1)}, bf16[1,128,6144]{2,1,0:T(8,128)(2,1)}, u32[]{:S(2)}) copy-start(bf16[1,128,6144]{2,1,0:T(8,128)(2,1)} %param.18) | copy-start | bytes 4718596
  282.1 248.7 %copy-start.2 = (bf16[1,32,6144]{2,1,0:T(8,128)(2,1)S(1)}, bf16[1,32,6144]{2,1,0:T(8,128)(2,1)}, u32[]{:S(2)}) copy-start(bf16[1,32,6144]{2,1,0:T(8,128)(2,1)} %param.11) | copy-start | bytes 1179652
  282.1 248.7 %copy-start.3 = (f32[1,6144]{1,0:T(1,128)S(1)}, f32[1,6144]{1,0:T(1,128)}, u32[]{:S(2)}) copy-start(f32[1,6144]{1,0:T(1,128)} %param.14) | copy-start | bytes 73732
  531.9 7.3 %collective-permute-start = (bf16[1,32,6144]{2,1,0:T(8,128)(2,1)S(1)}, bf16[1,32,6144]{2,1,0:T(8,128)(2,1)S(1)}, u32[]{:S(2)}, u32[]{:S(2)}) collective-permute-start(bf16[1,32,6144]{2,1,0:T(8,128)(2,1)S(1)} %fusion.19), channel_id=1, source_target_pairs={{0,32},{32,64},{64,96},{96,0},{1,33},{33,65},{65,97},{97,1},{2,34}... | collective-permute-start | bytes 1179656 | tf_op jit(solution)/shard_map/ppermute | solution.py:12
Sparse Core Ops, SparseCore 0:
  10.7 191.4 all-gather.1
  282.2 248.4 reduce-scatter.1
where the time goes:
time: 548 us; the launch traced here: 547 us
  waiting for transfers between devices  417 us (76%)
  matrix products  61.2 us (11%)
  other arithmetic  22.9 us (4%)
  starting transfers between devices  17.9 us (3%)
  between operations  14.1 us (3%)
  local copies, waits for them, and re-layouts  13.5 us (2%)
    reduce_scatter x1, waiting for transfers between devices, body(): lax.psum_scatter(jnp.dot(attended, w_out[0], preferred_element_type=jnp.f...  249 us
    all_gather x1, waiting for transfers between devices, body(): lax.all_gather(normed, 'seq', axis=0, tiled=True)  121 us
    all_to_all x1, waiting for transfers between devices, body(): lax.all_to_all(stale_keys[0], 'seq', split_axis=1, concat_axis=0, tiled=T...  40.4 us
    dot_general x1, matrix products, body(): jnp.dot(attended, w_out[0], preferred_element_type=jnp.float32)  29.3 us
    dot_general x1, matrix products, body(): jnp.einsum('qhd,khd->hqk', query_heads, key_heads, preferred_element_type...  21 us
    reduce_sum x1, other arithmetic, body(): probs = jax.nn.softmax(scores, axis=-1).astype(jnp.bfloat16)  17.8 us
    all_to_all x1, starting transfers between devices, body(): lax.all_to_all(stale_keys[0], 'seq', split_axis=1, concat_axis=0, tiled=T...  11 us
    dot_general x1, matrix products, body(): jnp.dot(lax.all_gather(normed, 'seq', axis=0, tiled=True), w_joint, prefe...  11 us
  transfers between devices with their start and end apart: 5, of which 4 were waited for; matrix products, arithmetic and copies ran while one was open for 4% of the time, Pallas kernels for 0%

commit v1 on v0

v1 whole, which is shorter than its diff:
```python
import functools

import jax
import jax.numpy as jnp
from jax import lax
from jax.experimental import pallas as pl
from jax.experimental.pallas import tpu as pltpu
from jax.sharding import PartitionSpec as P

HD = 128
NZ, NY, NX = 2, 4, 4
COUNT = NZ * NY * NX
PLANE = NY * NX
LOG2E = 1.4426950408889634
LOWEST = -1e30
BF = jnp.bfloat16
F32 = jnp.float32


def moved(value, dz=0, dy=0, dx=0):
    pairs = []
    for source in range(COUNT):
        z, y, x = source // PLANE, source // NX % NY, source % NX
        target = (z + dz) % NZ * PLANE + (y + dy) % NY * NX + (x + dx) % NX
        pairs.append((source, target))
    return lax.ppermute(value, "seq", pairs)


def onward(value, sections, dx):
    pairs = []
    for section in range(sections):
        for source in range(COUNT):
            target = source // NX * NX + (source % NX + dx) % NX
            pairs.append((section * COUNT + source, (section + 1) % sections * COUNT + target))
    return lax.ppermute(value, ("section", "seq"), pairs)


def from_behind(value, axis, steps):
    count = lax.axis_size(axis)
    pairs = [(source, (source + steps) % count) for source in range(count)]
    return lax.ppermute(value, axis, pairs)


def after(value, *others):
    return lax.optimization_barrier((value,) + others)[0]


def project_kernel(spot, *refs, pieces, rows):
    block_refs = refs[: len(pieces)]
    w_ref, q_ref, kv_ref, out_ref, x_ref = refs[len(pieces) :]
    z, y, x = spot[0], spot[1], spot[2]
    for ref, (column, steps) in zip(block_refs, pieces):
        wide = ref.shape[-1]
        for at, (dy, dx) in enumerate(steps):
            for plane in range(NZ):
                row = plane * PLANE * rows + lax.rem(y + NY - dy, NY) * NX * rows + lax.rem(x + NX - dx, NX) * rows
                x_ref[pl.ds(pl.multiple_of(row, rows), rows), column : column + wide] = ref[at, plane * rows : (plane + 1) * rows, :]
    half = PLANE * rows
    tile = half // 2

    def step(t, carry):
        start = pl.multiple_of(t * tile, tile)
        part = jnp.dot(x_ref[pl.ds(start, tile), :], w_ref[...], preferred_element_type=F32)
        for head in range(2):
            q = part[:, head * 3 * HD : head * 3 * HD + HD]
            q_ref[head, pl.ds(start, tile), :] = q
            out_ref[head, pl.ds(start, tile), :] = q.astype(BF)
        inner = pl.multiple_of(lax.rem(t, 2) * tile, tile)
        kept = t // 2 == z
        for head in range(2):
            for which in range(2):
                part_kv = part[:, (head * 3 + 1 + which) * HD : (head * 3 + 2 + which) * HD]

                @pl.when(kept)
                def _():
                    kv_ref[which * 2 + head, pl.ds(inner, tile), :] = part_kv

                @pl.when(jnp.logical_not(kept))
                def _():
                    out_ref[2 + which, pl.ds(pl.multiple_of(head * half + inner, tile), tile), :] = part_kv.astype(BF)

        return carry

    lax.fori_loop(0, 4, step, 0)


def project(spot, blocks, pieces, weights, rows):
    depth = weights.shape[0]
    patch = COUNT * rows
    vmem = pl.BlockSpec(memory_space=pltpu.VMEM)
    return pl.pallas_call(
        functools.partial(project_kernel, pieces=pieces, rows=rows),
        out_shape=(
            jax.ShapeDtypeStruct((2, patch, HD), F32),
            jax.ShapeDtypeStruct((4, patch // 2, HD), F32),
            jax.ShapeDtypeStruct((4, patch, HD), BF),
        ),
        in_specs=[pl.BlockSpec(memory_space=pltpu.SMEM)] + [vmem] * (len(blocks) + 1),
        out_specs=(vmem, vmem, vmem),
        scratch_shapes=[pltpu.VMEM((patch, depth), BF)],
        compiler_params=pltpu.CompilerParams(vmem_limit_bytes=44 * 2**20),
        cost_estimate=pl.CostEstimate(
            flops=2 * patch * depth * 6 * HD, bytes_accessed=2 * depth * (patch + 6 * HD) + 6 * patch * HD * 4, transcendentals=0
        ),
    )(spot, *blocks, weights)


def attend_kernel(lows, *refs, fresh, groups, first, last, length, patch):
    refs = list(refs)
    q_ref = refs.pop(0)
    if fresh:
        fresh_k, fresh_v = refs.pop(0), refs.pop(0)
    chunks = sum(groups)
    k_refs, v_refs = refs[:chunks], refs[chunks : 2 * chunks]
    refs = refs[2 * chunks :]
    if not first:
        acc_in, m_in, l_in = refs[:3]
        refs = refs[3:]
    if last:
        o_ref, lse_ref = refs[:2]
    else:
        acc_out, m_out, l_out = refs[:3]
    k_all, v_all, acc, m, l = refs[2 if last else 3 :]

    @pl.when(pl.program_id(1) == 0)
    def _():
        for at in range(chunks):
            k_all[at * length : (at + 1) * length, :] = k_refs[at][0]
            v_all[at * length : (at + 1) * length, :] = v_refs[at][0]

    if first:
        m[...] = jnp.full(m.shape, LOWEST, F32)
        l[...] = jnp.zeros(l.shape, F32)
        acc[...] = jnp.zeros(acc.shape, F32)
    else:
        m[...] = m_in[0]
        l[...] = l_in[0]
        acc[...] = acc_in[0]
    q = q_ref[0]
    scale = LOG2E / HD**0.5

    def update(keys, values, gone):
        s = lax.dot_general(q, keys, (((1,), (1,)), ((), ())), preferred_element_type=F32) * scale
        if gone is not None:
            s = jnp.where(gone, LOWEST, s)
        m_old = m[...]
        m_new = jnp.maximum(m_old, jnp.max(s, axis=1, keepdims=True))
        p = jnp.exp2(s - m_new[:, :1])
        alpha = jnp.exp2(m_old - m_new)
        l[...] = alpha * l[...] + jnp.sum(p, axis=1, keepdims=True)
        acc[...] = alpha * acc[...] + jnp.dot(p.astype(BF), values, preferred_element_type=F32)
        m[...] = m_new

    if fresh:
        update(fresh_k[0], fresh_v[0], None)
    base = 0
    for group in groups:
        size = group * length
        start = base * length
        touched = jnp.bool_(False)
        for at in range(group):
            low = lows[base + at]
            touched = touched | ((low < length) & (low + patch > 0))

        @pl.when(touched)
        def _():
            column = lax.broadcasted_iota(jnp.int32, (1, size), 1)
            gone = jnp.zeros((1, size), jnp.int32)
            for at in range(group):
                low = lows[base + at]
                begin = at * length + jnp.clip(low, 0, length)
                end = at * length + jnp.clip(low + patch, 0, length)
                gone = jnp.where((column >= begin) & (column < end), 1, gone)
            update(k_all[start : start + size, :], v_all[start : start + size, :], gone > 0)

        @pl.when(jnp.logical_not(touched))
        def _():
            update(k_all[start : start + size, :], v_all[start : start + size, :], None)

        base += group
    if last:
        o_ref[0] = acc[...] / l[...]
        lse = m[...] + jnp.log2(l[...])
        lse_ref[0] = jnp.transpose(lse)[:8, :]
    else:
        acc_out[0] = acc[...]
        m_out[0] = m[...]
        l_out[0] = l[...]


def attend(lows, q, fresh, chunks, groups, state, last, patch):
    heads, rows, _ = q.shape
    length = chunks[0].shape[1]
    tile = 256
    first = state is None
    row = pl.BlockSpec((1, tile, HD), lambda h, t: (h, t, 0))
    head = lambda which: (lambda h, t: (which + h, 0, 0))
    inputs, specs = [q], [row]
    if fresh is not None:
        for which in range(2):
            inputs.append(fresh)
            specs.append(pl.BlockSpec((1, fresh.shape[1], HD), head(2 * which)))
    for which in range(2):
        for chunk in chunks:
            inputs.append(chunk)
            specs.append(pl.BlockSpec((1, length, HD), head(2 * which)))
    full = jax.ShapeDtypeStruct((heads, rows, HD), F32)
    if not first:
        inputs += list(state)
        specs += [row] * 3
    if last:
        out_shape = (full, jax.ShapeDtypeStruct((heads, 8, rows), F32))
        out_specs = (row, pl.BlockSpec((1, 8, tile), lambda h, t: (h, 0, t)))
    else:
        out_shape, out_specs = (full,) * 3, (row,) * 3
    tokens = length * len(chunks) + (0 if fresh is None else fresh.shape[1])
    return pl.pallas_call(
        functools.partial(
            attend_kernel, fresh=fresh is not None, groups=groups, first=first, last=last, length=length, patch=patch
        ),
        grid=(heads, rows // tile),
        out_shape=out_shape,
        in_specs=[pl.BlockSpec(memory_space=pltpu.SMEM)] + specs,
        out_specs=out_specs,
        scratch_shapes=[pltpu.VMEM((length * len(chunks), HD), BF)] * 2 + [pltpu.VMEM((tile, HD), F32)] * 3,
        compiler_params=pltpu.CompilerParams(vmem_limit_bytes=40 * 2**20),
        cost_estimate=pl.CostEstimate(
            flops=heads * rows * tokens * HD * 8, bytes_accessed=heads * tokens * HD * 4, transcendentals=heads * rows * tokens
        ),
    )(lows, *inputs)


def body(
    tokens,
    mod_shift,
    mod_scale,
    mod_gate,
    w_query,
    w_key,
    w_value,
    w_out,
    stale_keys,
    stale_values,
    patch_index,
):
    sections = lax.axis_size("section")
    me = lax.axis_index("seq")
    z, y, x = me // PLANE, me // NX % NY, me % NX
    spot = jnp.stack([z, y, x]).astype(jnp.int32)
    rows, width = tokens.shape[1:]
    patch = COUNT * rows
    length = stale_keys.shape[1]
    half = width // NZ

    def kv_chunk(dy, dx, *deps):
        unit = (y + dy) % NY * NX + (x + dx) % NX
        if deps:
            unit = after(unit, *deps)
        parts = []
        for array in (stale_keys, stale_values):
            for plane in (z, 1 - z):
                parts.append(lax.dynamic_slice(array[0], (0, (plane * PLANE + unit) * HD), (length, HD)))
        return jnp.stack(parts)

    inputs = tokens[0].astype(F32)
    meansq = jnp.mean(inputs * inputs, axis=-1, keepdims=True)
    normed = (inputs * lax.rsqrt(meansq + 1e-06) * (1.0 + mod_scale[0]) + mod_shift[0]).astype(BF)
    own = lax.dynamic_slice(normed, (0, z * half), (rows, half))
    sent = lax.dynamic_slice(normed, (0, (1 - z) * half), (rows, half))
    got = moved(sent, dz=1)
    pair = jnp.concatenate((jnp.where(z == 0, own, got), jnp.where(z == 0, got, own)), axis=0)

    stale = {(0, 0): kv_chunk(0, 0)}
    for dy, dx in ((0, 1), (1, 0), (0, 3), (3, 0)):
        stale[dy, dx] = moved(kv_chunk(dy, dx, sent), dy=dy, dx=dx)

    def rows_of(plane):
        return jnp.concatenate(
            [lax.dynamic_slice(w[0], (plane * half, 0), (half, HD)) for w in (w_query, w_key, w_value)], axis=1
        )

    w_got = moved(after(rows_of(1 - z), got), dz=1)
    weights = jnp.concatenate((rows_of(z), w_got), axis=1)

    quarter = half // 2

    def ring(value, axis):
        return jnp.stack([value, moved(value, **{axis: 1}), moved(value, **{axis: 2}), moved(value, **{axis: -1})])

    def spread(block, axis):
        behind = moved(block, **{axis: 1})
        ahead = moved(block, **{axis: -1})
        return [block, behind, ahead, moved(behind[:2], **{axis: 1}), moved(ahead[2:], **{axis: -1})]

    first = ring(pair[:, :quarter], "dy")
    second = ring(pair[:, quarter:], "dx")
    blocks = spread(first, "dx") + spread(second, "dy")
    order = ((0, range(4)), (1, range(4)), (3, range(4)), (2, (0, 1)), (2, (2, 3)))
    pieces = [(0, tuple((j, k) for j in inner)) for k, inner in order]
    pieces += [(quarter, tuple((k, j) for j in inner)) for k, inner in order]

    for dy, dx in ((1, 1), (3, 3), (1, 3)):
        stale[dy, dx] = moved(kv_chunk(dy, dx, pair), dy=dy, dx=dx)
    for dy, dx in ((3, 1), (0, 2), (2, 0), (1, 2), (2, 1), (3, 2), (2, 3), (2, 2)):
        stale[dy, dx] = moved(kv_chunk(dy, dx, first, second), dy=dy, dx=dx)

    q_own, kv_own, sent = project(spot, blocks, pieces, weights, rows)
    got = moved(sent, dz=1)
    q = (q_own + got[1::-1].astype(F32)).astype(BF)
    kv_got = jnp.stack([got[2, patch // 2 :], got[2, : patch // 2], got[3, patch // 2 :], got[3, : patch // 2]])
    fresh = (kv_own + kv_got.astype(F32)).astype(BF)

    wide = width // NX
    w_pair = jnp.concatenate((w_out[0], moved(after(w_out[0], w_got), dz=1)), axis=0)
    w_parts = []
    for k in range(NX):
        part = lax.dynamic_slice(w_pair, (0, (x + k) % NX * wide), (NZ * HD, wide))
        w_parts.append(moved(part, dx=k) if k else part)
    w_columns = jnp.concatenate(w_parts, axis=0)
    tokens_behind = from_behind(tokens[0], "section", 1)
    gate_behind = from_behind(mod_gate, "section", 1)

    offset = patch_index[0] * patch
    keys = list(stale)
    lows = jnp.stack([offset - (z * PLANE + (y - dy) % NY * NX + (x - dx) % NX) * length for dy, dx in keys]).astype(jnp.int32)
    state = attend(lows[:8], q, fresh, [stale[key] for key in keys[:8]], (4, 4), None, False, patch)
    state = attend(lows[8:12], q, None, [stale[key] for key in keys[8:12]], (4,), state, False, patch)
    o, lse = attend(lows[12:], q, None, [stale[key] for key in keys[12:]], (4,), state, True, patch)

    lse = lse[:, 0]
    there = (1 - z) * (patch // 2)
    here = z * (patch // 2)
    o_got = moved(lax.dynamic_slice(o, (0, there, 0), (2, patch // 2, HD)).astype(BF), dz=1)[::-1]
    lse_got = moved(lax.dynamic_slice(lse, (0, there), (2, patch // 2)), dz=1)[::-1]
    o_here = lax.dynamic_slice(o, (0, here, 0), (2, patch // 2, HD))
    lse_here = lax.dynamic_slice(lse, (0, here), (2, patch // 2))
    share = 1.0 / (1.0 + jnp.exp2(lse_got - lse_here))
    share = share[:, :, None]
    attended = (o_here * share + o_got.astype(F32) * (1.0 - share)).astype(BF)
    attended = jnp.concatenate((attended[0], attended[1]), axis=1)

    gathered = jnp.concatenate([attended] + [moved(attended, dx=k) for k in range(1, NX)], axis=1)
    partial = jnp.dot(gathered, w_columns, preferred_element_type=F32).astype(BF)
    band = NX * rows
    total = lax.dynamic_slice(partial, (y * band, 0), (band, wide)).astype(F32)
    for k in range(1, NY):
        part = lax.dynamic_slice(partial, ((y + k) % NY * band, 0), (band, wide))
        total = total + moved(part, dy=k).astype(F32)
    total = total.astype(BF)
    projected = jnp.zeros((rows, width), BF)
    for k in range(NX):
        part = onward(lax.dynamic_slice(total, ((x + k) % NX * rows, 0), (rows, wide)), sections, k)
        projected = lax.dynamic_update_slice(projected, part, (0, (x - k) % NX * wide))
    updated = tokens_behind.astype(F32) + gate_behind * projected.astype(F32)
    return updated.astype(BF)[None]


def solution(mesh):
    placed = (
        P("section", "seq", None),
        P("section", None),
        P("section", None),
        P("section", None),
        P("section", None, "seq"),
        P("section", None, "seq"),
        P("section", None, "seq"),
        P("section", "seq", None),
        P("section", "seq", None),
        P("section", "seq", None),
        P("section"),
    )
    return jax.shard_map(
        body, mesh=mesh, in_specs=placed, out_specs=P("section", "seq", None), check_vma=False
    )
```

time: 548 us -> 343 us (0.63)
  waiting for transfers between devices: 417 us -> 143 us
  starting transfers between devices: 17.9 us -> 112 us
  matrix products: 61.2 us -> 2.01 us
  Pallas kernels: 0 us -> 55.6 us
  between operations: 14.1 us -> 1.63 us
  other arithmetic: 22.9 us -> 14.5 us
    reduce_scatter x1 -> x0, waiting for transfers between devices: 249 us -> none  [body(): lax.psum_scatter(jnp.dot(attended, w_out[0], preferred_element_type=jnp.f...]
    ppermute x0 -> x48, waiting for transfers between devices: none -> 142 us  [the longest x44 133 us: moved(): return lax.ppermute(value, 'seq', pairs)]
    all_gather x1 -> x0, waiting for transfers between devices: 121 us -> none  [body(): lax.all_gather(normed, 'seq', axis=0, tiled=True)]
    ppermute x0 -> x48, starting transfers between devices: none -> 112 us  [the longest x44 111 us: moved(): return lax.ppermute(value, 'seq', pairs)]
    dot_general x3 -> x1, matrix products: 61.2 us -> 2.01 us  [body(): jnp.dot(gathered, w_columns, preferred_element_type=F32).astype(BF)]
    pallas_call x0 -> x4, Pallas kernels: none -> 55.6 us  [the longest x3 46.5 us: attend(): pl.pallas_call(functools.partial(attend_kernel, fresh=fresh is not None,...]
    all_to_all x2 -> x0, waiting for transfers between devices: 40.4 us -> none  [the longest x1 40.4 us: body(): lax.all_to_all(stale_keys[0], 'seq', split_axis=1, concat_axis=0, tiled=T...]
    reduce_sum x1 -> x0, other arithmetic: 17.8 us -> none  [body(): probs = jax.nn.softmax(scores, axis=-1).astype(jnp.bfloat16)]
  transfers between devices with their start and end apart: 5 -> 50, of which waited for: 4 -> 20; matrix products, arithmetic and copies ran while one was open for 4% -> 5% of each run, Pallas kernels for 0% -> 16%
where the time goes in v1:
time: 343 us; the launch traced here: 340 us
  waiting for transfers between devices  143 us (42%)
  starting transfers between devices  112 us (33%)
  Pallas kernels  55.6 us (16%)
  other arithmetic  14.5 us (4%)
  local copies, waits for them, and re-layouts  11.3 us (3%)
    ppermute x44, waiting for transfers between devices, moved(): return lax.ppermute(value, 'seq', pairs)  133 us
    ppermute x44, starting transfers between devices, moved(): return lax.ppermute(value, 'seq', pairs)  111 us
    pallas_call x3, Pallas kernels, attend(): pl.pallas_call(functools.partial(attend_kernel, fresh=fresh is not None,...  46.5 us
    pallas_call x1, Pallas kernels, project(): pl.pallas_call(functools.partial(project_kernel, pieces=pieces, rows=rows...  9.09 us
    ppermute x4, waiting for transfers between devices, onward(): return lax.ppermute(value, ('section', 'seq'), pairs)  8.99 us
  transfers between devices with their start and end apart: 50, of which 20 were waited for; matrix products, arithmetic and copies ran while one was open for 5% of the time, Pallas kernels for 16%

profile of v1, /device:TPU:2, one launch (start us, length us, event | category | flops | bytes accessed | tf_op | source)
XLA Modules:
  0.0 340.0 jit_solution(12327391234490149011)
XLA Ops:
  3.3 4.0 %collective-permute-start.2 = (bf16[32,3072]{1,0:T(8,128)(2,1)S(1)}, bf16[32,3072]{1,0:T(8,128)(2,1)S(1)}, u32[]{:S(2)}, u32[]{:S(2)}) collective-permute-start(bf16[32,3072]{1,0:T(8,128)(2,1)S(1)} %constant_dynamic-slice_fusion.73), channel_id=1, source_target_pairs={{0,16},{1,17},{2,18},{3,19},{4,20},{5,21},{6,22},{7,23},{8,24},{9,... | collective-permute-start | bytes 589832 | tf_op jit(solution)/shard_map/ppermute | solution.py:26
  11.6 1.7 pad_maximum_fusion.1
  13.5 1.9 collective-permute-start.17
  15.5 3.1 collective-permute-start.5
  20.8 5.1 %collective-permute-done.5 = bf16[64,1536]{1,0:T(8,128)(2,1)S(1)} collective-permute-done((bf16[64,1536]{1,0:T(8,128)(2,1)S(1)}, bf16[64,1536]{1,0:T(8,128)(2,1)S(1)}, u32[]{:S(2)}, u32[]{:S(2)}) %collective-permute-start.5) | collective-permute-done | bytes 196640 | tf_op jit(solution)/shard_map/ppermute | solution.py:26
  25.9 2.1 collective-permute-start.11
  33.0 5.5 %collective-permute-done.10 = bf16[64,1536]{1,0:T(8,128)(2,1)S(1)} collective-permute-done((bf16[64,1536]{1,0:T(8,128)(2,1)S(1)}, bf16[64,1536]{1,0:T(8,128)(2,1)S(1)}, u32[]{:S(2)}, u32[]{:S(2)}) %collective-permute-start.10) | collective-permute-done | bytes 196640 | tf_op jit(solution)/shard_map/ppermute | solution.py:26
  38.7 4.7 %collective-permute-start.14 = (bf16[4,64,1536]{2,1,0:T(8,128)(2,1)S(1)}, bf16[4,64,1536]{2,1,0:T(8,128)(2,1)}, u32[]{:S(2)}, u32[]{:S(2)}) collective-permute-start(bf16[4,64,1536]{2,1,0:T(8,128)(2,1)S(1)} %pad_maximum_fusion.3.refs_5_), channel_id=1, source_target_pairs={{0,12},{1,13},{2,14},{3,15},{4,0},{5,1},{6,2},{7,3},{8,4},{9,5},{1... | collective-permute-start | bytes 2359304 | tf_op jit(solution)/shard_map/ppermute | solution.py:26
  43.4 2.6 constant_dynamic-slice_fusion.9
  48.7 3.3 collective-permute-done.6.refs_1_
  52.0 4.2 %collective-permute-start.23 = (bf16[4,416,128]{2,1,0:T(8,128)(2,1)S(1)}, bf16[4,416,128]{2,1,0:T(8,128)(2,1)S(1)}, u32[]{:S(2)}, u32[]{:S(2)}) collective-permute-start(bf16[4,416,128]{2,1,0:T(8,128)(2,1)S(1)} %pad_maximum_fusion.9), channel_id=1, source_target_pairs={{0,13},{1,14},{2,15},{3,12},{4,1},{5,2},{6,3},{7,0},{8,5},{9,6},{1... | collective-permute-start | bytes 1277960 | tf_op jit(solution)/shard_map/ppermute | solution.py:26
  56.4 2.3 collective-permute-start.9
  59.8 2.8 collective-permute-start.15
  63.6 4.5 %collective-permute-done.17 = bf16[3072,384]{1,0:T(8,128)(2,1)} collective-permute-done((bf16[3072,384]{1,0:T(8,128)(2,1)}, bf16[3072,384]{1,0:T(8,128)(2,1)}, u32[]{:S(2)}, u32[]{:S(2)}) %collective-permute-start.17) | collective-permute-done | bytes 2359328 | tf_op jit(solution)/shard_map/ppermute | solution.py:26
  68.1 3.0 collective-permute-start.16
  71.1 3.7 %pad_maximum_fusion.refs_10_ = bf16[3072,768]{1,0:T(8,128)(2,1)} fusion(bf16[3072,384]{1,0:T(8,128)(2,1)} %collective-permute-done.17, bf16[3072,128]{1,0:T(8,128)(2,1)S(1)} %copy-done.3, bf16[3072,128]{1,0:T(8,128)(2,1)S(1)} %copy-done.4, bf16[3072,128]{1,0:T(8,128)(2,1)S(1)} %copy-done.2), kind=kLoop, calls=%fused_computation | loop fusion | flops 18874368 | bytes 9437184 | tf_op jit(solution)/shard_map/concatenate | solution.py:283
  74.8 2.1 collective-permute-start.24
  77.8 9.6 %collective-permute-done.16.refs_9_ = bf16[2,64,1536]{2,1,0:T(8,128)(2,1)S(1)} collective-permute-done((bf16[2,64,1536]{2,1,0:T(8,128)(2,1)S(1)}, bf16[2,64,1536]{2,1,0:T(8,128)(2,1)S(1)}, u32[]{:S(2)}, u32[]{:S(2)}) %collective-permute-start.16) | collective-permute-done | bytes 393248 | tf_op jit(solution)/shard_map/ppermute | solution.py:26
  87.4 9.1 %shard_map.109 = (f32[2,1024,128]{2,1,0:T(8,128)S(1)}, f32[4,512,128]{2,1,0:T(8,128)S(1)}, bf16[4,1024,128]{2,1,0:T(8,128)(2,1)S(1)}) custom-call(s32[3]{0:T(128)S(1)} %pad_add_fusion.1.spot, bf16[4,64,1536]{2,1,0:T(8,128)(2,1)S(1)} %pad_maximum_fusion.2.refs_0_, bf16[4,64,1536]{2,1,0:T(8,128)(2,1)S(1)} %collective-permute-done.6.refs_1_, ...), custom_call_target="tpu_custom_call" | custom-call | flops 4831838208 | bytes 14155776 | tf_op jit(solution)/shard_map/pallas_call | solution.py:91
  98.2 14.7 %collective-permute-done.18 = bf16[4,1024,128]{2,1,0:T(8,128)(2,1)S(1)} collective-permute-done((bf16[4,1024,128]{2,1,0:T(8,128)(2,1)S(1)}, bf16[4,1024,128]{2,1,0:T(8,128)(2,1)S(1)}, u32[]{:S(2)}, u32[]{:S(2)}) %collective-permute-start.18) | collective-permute-done | bytes 1048608 | tf_op jit(solution)/shard_map/ppermute | solution.py:26
  113.2 8.0 %collective-permute-start.29 = (bf16[4,416,128]{2,1,0:T(8,128)(2,1)S(1)}, bf16[4,416,128]{2,1,0:T(8,128)(2,1)S(1)}, u32[]{:S(2)}, u32[]{:S(2)}) collective-permute-start(bf16[4,416,128]{2,1,0:T(8,128)(2,1)S(1)} %pad_maximum_fusion.16), channel_id=1, source_target_pairs={{0,3},{1,0},{2,1},{3,2},{4,7},{5,4},{6,5},{7,6},{8,11},{9,8},{10,9... | collective-permute-start | bytes 1277960 | tf_op jit(solution)/shard_map/ppermute | solution.py:26
  121.3 3.8 %collective-permute-start.30 = (bf16[4,416,128]{2,1,0:T(8,128)(2,1)S(1)}, bf16[4,416,128]{2,1,0:T(8,128)(2,1)S(1)}, u32[]{:S(2)}, u32[]{:S(2)}) collective-permute-start(bf16[4,416,128]{2,1,0:T(8,128)(2,1)S(1)} %pad_maximum_fusion.17), channel_id=1, source_target_pairs={{0,12},{1,13},{2,14},{3,15},{4,0},{5,1},{6,2},{7,3},{8,4},{9,5},{1... | collective-permute-start | bytes 1277960 | tf_op jit(solution)/shard_map/ppermute | solution.py:26
  125.1 4.1 %collective-permute-start.32 = (bf16[4,416,128]{2,1,0:T(8,128)(2,1)S(1)}, bf16[4,416,128]{2,1,0:T(8,128)(2,1)S(1)}, u32[]{:S(2)}, u32[]{:S(2)}) collective-permute-start(bf16[4,416,128]{2,1,0:T(8,128)(2,1)S(1)} %pad_maximum_fusion.19), channel_id=1, source_target_pairs={{0,15},{1,12},{2,13},{3,14},{4,3},{5,0},{6,1},{7,2},{8,7},{9,4},{1... | collective-permute-start | bytes 1277960 | tf_op jit(solution)/shard_map/ppermute | solution.py:26
  129.2 9.3 %collective-permute-start.33 = (bf16[4,416,128]{2,1,0:T(8,128)(2,1)S(1)}, bf16[4,416,128]{2,1,0:T(8,128)(2,1)S(1)}, u32[]{:S(2)}, u32[]{:S(2)}) collective-permute-start(bf16[4,416,128]{2,1,0:T(8,128)(2,1)S(1)} %pad_maximum_fusion.20), channel_id=1, source_target_pairs={{0,7},{1,4},{2,5},{3,6},{4,11},{5,8},{6,9},{7,10},{8,15},{9,12},{1... | collective-permute-start | bytes 1277960 | tf_op jit(solution)/shard_map/ppermute | solution.py:26
  138.8 6.0 %collective-permute-done.30.refs_7_.refs_15_ = bf16[4,416,128]{2,1,0:T(8,128)(2,1)S(1)} collective-permute-done((bf16[4,416,128]{2,1,0:T(8,128)(2,1)S(1)}, bf16[4,416,128]{2,1,0:T(8,128)(2,1)S(1)}, u32[]{:S(2)}, u32[]{:S(2)}) %collective-permute-start.30) | collective-permute-done | bytes 426016 | tf_op jit(solution)/shard_map/ppermute | solution.py:26
  144.9 5.6 %collective-permute-start.21 = (bf16[4,416,128]{2,1,0:T(8,128)(2,1)S(1)}, bf16[4,416,128]{2,1,0:T(8,128)(2,1)S(1)}, u32[]{:S(2)}, u32[]{:S(2)}) collective-permute-start(bf16[4,416,128]{2,1,0:T(8,128)(2,1)S(1)} %pad_maximum_fusion.7), channel_id=1, source_target_pairs={{0,11},{1,8},{2,9},{3,10},{4,15},{5,12},{6,13},{7,14},{8,3},{9,0},... | collective-permute-start | bytes 1277960 | tf_op jit(solution)/shard_map/ppermute | solution.py:26
  150.4 8.7 %collective-permute-start.22 = (bf16[4,416,128]{2,1,0:T(8,128)(2,1)S(1)}, bf16[4,416,128]{2,1,0:T(8,128)(2,1)S(1)}, u32[]{:S(2)}, u32[]{:S(2)}) collective-permute-start(bf16[4,416,128]{2,1,0:T(8,128)(2,1)S(1)} %pad_maximum_fusion.8), channel_id=1, source_target_pairs={{0,10},{1,11},{2,8},{3,9},{4,14},{5,15},{6,12},{7,13},{8,2},{9,3},... | collective-permute-start | bytes 1277960 | tf_op jit(solution)/shard_map/ppermute | solution.py:26
  159.1 6.7 %collective-permute-start.26 = (bf16[4,416,128]{2,1,0:T(8,128)(2,1)S(1)}, bf16[4,416,128]{2,1,0:T(8,128)(2,1)S(1)}, u32[]{:S(2)}, u32[]{:S(2)}) collective-permute-start(bf16[4,416,128]{2,1,0:T(8,128)(2,1)S(1)} %pad_maximum_fusion.12), channel_id=1, source_target_pairs={{0,6},{1,7},{2,4},{3,5},{4,10},{5,11},{6,8},{7,9},{8,14},{9,15},{1... | collective-permute-start | bytes 1277960 | tf_op jit(solution)/shard_map/ppermute | solution.py:26
  165.8 24.5 %shard_map.110 = (f32[2,1024,128]{2,1,0:T(8,128)S(1)}, f32[2,1024,128]{2,1,0:T(8,128)S(1)}, f32[2,1024,128]{2,1,0:T(8,128)S(1)}) custom-call(s32[8]{0:T(128)S(1)} %stack.252.lows, bf16[2,1024,128]{2,1,0:T(8,128)(2,1)S(1)} %add_convert_fusion.1.refs_0_, bf16[4,512,128]{2,1,0:T(8,128)(2,1)S(1)} %add_convert_fusion.refs_1_.refs_2_, ...), custom_call_target="tpu_custom_call" | custom-call | flops 8053063680 | bytes 3932160 | tf_op jit(solution)/shard_map/pallas_call | solution.py:217
  190.4 12.1 %collective-permute-done.26.refs_4_.refs_8_ = bf16[4,416,128]{2,1,0:T(8,128)(2,1)S(1)} collective-permute-done((bf16[4,416,128]{2,1,0:T(8,128)(2,1)S(1)}, bf16[4,416,128]{2,1,0:T(8,128)(2,1)S(1)}, u32[]{:S(2)}, u32[]{:S(2)}) %collective-permute-start.26) | collective-permute-done | bytes 426016 | tf_op jit(solution)/shard_map/ppermute | solution.py:26
  202.4 10.2 %collective-permute-start.39 = (bf16[128,6144]{1,0:T(8,128)(2,1)S(1)}, bf16[128,6144]{1,0:T(8,128)(2,1)}, u32[]{:S(2)}, u32[]{:S(2)}) collective-permute-start(bf16[128,6144]{1,0:T(8,128)(2,1)S(1)} %bitcast.73), channel_id=1, source_target_pairs={{0,16},{1,17},{2,18},{3,19},{4,20},{5,21},{6,22},{7,23},{8,24},{9,... | collective-permute-start | bytes 4718600 | tf_op jit(solution)/shard_map/ppermute | solution.py:26
  212.6 10.8 %shard_map.111 = (f32[2,1024,128]{2,1,0:T(8,128)S(1)}, f32[2,1024,128]{2,1,0:T(8,128)S(1)}, f32[2,1024,128]{2,1,0:T(8,128)S(1)}) custom-call(s32[4]{0:T(128)S(1)} %pad_add_fusion.2.lows, bf16[2,1024,128]{2,1,0:T(8,128)(2,1)S(1)} %add_convert_fusion.1.refs_0_, bf16[4,416,128]{2,1,0:T(8,128)(2,1)S(1)} %collective-permute-done.23.refs_1_.refs_5_, ...), custom_call_target="tpu_custom_call" | custom-call | flops 3489660928 | bytes 1703936 | tf_op jit(solution)/shard_map/pallas_call | solution.py:217
  223.5 11.1 %shard_map.112 = (f32[2,1024,128]{2,1,0:T(8,128)S(1)}, f32[2,8,1024]{2,1,0:T(8,128)S(1)}) custom-call(s32[4]{0:T(128)S(1)} %pad_add_fusion.lows, bf16[2,1024,128]{2,1,0:T(8,128)(2,1)S(1)} %add_convert_fusion.1.refs_0_, bf16[4,416,128]{2,1,0:T(8,128)(2,1)S(1)} %collective-permute-done.19.refs_1_.refs_5_, ...), custom_call_target="tpu_custom_call" | custom-call | flops 3489660928 | bytes 1703936 | tf_op jit(solution)/shard_map/pallas_call | solution.py:217
  234.7 1.8 collective-permute-start.35
  236.5 1.8 collective-permute-start.34
  238.3 13.4 %collective-permute-done.34 = f32[2,512]{1,0:T(2,128)S(1)} collective-permute-done((f32[2,512]{1,0:T(2,128)S(1)}, f32[2,512]{1,0:T(2,128)S(1)}, u32[]{:S(2)}, u32[]{:S(2)}) %collective-permute-start.34) | collective-permute-done | bytes 4128 | tf_op jit(solution)/shard_map/ppermute | solution.py:26
  252.5 1.7 fusion.16
  254.2 2.0 collective-permute-start.42
  256.1 2.9 collective-permute-start.41
  260.4 17.1 %collective-permute-done.36 = bf16[512,256]{1,0:T(8,128)(2,1)S(1)} collective-permute-done((bf16[512,256]{1,0:T(8,128)(2,1)S(1)}, bf16[512,256]{1,0:T(8,128)(2,1)S(1)}, u32[]{:S(2)}, u32[]{:S(2)}) %collective-permute-start.36) | collective-permute-done | bytes 262176 | tf_op jit(solution)/shard_map/ppermute | solution.py:26
  277.6 20.1 %collective-permute-done.38 = bf16[512,256]{1,0:T(8,128)(2,1)S(1)} collective-permute-done((bf16[512,256]{1,0:T(8,128)(2,1)S(1)}, bf16[512,256]{1,0:T(8,128)(2,1)S(1)}, u32[]{:S(2)}, u32[]{:S(2)}) %collective-permute-start.38) | collective-permute-done | bytes 262176 | tf_op jit(solution)/shard_map/ppermute | solution.py:26
  297.7 2.0 fusion.8
  299.8 5.7 %collective-permute-start.45 = (bf16[128,1536]{1,0:T(8,128)(2,1)S(1)}, bf16[128,1536]{1,0:T(8,128)(2,1)S(1)}, u32[]{:S(2)}, u32[]{:S(2)}) collective-permute-start(bf16[128,1536]{1,0:T(8,128)(2,1)S(1)} %get-tuple-element.132), channel_id=1, source_target_pairs={{0,12},{1,13},{2,14},{3,15},{4,0},{5,1},{6,2},{7,3},{8,4},{9,5},{1... | collective-permute-start | bytes 1179656 | tf_op jit(solution)/shard_map/ppermute | solution.py:26
  306.5 15.8 %collective-permute-done.45 = bf16[128,1536]{1,0:T(8,128)(2,1)S(1)} collective-permute-done((bf16[128,1536]{1,0:T(8,128)(2,1)S(1)}, bf16[128,1536]{1,0:T(8,128)(2,1)S(1)}, u32[]{:S(2)}, u32[]{:S(2)}) %collective-permute-start.45) | collective-permute-done | bytes 393248 | tf_op jit(solution)/shard_map/ppermute | solution.py:26
  322.3 3.5 %collective-permute-done.43 = bf16[128,1536]{1,0:T(8,128)(2,1)} collective-permute-done((bf16[128,1536]{1,0:T(8,128)(2,1)S(1)}, bf16[128,1536]{1,0:T(8,128)(2,1)}, u32[]{:S(2)}, u32[]{:S(2)}) %collective-permute-start.43) | collective-permute-done | bytes 393248 | tf_op jit(solution)/shard_map/ppermute | solution.py:26
  328.8 2.5 collective-permute-done.46
  332.9 3.1 collective-permute-done.48
  336.0 1.9 collective-permute-done.49
  (145 shorter events, 32.1 us)
Async XLA Ops:
  3.3 10.2 %collective-permute-start.2 = (bf16[32,3072]{1,0:T(8,128)(2,1)S(1)}, bf16[32,3072]{1,0:T(8,128)(2,1)S(1)}, u32[]{:S(2)}, u32[]{:S(2)}) collective-permute-start(bf16[32,3072]{1,0:T(8,128)(2,1)S(1)} %constant_dynamic-slice_fusion.73), channel_id=1, source_target_pairs={{0,16},{1,17},{2,18},{3,19},{4,20},{5,21},{6,22},{7,23},{8,24},{9,... | collective-permute-start | bytes 589832 | tf_op jit(solution)/shard_map/ppermute | solution.py:26
  13.5 54.6 %collective-permute-start.17 = (bf16[3072,384]{1,0:T(8,128)(2,1)}, bf16[3072,384]{1,0:T(8,128)(2,1)}, u32[]{:S(2)}, u32[]{:S(2)}) collective-permute-start(bf16[3072,384]{1,0:T(8,128)(2,1)} %pad_maximum_fusion.1), channel_id=1, source_target_pairs={{0,16},{1,17},{2,18},{3,19},{4,20},{5,21},{6,22},{7,23},{8,24},{9,... | collective-permute-start | bytes 7077896 | tf_op jit(solution)/shard_map/ppermute | solution.py:26
  15.5 10.3 %collective-permute-start.5 = (bf16[64,1536]{1,0:T(8,128)(2,1)S(1)}, bf16[64,1536]{1,0:T(8,128)(2,1)S(1)}, u32[]{:S(2)}, u32[]{:S(2)}) collective-permute-start(bf16[64,1536]{1,0:T(8,128)(2,1)S(1)} %get-tuple-element.151), channel_id=1, source_target_pairs={{0,12},{1,13},{2,14},{3,15},{4,0},{5,1},{6,2},{7,3},{8,4},{9,5},{1... | collective-permute-start | bytes 589832 | tf_op jit(solution)/shard_map/ppermute | solution.py:26
  18.6 9.3 %collective-permute-start.4 = (bf16[64,1536]{1,0:T(8,128)(2,1)S(1)}, bf16[64,1536]{1,0:T(8,128)(2,1)S(1)}, u32[]{:S(2)}, u32[]{:S(2)}) collective-permute-start(bf16[64,1536]{1,0:T(8,128)(2,1)S(1)} %get-tuple-element.151), channel_id=1, source_target_pairs={{0,8},{1,9},{2,10},{3,11},{4,12},{5,13},{6,14},{7,15},{8,0},{9,1},... | collective-permute-start | bytes 589832 | tf_op jit(solution)/shard_map/ppermute | solution.py:26
  19.3 10.3 %collective-permute-start.3 = (bf16[64,1536]{1,0:T(8,128)(2,1)S(1)}, bf16[64,1536]{1,0:T(8,128)(2,1)S(1)}, u32[]{:S(2)}, u32[]{:S(2)}) collective-permute-start(bf16[64,1536]{1,0:T(8,128)(2,1)S(1)} %get-tuple-element.151), channel_id=1, source_target_pairs={{0,4},{1,5},{2,6},{3,7},{4,8},{5,9},{6,10},{7,11},{8,12},{9,13},{1... | collective-permute-start | bytes 589832 | tf_op jit(solution)/shard_map/ppermute | solution.py:26
  20.2 11.0 %collective-permute-start.12 = (bf16[64,1536]{1,0:T(8,128)(2,1)S(1)}, bf16[64,1536]{1,0:T(8,128)(2,1)S(1)}, u32[]{:S(2)}, u32[]{:S(2)}) collective-permute-start(bf16[64,1536]{1,0:T(8,128)(2,1)S(1)} %get-tuple-element.150), channel_id=1, source_target_pairs={{0,3},{1,0},{2,1},{3,2},{4,7},{5,4},{6,5},{7,6},{8,11},{9,8},{10,9... | collective-permute-start | bytes 589832 | tf_op jit(solution)/shard_map/ppermute | solution.py:26
  25.9 7.2 %collective-permute-start.11 = (bf16[64,1536]{1,0:T(8,128)(2,1)S(1)}, bf16[64,1536]{1,0:T(8,128)(2,1)S(1)}, u32[]{:S(2)}, u32[]{:S(2)}) collective-permute-start(bf16[64,1536]{1,0:T(8,128)(2,1)S(1)} %get-tuple-element.150), channel_id=1, source_target_pairs={{0,2},{1,3},{2,0},{3,1},{4,6},{5,7},{6,4},{7,5},{8,10},{9,11},{10,... | collective-permute-start | bytes 589832 | tf_op jit(solution)/shard_map/ppermute | solution.py:26
  28.0 10.5 %collective-permute-start.10 = (bf16[64,1536]{1,0:T(8,128)(2,1)S(1)}, bf16[64,1536]{1,0:T(8,128)(2,1)S(1)}, u32[]{:S(2)}, u32[]{:S(2)}) collective-permute-start(bf16[64,1536]{1,0:T(8,128)(2,1)S(1)} %get-tuple-element.150), channel_id=1, source_target_pairs={{0,1},{1,2},{2,3},{3,0},{4,5},{5,6},{6,7},{7,4},{8,9},{9,10},{10,1... | collective-permute-start | bytes 589832 | tf_op jit(solution)/shard_map/ppermute | solution.py:26
  29.7 22.4 %collective-permute-start.6 = (bf16[4,64,1536]{2,1,0:T(8,128)(2,1)S(1)}, bf16[4,64,1536]{2,1,0:T(8,128)(2,1)S(1)}, u32[]{:S(2)}, u32[]{:S(2)}) collective-permute-start(bf16[4,64,1536]{2,1,0:T(8,128)(2,1)S(1)} %pad_maximum_fusion.2.refs_0_), channel_id=1, source_target_pairs={{0,1},{1,2},{2,3},{3,0},{4,5},{5,6},{6,7},{7,4},{8,9},{9,10},{10,1... | collective-permute-start | bytes 2359304 | tf_op jit(solution)/shard_map/ppermute | solution.py:26
  31.2 25.1 %collective-permute-start.7 = (bf16[4,64,1536]{2,1,0:T(8,128)(2,1)S(1)}, bf16[4,64,1536]{2,1,0:T(8,128)(2,1)S(1)}, u32[]{:S(2)}, u32[]{:S(2)}) collective-permute-start(bf16[4,64,1536]{2,1,0:T(8,128)(2,1)S(1)} %pad_maximum_fusion.2.refs_0_), channel_id=1, source_target_pairs={{0,3},{1,0},{2,1},{3,2},{4,7},{5,4},{6,5},{7,6},{8,11},{9,8},{10,9... | collective-permute-start | bytes 2359304 | tf_op jit(solution)/shard_map/ppermute | solution.py:26
  38.6 17.8 %collective-permute-start.13 = (bf16[4,64,1536]{2,1,0:T(8,128)(2,1)S(1)}, bf16[4,64,1536]{2,1,0:T(8,128)(2,1)}, u32[]{:S(2)}, u32[]{:S(2)}) collective-permute-start(bf16[4,64,1536]{2,1,0:T(8,128)(2,1)S(1)} %pad_maximum_fusion.3.refs_5_), channel_id=1, source_target_pairs={{0,4},{1,5},{2,6},{3,7},{4,8},{5,9},{6,10},{7,11},{8,12},{9,13},{1... | collective-permute-start | bytes 2359304 | tf_op jit(solution)/shard_map/ppermute | solution.py:26
  38.7 21.0 %collective-permute-start.14 = (bf16[4,64,1536]{2,1,0:T(8,128)(2,1)S(1)}, bf16[4,64,1536]{2,1,0:T(8,128)(2,1)}, u32[]{:S(2)}, u32[]{:S(2)}) collective-permute-start(bf16[4,64,1536]{2,1,0:T(8,128)(2,1)S(1)} %pad_maximum_fusion.3.refs_5_), channel_id=1, source_target_pairs={{0,12},{1,13},{2,14},{3,15},{4,0},{5,1},{6,2},{7,3},{8,4},{9,5},{1... | collective-permute-start | bytes 2359304 | tf_op jit(solution)/shard_map/ppermute | solution.py:26
  52.0 61.2 %collective-permute-start.23 = (bf16[4,416,128]{2,1,0:T(8,128)(2,1)S(1)}, bf16[4,416,128]{2,1,0:T(8,128)(2,1)S(1)}, u32[]{:S(2)}, u32[]{:S(2)}) collective-permute-start(bf16[4,416,128]{2,1,0:T(8,128)(2,1)S(1)} %pad_maximum_fusion.9), channel_id=1, source_target_pairs={{0,13},{1,14},{2,15},{3,12},{4,1},{5,2},{6,3},{7,0},{8,5},{9,6},{1... | collective-permute-start | bytes 1277960 | tf_op jit(solution)/shard_map/ppermute | solution.py:26
  56.3 18.5 %collective-permute-start.8 = (bf16[2,64,1536]{2,1,0:T(8,128)(2,1)S(1)}, bf16[2,64,1536]{2,1,0:T(8,128)(2,1)S(1)}, u32[]{:S(2)}, u32[]{:S(2)}) collective-permute-start(bf16[2,64,1536]{2,1,0:T(8,128)(2,1)S(1)} %slice.64), channel_id=1, source_target_pairs={{0,1},{1,2},{2,3},{3,0},{4,5},{5,6},{6,7},{7,4},{8,9},{9,10},{10,1... | collective-permute-start | bytes 1179656 | tf_op jit(solution)/shard_map/ppermute | solution.py:26
  56.4 20.5 %collective-permute-start.9 = (bf16[2,64,1536]{2,1,0:T(8,128)(2,1)S(1)}, bf16[2,64,1536]{2,1,0:T(8,128)(2,1)S(1)}, u32[]{:S(2)}, u32[]{:S(2)}) collective-permute-start(bf16[2,64,1536]{2,1,0:T(8,128)(2,1)S(1)} %slice.65), channel_id=1, source_target_pairs={{0,3},{1,0},{2,1},{3,2},{4,7},{5,4},{6,5},{7,6},{8,11},{9,8},{10,9... | collective-permute-start | bytes 1179656 | tf_op jit(solution)/shard_map/ppermute | solution.py:26
  59.8 17.8 %collective-permute-start.15 = (bf16[2,64,1536]{2,1,0:T(8,128)(2,1)S(1)}, bf16[2,64,1536]{2,1,0:T(8,128)(2,1)S(1)}, u32[]{:S(2)}, u32[]{:S(2)}) collective-permute-start(bf16[2,64,1536]{2,1,0:T(8,128)(2,1)S(1)} %slice.68), channel_id=1, source_target_pairs={{0,4},{1,5},{2,6},{3,7},{4,8},{5,9},{6,10},{7,11},{8,12},{9,13},{1... | collective-permute-start | bytes 1179656 | tf_op jit(solution)/shard_map/ppermute | solution.py:26
  68.1 19.3 %collective-permute-start.16 = (bf16[2,64,1536]{2,1,0:T(8,128)(2,1)S(1)}, bf16[2,64,1536]{2,1,0:T(8,128)(2,1)S(1)}, u32[]{:S(2)}, u32[]{:S(2)}) collective-permute-start(bf16[2,64,1536]{2,1,0:T(8,128)(2,1)S(1)} %slice.69), channel_id=1, source_target_pairs={{0,12},{1,13},{2,14},{3,15},{4,0},{5,1},{6,2},{7,3},{8,4},{9,5},{1... | collective-permute-start | bytes 1179656 | tf_op jit(solution)/shard_map/ppermute | solution.py:26
  74.8 46.5 %collective-permute-start.24 = (bf16[4,416,128]{2,1,0:T(8,128)(2,1)S(1)}, bf16[4,416,128]{2,1,0:T(8,128)(2,1)S(1)}, u32[]{:S(2)}, u32[]{:S(2)}) collective-permute-start(bf16[4,416,128]{2,1,0:T(8,128)(2,1)S(1)} %pad_maximum_fusion.10), channel_id=1, source_target_pairs={{0,2},{1,3},{2,0},{3,1},{4,6},{5,7},{6,4},{7,5},{8,10},{9,11},{10,... | collective-permute-start | bytes 1277960 | tf_op jit(solution)/shard_map/ppermute | solution.py:26
  76.9 48.2 %collective-permute-start.25 = (bf16[4,416,128]{2,1,0:T(8,128)(2,1)S(1)}, bf16[4,416,128]{2,1,0:T(8,128)(2,1)S(1)}, u32[]{:S(2)}, u32[]{:S(2)}) collective-permute-start(bf16[4,416,128]{2,1,0:T(8,128)(2,1)S(1)} %pad_maximum_fusion.11), channel_id=1, source_target_pairs={{0,8},{1,9},{2,10},{3,11},{4,12},{5,13},{6,14},{7,15},{8,0},{9,1},... | collective-permute-start | bytes 1277960 | tf_op jit(solution)/shard_map/ppermute | solution.py:26
  77.6 47.5 %collective-permute-start.27 = (bf16[4,416,128]{2,1,0:T(8,128)(2,1)S(1)}, bf16[4,416,128]{2,1,0:T(8,128)(2,1)S(1)}, u32[]{:S(2)}, u32[]{:S(2)}) collective-permute-start(bf16[4,416,128]{2,1,0:T(8,128)(2,1)S(1)} %pad_maximum_fusion.14), channel_id=1, source_target_pairs={{0,1},{1,2},{2,3},{3,0},{4,5},{5,6},{6,7},{7,4},{8,9},{9,10},{10,1... | collective-permute-start | bytes 1277960 | tf_op jit(solution)/shard_map/ppermute | solution.py:26
  96.5 16.4 %collective-permute-start.18 = (bf16[4,1024,128]{2,1,0:T(8,128)(2,1)S(1)}, bf16[4,1024,128]{2,1,0:T(8,128)(2,1)S(1)}, u32[]{:S(2)}, u32[]{:S(2)}) collective-permute-start(bf16[4,1024,128]{2,1,0:T(8,128)(2,1)S(1)} %get-tuple-element.35), channel_id=1, source_target_pairs={{0,16},{1,17},{2,18},{3,19},{4,20},{5,21},{6,22},{7,23},{8,24},{9,... | collective-permute-start | bytes 3145736 | tf_op jit(solution)/shard_map/ppermute | solution.py:26
  112.9 16.3 %collective-permute-start.28 = (bf16[4,416,128]{2,1,0:T(8,128)(2,1)S(1)}, bf16[4,416,128]{2,1,0:T(8,128)(2,1)S(1)}, u32[]{:S(2)}, u32[]{:S(2)}) collective-permute-start(bf16[4,416,128]{2,1,0:T(8,128)(2,1)S(1)} %pad_maximum_fusion.15), channel_id=1, source_target_pairs={{0,4},{1,5},{2,6},{3,7},{4,8},{5,9},{6,10},{7,11},{8,12},{9,13},{1... | collective-permute-start | bytes 1277960 | tf_op jit(solution)/shard_map/ppermute | solution.py:26
  113.2 25.5 %collective-permute-start.29 = (bf16[4,416,128]{2,1,0:T(8,128)(2,1)S(1)}, bf16[4,416,128]{2,1,0:T(8,128)(2,1)S(1)}, u32[]{:S(2)}, u32[]{:S(2)}) collective-permute-start(bf16[4,416,128]{2,1,0:T(8,128)(2,1)S(1)} %pad_maximum_fusion.16), channel_id=1, source_target_pairs={{0,3},{1,0},{2,1},{3,2},{4,7},{5,4},{6,5},{7,6},{8,11},{9,8},{10,9... | collective-permute-start | bytes 1277960 | tf_op jit(solution)/shard_map/ppermute | solution.py:26
  121.3 23.6 %collective-permute-start.30 = (bf16[4,416,128]{2,1,0:T(8,128)(2,1)S(1)}, bf16[4,416,128]{2,1,0:T(8,128)(2,1)S(1)}, u32[]{:S(2)}, u32[]{:S(2)}) collective-permute-start(bf16[4,416,128]{2,1,0:T(8,128)(2,1)S(1)} %pad_maximum_fusion.17), channel_id=1, source_target_pairs={{0,12},{1,13},{2,14},{3,15},{4,0},{5,1},{6,2},{7,3},{8,4},{9,5},{1... | collective-permute-start | bytes 1277960 | tf_op jit(solution)/shard_map/ppermute | solution.py:26
  125.1 19.8 %collective-permute-start.31 = (bf16[4,416,128]{2,1,0:T(8,128)(2,1)S(1)}, bf16[4,416,128]{2,1,0:T(8,128)(2,1)S(1)}, u32[]{:S(2)}, u32[]{:S(2)}) collective-permute-start(bf16[4,416,128]{2,1,0:T(8,128)(2,1)S(1)} %pad_maximum_fusion.18), channel_id=1, source_target_pairs={{0,5},{1,6},{2,7},{3,4},{4,9},{5,10},{6,11},{7,8},{8,13},{9,14},{1... | collective-permute-start | bytes 1277960 | tf_op jit(solution)/shard_map/ppermute | solution.py:26
  125.1 25.3 %collective-permute-start.32 = (bf16[4,416,128]{2,1,0:T(8,128)(2,1)S(1)}, bf16[4,416,128]{2,1,0:T(8,128)(2,1)S(1)}, u32[]{:S(2)}, u32[]{:S(2)}) collective-permute-start(bf16[4,416,128]{2,1,0:T(8,128)(2,1)S(1)} %pad_maximum_fusion.19), channel_id=1, source_target_pairs={{0,15},{1,12},{2,13},{3,14},{4,3},{5,0},{6,1},{7,2},{8,7},{9,4},{1... | collective-permute-start | bytes 1277960 | tf_op jit(solution)/shard_map/ppermute | solution.py:26
  129.2 29.9 %collective-permute-start.33 = (bf16[4,416,128]{2,1,0:T(8,128)(2,1)S(1)}, bf16[4,416,128]{2,1,0:T(8,128)(2,1)S(1)}, u32[]{:S(2)}, u32[]{:S(2)}) collective-permute-start(bf16[4,416,128]{2,1,0:T(8,128)(2,1)S(1)} %pad_maximum_fusion.20), channel_id=1, source_target_pairs={{0,7},{1,4},{2,5},{3,6},{4,11},{5,8},{6,9},{7,10},{8,15},{9,12},{1... | collective-permute-start | bytes 1277960 | tf_op jit(solution)/shard_map/ppermute | solution.py:26
  138.7 84.8 %collective-permute-start.19 = (bf16[4,416,128]{2,1,0:T(8,128)(2,1)S(1)}, bf16[4,416,128]{2,1,0:T(8,128)(2,1)S(1)}, u32[]{:S(2)}, u32[]{:S(2)}) collective-permute-start(bf16[4,416,128]{2,1,0:T(8,128)(2,1)S(1)} %pad_maximum_fusion.5), channel_id=1, source_target_pairs={{0,9},{1,10},{2,11},{3,8},{4,13},{5,14},{6,15},{7,12},{8,1},{9,2},... | collective-permute-start | bytes 1277960 | tf_op jit(solution)/shard_map/ppermute | solution.py:26
  144.9 78.7 %collective-permute-start.20 = (bf16[4,416,128]{2,1,0:T(8,128)(2,1)S(1)}, bf16[4,416,128]{2,1,0:T(8,128)(2,1)S(1)}, u32[]{:S(2)}, u32[]{:S(2)}) collective-permute-start(bf16[4,416,128]{2,1,0:T(8,128)(2,1)S(1)} %pad_maximum_fusion.6), channel_id=1, source_target_pairs={{0,14},{1,15},{2,12},{3,13},{4,2},{5,3},{6,0},{7,1},{8,6},{9,7},{1... | collective-permute-start | bytes 1277960 | tf_op jit(solution)/shard_map/ppermute | solution.py:26
  144.9 78.7 %collective-permute-start.21 = (bf16[4,416,128]{2,1,0:T(8,128)(2,1)S(1)}, bf16[4,416,128]{2,1,0:T(8,128)(2,1)S(1)}, u32[]{:S(2)}, u32[]{:S(2)}) collective-permute-start(bf16[4,416,128]{2,1,0:T(8,128)(2,1)S(1)} %pad_maximum_fusion.7), channel_id=1, source_target_pairs={{0,11},{1,8},{2,9},{3,10},{4,15},{5,12},{6,13},{7,14},{8,3},{9,0},... | collective-permute-start | bytes 1277960 | tf_op jit(solution)/shard_map/ppermute | solution.py:26
  150.4 73.1 %collective-permute-start.22 = (bf16[4,416,128]{2,1,0:T(8,128)(2,1)S(1)}, bf16[4,416,128]{2,1,0:T(8,128)(2,1)S(1)}, u32[]{:S(2)}, u32[]{:S(2)}) collective-permute-start(bf16[4,416,128]{2,1,0:T(8,128)(2,1)S(1)} %pad_maximum_fusion.8), channel_id=1, source_target_pairs={{0,10},{1,11},{2,8},{3,9},{4,14},{5,15},{6,12},{7,13},{8,2},{9,3},... | collective-permute-start | bytes 1277960 | tf_op jit(solution)/shard_map/ppermute | solution.py:26
  159.1 43.3 %collective-permute-start.26 = (bf16[4,416,128]{2,1,0:T(8,128)(2,1)S(1)}, bf16[4,416,128]{2,1,0:T(8,128)(2,1)S(1)}, u32[]{:S(2)}, u32[]{:S(2)}) collective-permute-start(bf16[4,416,128]{2,1,0:T(8,128)(2,1)S(1)} %pad_maximum_fusion.12), channel_id=1, source_target_pairs={{0,6},{1,7},{2,4},{3,5},{4,10},{5,11},{6,8},{7,9},{8,14},{9,15},{1... | collective-permute-start | bytes 1277960 | tf_op jit(solution)/shard_map/ppermute | solution.py:26
  202.4 50.0 %collective-permute-start.39 = (bf16[128,6144]{1,0:T(8,128)(2,1)S(1)}, bf16[128,6144]{1,0:T(8,128)(2,1)}, u32[]{:S(2)}, u32[]{:S(2)}) collective-permute-start(bf16[128,6144]{1,0:T(8,128)(2,1)S(1)} %bitcast.73), channel_id=1, source_target_pairs={{0,16},{1,17},{2,18},{3,19},{4,20},{5,21},{6,22},{7,23},{8,24},{9,... | collective-permute-start | bytes 4718600 | tf_op jit(solution)/shard_map/ppermute | solution.py:26
  234.7 17.2 %collective-permute-start.35 = (bf16[2,512,128]{2,1,0:T(8,128)(2,1)S(1)}, bf16[2,512,128]{2,1,0:T(8,128)(2,1)S(1)}, u32[]{:S(2)}, u32[]{:S(2)}) collective-permute-start(bf16[2,512,128]{2,1,0:T(8,128)(2,1)S(1)} %dynamic-slice_convert_fusion), channel_id=1, source_target_pairs={{0,16},{1,17},{2,18},{3,19},{4,20},{5,21},{6,22},{7,23},{8,24},{9,... | collective-permute-start | bytes 786440 | tf_op jit(solution)/shard_map/ppermute | solution.py:26
  236.5 15.2 %collective-permute-start.34 = (f32[2,512]{1,0:T(2,128)S(1)}, f32[2,512]{1,0:T(2,128)S(1)}, u32[]{:S(2)}, u32[]{:S(2)}) collective-permute-start(f32[2,512]{1,0:T(2,128)S(1)} %bitcast.86), channel_id=1, source_target_pairs={{0,16},{1,17},{2,18},{3,19},{4,20},{5,21},{6,22},{7,23},{8,24},{9,... | collective-permute-start | bytes 12296 | tf_op jit(solution)/shard_map/ppermute | solution.py:26
  252.3 25.2 %collective-permute-start.36 = (bf16[512,256]{1,0:T(8,128)(2,1)S(1)}, bf16[512,256]{1,0:T(8,128)(2,1)S(1)}, u32[]{:S(2)}, u32[]{:S(2)}) collective-permute-start(bf16[512,256]{1,0:T(8,128)(2,1)S(1)} %pad_maximum_fusion.21), channel_id=1, source_target_pairs={{0,1},{1,2},{2,3},{3,0},{4,5},{5,6},{6,7},{7,4},{8,9},{9,10},{10,1... | collective-permute-start | bytes 786440 | tf_op jit(solution)/shard_map/ppermute | solution.py:26
  252.4 25.2 %collective-permute-start.37 = (bf16[512,256]{1,0:T(8,128)(2,1)S(1)}, bf16[512,256]{1,0:T(8,128)(2,1)S(1)}, u32[]{:S(2)}, u32[]{:S(2)}) collective-permute-start(bf16[512,256]{1,0:T(8,128)(2,1)S(1)} %pad_maximum_fusion.21), channel_id=1, source_target_pairs={{0,2},{1,3},{2,0},{3,1},{4,6},{5,7},{6,4},{7,5},{8,10},{9,11},{10,... | collective-permute-start | bytes 786440 | tf_op jit(solution)/shard_map/ppermute | solution.py:26
  254.2 43.5 %collective-permute-start.42 = (bf16[256,1536]{1,0:T(8,128)(2,1)S(1)}, bf16[256,1536]{1,0:T(8,128)(2,1)S(1)}, u32[]{:S(2)}, u32[]{:S(2)}) collective-permute-start(bf16[256,1536]{1,0:T(8,128)(2,1)S(1)} %get-tuple-element.130), channel_id=1, source_target_pairs={{0,3},{1,0},{2,1},{3,2},{4,7},{5,4},{6,5},{7,6},{8,11},{9,8},{10,9... | collective-permute-start | bytes 2359304 | tf_op jit(solution)/shard_map/ppermute | solution.py:26
  256.1 41.5 %collective-permute-start.41 = (bf16[256,1536]{1,0:T(8,128)(2,1)S(1)}, bf16[256,1536]{1,0:T(8,128)(2,1)S(1)}, u32[]{:S(2)}, u32[]{:S(2)}) collective-permute-start(bf16[256,1536]{1,0:T(8,128)(2,1)S(1)} %get-tuple-element.129), channel_id=1, source_target_pairs={{0,2},{1,3},{2,0},{3,1},{4,6},{5,7},{6,4},{7,5},{8,10},{9,11},{10,... | collective-permute-start | bytes 2359304 | tf_op jit(solution)/shard_map/ppermute | solution.py:26
  259.1 38.6 %collective-permute-start.40 = (bf16[256,1536]{1,0:T(8,128)(2,1)S(1)}, bf16[256,1536]{1,0:T(8,128)(2,1)S(1)}, u32[]{:S(2)}, u32[]{:S(2)}) collective-permute-start(bf16[256,1536]{1,0:T(8,128)(2,1)S(1)} %get-tuple-element.128), channel_id=1, source_target_pairs={{0,1},{1,2},{2,3},{3,0},{4,5},{5,6},{6,7},{7,4},{8,9},{9,10},{10,1... | collective-permute-start | bytes 2359304 | tf_op jit(solution)/shard_map/ppermute | solution.py:26
  277.5 20.2 %collective-permute-start.38 = (bf16[512,256]{1,0:T(8,128)(2,1)S(1)}, bf16[512,256]{1,0:T(8,128)(2,1)S(1)}, u32[]{:S(2)}, u32[]{:S(2)}) collective-permute-start(bf16[512,256]{1,0:T(8,128)(2,1)S(1)} %pad_maximum_fusion.21), channel_id=1, source_target_pairs={{0,3},{1,0},{2,1},{3,2},{4,7},{5,4},{6,5},{7,6},{8,11},{9,8},{10,9... | collective-permute-start | bytes 786440 | tf_op jit(solution)/shard_map/ppermute | solution.py:26
  299.8 22.5 %collective-permute-start.45 = (bf16[128,1536]{1,0:T(8,128)(2,1)S(1)}, bf16[128,1536]{1,0:T(8,128)(2,1)S(1)}, u32[]{:S(2)}, u32[]{:S(2)}) collective-permute-start(bf16[128,1536]{1,0:T(8,128)(2,1)S(1)} %get-tuple-element.132), channel_id=1, source_target_pairs={{0,12},{1,13},{2,14},{3,15},{4,0},{5,1},{6,2},{7,3},{8,4},{9,5},{1... | collective-permute-start | bytes 1179656 | tf_op jit(solution)/shard_map/ppermute | solution.py:26
  305.6 16.8 %collective-permute-start.44 = (bf16[128,1536]{1,0:T(8,128)(2,1)S(1)}, bf16[128,1536]{1,0:T(8,128)(2,1)}, u32[]{:S(2)}, u32[]{:S(2)}) collective-permute-start(bf16[128,1536]{1,0:T(8,128)(2,1)S(1)} %get-tuple-element.133), channel_id=1, source_target_pairs={{0,8},{1,9},{2,10},{3,11},{4,12},{5,13},{6,14},{7,15},{8,0},{9,1},... | collective-permute-start | bytes 1179656 | tf_op jit(solution)/shard_map/ppermute | solution.py:26
  305.6 20.3 %collective-permute-start.43 = (bf16[128,1536]{1,0:T(8,128)(2,1)S(1)}, bf16[128,1536]{1,0:T(8,128)(2,1)}, u32[]{:S(2)}, u32[]{:S(2)}) collective-permute-start(bf16[128,1536]{1,0:T(8,128)(2,1)S(1)} %get-tuple-element.131), channel_id=1, source_target_pairs={{0,4},{1,5},{2,6},{3,7},{4,8},{5,9},{6,10},{7,11},{8,12},{9,13},{1... | collective-permute-start | bytes 1179656 | tf_op jit(solution)/shard_map/ppermute | solution.py:26
  327.3 11.7 %collective-permute-start = (bf16[32,6144]{1,0:T(8,128)(2,1)S(1)}, bf16[32,6144]{1,0:T(8,128)(2,1)S(1)}, u32[]{:S(2)}, u32[]{:S(2)}) collective-permute-start(bf16[32,6144]{1,0:T(8,128)(2,1)S(1)} %bitcast.72), channel_id=1, source_target_pairs={{0,32},{32,64},{64,96},{96,0},{1,33},{33,65},{65,97},{97,1},{2,34}... | collective-permute-start | bytes 1179656 | tf_op jit(solution)/shard_map/ppermute | solution.py:41
  327.4 11.6 %collective-permute-start.1 = (f32[1,6144]{1,0:T(1,128)}, f32[1,6144]{1,0:T(1,128)S(1)}, u32[]{:S(2)}, u32[]{:S(2)}) collective-permute-start(f32[1,6144]{1,0:T(1,128)} %param.14), channel_id=1, source_target_pairs={{0,32},{32,64},{64,96},{96,0},{1,33},{33,65},{65,97},{97,1},{2,34}... | collective-permute-start | bytes 73736 | tf_op jit(solution)/shard_map/ppermute | solution.py:41
  328.7 7.3 %collective-permute-start.48 = (bf16[32,1536]{1,0:T(8,128)(2,1)S(1)}, bf16[32,1536]{1,0:T(8,128)(2,1)S(1)}, u32[]{:S(2)}, u32[]{:S(2)}) collective-permute-start(bf16[32,1536]{1,0:T(8,128)(2,1)S(1)} %get-tuple-element.147), channel_id=1, source_target_pairs={{0,34},{1,35},{2,32},{3,33},{4,38},{5,39},{6,36},{7,37},{8,42},{9,... | collective-permute-start | bytes 294920 | tf_op jit(solution)/shard_map/ppermute | solution.py:35
  331.3 6.6 %collective-permute-start.49 = (bf16[32,1536]{1,0:T(8,128)(2,1)S(1)}, bf16[32,1536]{1,0:T(8,128)(2,1)S(1)}, u32[]{:S(2)}, u32[]{:S(2)}) collective-permute-start(bf16[32,1536]{1,0:T(8,128)(2,1)S(1)} %get-tuple-element.146), channel_id=1, source_target_pairs={{0,35},{1,32},{2,33},{3,34},{4,39},{5,36},{6,37},{7,38},{8,43},{9,... | collective-permute-start | bytes 294920 | tf_op jit(solution)/shard_map/ppermute | solution.py:35
  (12 other events, 185.3 us)

commit v2 on v0

v2 whole, which is shorter than its diff:
```python
import functools

import jax
import jax.numpy as jnp
from jax import lax
from jax.experimental import pallas as pl
from jax.experimental.pallas import tpu as pltpu
from jax.sharding import PartitionSpec as P

HD = 128
NZ, NY, NX = 2, 4, 4
COUNT = NZ * NY * NX
PLANE = NY * NX
LOG2E = 1.4426950408889634
LOWEST = -1e30
BF = jnp.bfloat16
F32 = jnp.float32


def moved(value, dz=0, dy=0, dx=0):
    pairs = []
    for source in range(COUNT):
        z, y, x = source // PLANE, source // NX % NY, source % NX
        target = (z + dz) % NZ * PLANE + (y + dy) % NY * NX + (x + dx) % NX
        pairs.append((source, target))
    return lax.ppermute(value, "seq", pairs)


def onward(value, sections, dx):
    pairs = []
    for section in range(sections):
        for source in range(COUNT):
            target = source // NX * NX + (source % NX + dx) % NX
            pairs.append((section * COUNT + source, (section + 1) % sections * COUNT + target))
    return lax.ppermute(value, ("section", "seq"), pairs)


def from_behind(value, axis, steps):
    count = lax.axis_size(axis)
    pairs = [(source, (source + steps) % count) for source in range(count)]
    return lax.ppermute(value, axis, pairs)


def after(value, *others):
    return lax.optimization_barrier((value,) + others)[0]


def lay_out_kernel(turn, k_ref, v_ref, out_ref):
    for which, ref in enumerate((k_ref, v_ref)):
        for step in range(NZ):
            base = step * PLANE * HD
            for unit in range(PLANE):
                column = base + unit * HD
                out_ref[unit, which * NZ + step] = ref[:, column : column + HD]


def lay_out(turn, keys, values, begin, length):
    rows = 32
    wide = keys.shape[1]
    block = pl.BlockSpec((rows, wide), lambda i: (begin // rows + i, 0))
    return pl.pallas_call(
        lay_out_kernel,
        grid=(length // rows,),
        out_shape=jax.ShapeDtypeStruct((PLANE, 2 * NZ, length, HD), BF),
        in_specs=[pl.BlockSpec(memory_space=pltpu.SMEM), block, block],
        out_specs=pl.BlockSpec((PLANE, 2 * NZ, rows, HD), lambda i: (0, 0, i, 0)),
        compiler_params=pltpu.CompilerParams(vmem_limit_bytes=56 * 2**20),
        cost_estimate=pl.CostEstimate(flops=0, bytes_accessed=PLANE * 4 * NZ * length * HD * 2, transcendentals=0),
    )(turn, keys, values)


def project_kernel(spot, x_hbm, *refs):
    w_hbm, (q_ref, kv_ref, x_ref, w_ref, x_sem, w_sem) = refs[:6], refs[6:]
    tile = x_ref.shape[0] // 2
    x_copies, w_copies = [], []
    for t in range(2):
        some = pl.ds(t * tile, tile)
        x_copies.append(pltpu.make_async_copy(x_hbm.at[some], x_ref.at[some], x_sem.at[t]))
    for at, ref in enumerate(w_hbm):
        w_copies.append(pltpu.make_async_copy(ref, w_ref.at[at // 2, :, pl.ds(at % 2 * HD, HD)], w_sem.at[at]))
    for copy in x_copies[:1] + w_copies[:2] + x_copies[1:] + w_copies[2:]:
        copy.start()
    for kind in range(3):
        for copy in w_copies[2 * kind : 2 * kind + 2]:
            copy.wait()
        for t in range(2):
            if kind == 0:
                x_copies[t].wait()
            some = slice(t * tile, (t + 1) * tile)
            part = jnp.dot(x_ref[some, :], w_ref[kind], preferred_element_type=F32)
            for other in range(NZ):
                head = lax.rem(spot[0] + other, NZ)
                one = part[:, other * HD : (other + 1) * HD]
                if kind == 0:
                    q_ref[head, some, :] = (one * (LOG2E / HD**0.5)).astype(BF)
                else:
                    kv_ref[(kind - 1) * NZ + head, some, :] = one.astype(BF)


def project(spot, normed, weights):
    patch, depth = normed.shape
    vmem = pl.BlockSpec(memory_space=pltpu.VMEM)
    return pl.pallas_call(
        project_kernel,
        out_shape=(jax.ShapeDtypeStruct((NZ, patch, HD), BF), jax.ShapeDtypeStruct((2 * NZ, patch, HD), BF)),
        in_specs=[pl.BlockSpec(memory_space=pltpu.SMEM)] + [pl.BlockSpec(memory_space=pl.ANY)] * 7,
        out_specs=(vmem, vmem),
        scratch_shapes=[
            pltpu.VMEM((patch, depth), BF),
            pltpu.VMEM((3, depth, 2 * HD), BF),
            pltpu.SemaphoreType.DMA((2,)),
            pltpu.SemaphoreType.DMA((6,)),
        ],
        compiler_params=pltpu.CompilerParams(vmem_limit_bytes=58 * 2**20),
        cost_estimate=pl.CostEstimate(
            flops=12 * patch * depth * HD, bytes_accessed=2 * depth * (patch + 6 * HD) + 12 * patch * HD, transcendentals=0
        ),
    )(spot, normed, *weights)


def attend_kernel(spot, here_ref, there_ref, kv_ref, *refs, fresh, first, last, begin, length, patch):
    refs = list(refs)
    if fresh:
        fresh_ref = refs.pop(0)
    if not first:
        acc_in, m_in = refs[:2]
        refs = refs[2:]
    out_refs, (v_wide, acc, m) = refs[:-3], refs[-3:]
    sources, _, share, _ = kv_ref.shape
    size = sources * share
    heads, part, _ = here_ref.shape
    rows = 2 * part
    step = pl.program_id(0)
    sub = 256

    @pl.when(step == 0)
    def _():
        v_wide[:, :, HD:] = jnp.ones((heads, v_wide.shape[1], HD), BF)
        if first:
            m[...] = jnp.full(m.shape, LOWEST, F32)
            acc[...] = jnp.zeros(acc.shape, F32)
        else:
            m[...] = m_in[...]
            acc[...] = acc_in[...]

    def update(keys, count, gone):
        chains = [(head, at) for head in range(heads) for at in range(0, rows, sub)]
        scores = [
            lax.dot_general(
                (here_ref if at < part else there_ref)[head, at % part : at % part + sub],
                keys[head],
                (((1,), (1,)), ((), ())),
                preferred_element_type=F32,
            )
            for head, at in chains
        ]
        for (head, at), s in zip(chains, scores):
            if gone is not None:
                s = jnp.where(gone, LOWEST, s)
            m_old = m[head, at : at + sub]
            m_new = jnp.maximum(m_old, jnp.max(s, axis=1, keepdims=True))
            p = jnp.exp2(s - m_new[:, :1])
            alpha = jnp.exp2(m_old - m_new)
            acc[head, at : at + sub] = jnp.concatenate((alpha, alpha), axis=1) * acc[head, at : at + sub] + jnp.dot(
                p.astype(BF), v_wide[head, :count], preferred_element_type=F32
            )
            m[head, at : at + sub] = m_new

    def low(at):
        return spot[3] - (spot[0] * PLANE + step * sources + at) * length - begin

    touched = jnp.bool_(False)
    for at in range(sources):
        touched = touched | ((low(at) < share) & (low(at) + patch > 0))
    keys = [kv_ref[:, head].reshape(size, HD) for head in range(heads)]
    for head in range(heads):
        v_wide[head, :size, :HD] = kv_ref[:, heads + head].reshape(size, HD)

    @pl.when(touched)
    def _():
        column = lax.broadcasted_iota(jnp.int32, (1, size), 1)
        gone = jnp.zeros((1, size), jnp.int32)
        for at in range(sources):
            start = at * share + jnp.clip(low(at), 0, share)
            end = at * share + jnp.clip(low(at) + patch, 0, share)
            gone = jnp.where((column >= start) & (column < end), 1, gone)
        update(keys, size, gone > 0)

    @pl.when(jnp.logical_not(touched))
    def _():
        update(keys, size, None)

    @pl.when(step == pl.num_programs(0) - 1)
    def _():
        if fresh:
            count = fresh_ref.shape[1]
            for head in range(heads):
                v_wide[head, :count, :HD] = fresh_ref[heads + head]
            update([fresh_ref[head] for head in range(heads)], count, None)
        if last:
            for start, o_ref, lse_ref in ((0, *out_refs[:2]), (part, *out_refs[2:])):
                some = slice(start, start + part)
                for head in range(heads):
                    both = acc[head, some, :]
                    o_ref[head] = (both[:, :HD] / both[:, HD:]).astype(o_ref.dtype)
                    lse_ref[head] = jnp.transpose(m[head, some, :] + jnp.log2(both[:, HD:]))[:8, :]
        else:
            out_refs[0][...] = acc[...]
            out_refs[1][...] = m[...]


def attend(spot, q, stale, fresh, state, last, begin, length, patch, steps):
    heads, rows, _ = q[0].shape
    rows *= 2
    share = stale.shape[2]
    first = state is None
    whole = lambda shape: pl.BlockSpec(shape, lambda g, spot: (0,) * len(shape))
    sources = PLANE // steps
    inputs = [*q, stale]
    specs = [whole(q[0].shape), whole(q[1].shape), pl.BlockSpec((sources, 2 * heads, share, HD), lambda g, spot: (g, 0, 0, 0))]
    count = sources * share
    if fresh is not None:
        inputs.append(fresh)
        specs.append(whole(fresh.shape))
        count = max(count, fresh.shape[1])
    scratch = [pltpu.VMEM((heads, count, 2 * HD), BF), pltpu.VMEM((heads, rows, 2 * HD), F32), pltpu.VMEM((heads, rows, HD), F32)]
    if not first:
        inputs += list(state)
        specs += [whole(part.shape) for part in state]
    shapes = [((heads, rows, 2 * HD), F32), ((heads, rows, HD), F32)]
    if last:
        lse = ((heads, 8, rows // 2), F32)
        shapes = [((heads, rows // 2, HD), F32), lse, ((heads, rows // 2, HD), BF), lse]
    tokens = PLANE * share + (0 if fresh is None else fresh.shape[1])
    return pl.pallas_call(
        functools.partial(
            attend_kernel, fresh=fresh is not None, first=first, last=last, begin=begin, length=length, patch=patch
        ),
        grid_spec=pltpu.PrefetchScalarGridSpec(
            num_scalar_prefetch=1,
            grid=(steps,),
            in_specs=specs,
            out_specs=tuple(whole(shape) for shape, _ in shapes),
            scratch_shapes=scratch,
        ),
        out_shape=tuple(jax.ShapeDtypeStruct(*one) for one in shapes),
        compiler_params=pltpu.CompilerParams(vmem_limit_bytes=56 * 2**20),
        cost_estimate=pl.CostEstimate(
            flops=heads * rows * tokens * HD * 8, bytes_accessed=heads * tokens * HD * 4, transcendentals=heads * rows * tokens
        ),
    )(spot, *inputs)


def body(
    tokens,
    mod_shift,
    mod_scale,
    mod_gate,
    w_query,
    w_key,
    w_value,
    w_out,
    stale_keys,
    stale_values,
    patch_index,
):
    sections = lax.axis_size("section")
    me = lax.axis_index("seq")
    z, y, x = me // PLANE, me // NX % NY, me % NX
    rows, width = tokens.shape[1:]
    patch = COUNT * rows
    length = stale_keys.shape[1]
    spot = jnp.stack([z, y, x, patch_index[0] * patch]).astype(jnp.int32)
    planes = [list(range(plane * PLANE, (plane + 1) * PLANE)) for plane in range(NZ)]

    def stale_laid(begin, share, *deps):
        return lay_out(after(spot[:1], *deps) if deps else spot[:1], stale_keys[0], stale_values[0], begin, share)

    def stale_share(laid, *deps):
        laid = after(laid, *deps) if deps else laid
        return lax.all_to_all(laid, "seq", split_axis=0, concat_axis=0, tiled=True, axis_index_groups=planes)

    weights = []
    for w in (w_query, w_key, w_value):
        weights += [w[0], moved(w[0], dz=1)]

    inputs = tokens[0].astype(F32)
    meansq = jnp.mean(inputs * inputs, axis=-1, keepdims=True)
    normed = (inputs * lax.rsqrt(meansq + 1e-06) * (1.0 + mod_scale[0]) + mod_shift[0]).astype(BF)
    normed = lax.all_gather(normed, "seq", axis=0, tiled=True, axis_index_groups=planes)

    wide = width // NX
    w_slices, w_parts = [], []
    for k in range(NX):
        w_slices.append(lax.dynamic_slice(w_out[0], (0, (x + k) % NX * wide), (HD, wide)))
        w_parts.append(moved(w_slices[k], dx=k) if k else w_slices[k])
    normed, weights, w_parts = lax.optimization_barrier((normed, weights, w_parts))
    w_plane = jnp.concatenate(w_parts, axis=0)

    early = 6 * rows
    stale_first = stale_share(stale_laid(0, early, *w_slices))
    stale_second = stale_share(stale_laid(early, length - early), normed)

    q, fresh = project(spot, normed, weights)
    q = (q, moved(q, dz=1))
    tokens_behind = from_behind(after(tokens[0], q[1]), "section", 1)
    gate_behind = from_behind(after(mod_gate, q[1]), "section", 1)
    w_other = moved(w_plane, dz=1)
    spot, w_other = lax.optimization_barrier((spot, w_other))

    state = attend(spot, q, stale_first, fresh, None, False, 0, length, patch, 4)
    w_columns = jnp.concatenate((jnp.where(z == 0, w_plane, w_other), jnp.where(z == 0, w_other, w_plane)), axis=0)
    o_here, lse_here, o_there, lse_there = attend(spot, q, stale_second, None, state, True, early, length, patch, 4)

    o_got = moved(o_there, dz=1).astype(F32)
    lse_got = moved(lse_there, dz=1)
    part_here = (1.0 / (1.0 + jnp.exp2(lse_got - lse_here)))[:, 0, :, None]
    attended = (o_here * part_here + o_got * (1.0 - part_here)).astype(BF)
    attended = jnp.concatenate((attended[0], attended[1]), axis=1)

    along = [attended] + [moved(attended, dx=k) for k in range(1, NX)]
    gathered = jnp.concatenate([a[:, :HD] for a in along] + [a[:, HD:] for a in along], axis=1)
    partial = jnp.dot(gathered, w_columns, preferred_element_type=F32).astype(BF)
    band = NX * rows
    total = lax.dynamic_slice(partial, (y * band, 0), (band, wide)).astype(F32)
    for k in range(1, NY):
        part = lax.dynamic_slice(partial, ((y + k) % NY * band, 0), (band, wide))
        total = total + moved(part, dy=k).astype(F32)
    total = total.astype(BF)
    projected = jnp.zeros((rows, width), BF)
    for k in range(NX):
        part = onward(lax.dynamic_slice(total, ((x + k) % NX * rows, 0), (rows, wide)), sections, k)
        projected = lax.dynamic_update_slice(projected, part, (0, (x - k) % NX * wide))
    updated = tokens_behind.astype(F32) + gate_behind * projected.astype(F32)
    return updated.astype(BF)[None]


def solution(mesh):
    placed = (
        P("section", "seq", None),
        P("section", None),
        P("section", None),
        P("section", None),
        P("section", None, "seq"),
        P("section", None, "seq"),
        P("section", None, "seq"),
        P("section", "seq", None),
        P("section", "seq", None),
        P("section", "seq", None),
        P("section"),
    )
    return jax.shard_map(
        body, mesh=mesh, in_specs=placed, out_specs=P("section", "seq", None), check_vma=False
    )
```

time: 548 us -> 282 us (0.51)
  waiting for transfers between devices: 417 us -> 143 us
  matrix products: 61.2 us -> 1.8 us
  Pallas kernels: 0 us -> 55.9 us
  starting transfers between devices: 17.9 us -> 48.7 us
  other arithmetic: 22.9 us -> 9.26 us
  local copies, waits for them, and re-layouts: 13.5 us -> 7.01 us
    reduce_scatter x1 -> x0, waiting for transfers between devices: 249 us -> none  [body(): lax.psum_scatter(jnp.dot(attended, w_out[0], preferred_element_type=jnp.f...]
    ppermute x0 -> x20, waiting for transfers between devices: none -> 143 us  [the longest x16 138 us: moved(): return lax.ppermute(value, 'seq', pairs)]
    all_gather x1, waiting for transfers between devices: 121 us -> 0.01 us  [body(): lax.all_gather(normed, 'seq', axis=0, tiled=True, axis_index_groups=planes)]
    dot_general x3 -> x1, matrix products: 61.2 us -> 1.8 us  [body(): jnp.dot(gathered, w_columns, preferred_element_type=F32).astype(BF)]
    pallas_call x0 -> x5, Pallas kernels: none -> 55.9 us  [the longest x2 31.8 us: attend(): pl.pallas_call(functools.partial(attend_kernel, fresh=fresh is not None,...]
    all_to_all x2, waiting for transfers between devices: 40.4 us -> 0.01 us  [stale_share(): lax.all_to_all(laid, 'seq', split_axis=0, concat_axis=0, tiled=True, axis...]
    ppermute x0 -> x20, starting transfers between devices: none -> 32.9 us  [the longest x16 27.6 us: moved(): return lax.ppermute(value, 'seq', pairs)]
    reduce_sum x1 -> x0, other arithmetic: 17.8 us -> none  [body(): probs = jax.nn.softmax(scores, axis=-1).astype(jnp.bfloat16)]
  transfers between devices with their start and end apart: 5 -> 25, of which waited for: 4 -> 17; matrix products, arithmetic and copies ran while one was open for 4% -> 2% of each run, Pallas kernels for 0% -> 14%
where the time goes in v2:
time: 282 us; the launch traced here: 280 us
  waiting for transfers between devices  143 us (51%)
  Pallas kernels  55.9 us (20%)
  starting transfers between devices  48.7 us (17%)
  between operations  14.5 us (5%)
  other arithmetic  9.26 us (3%)
  local copies, waits for them, and re-layouts  7.01 us (2%)
    ppermute x16, waiting for transfers between devices, moved(): return lax.ppermute(value, 'seq', pairs)  138 us
    pallas_call x2, Pallas kernels, attend(): pl.pallas_call(functools.partial(attend_kernel, fresh=fresh is not None,...  31.8 us
    ppermute x16, starting transfers between devices, moved(): return lax.ppermute(value, 'seq', pairs)  27.6 us
    all_to_all x2, starting transfers between devices, stale_share(): lax.all_to_all(laid, 'seq', split_axis=0, concat_axis=0, tiled=True, axis...  14.7 us
    pallas_call x1, Pallas kernels, project(): pl.pallas_call(project_kernel, out_shape=(jax.ShapeDtypeStruct((NZ, patch...  12.4 us
    pallas_call x2, Pallas kernels, lay_out(): pl.pallas_call(lay_out_kernel, grid=(length // rows,), out_shape=jax.Shap...  11.7 us
  transfers between devices with their start and end apart: 25, of which 17 were waited for; matrix products, arithmetic and copies ran while one was open for 2% of the time, Pallas kernels for 14%

profile of v2, /device:TPU:2, one launch (start us, length us, event | category | flops | bytes accessed | tf_op | source)
XLA Modules:
  0.0 280.3 jit_solution(1774699338247733540)
XLA Ops:
  6.5 0.9 broadcast_add_fusion
  7.4 1.2 fusion.7
  8.6 2.0 fusion.10
  10.7 1.1 dynamic-slice_bitcast_fusion
  11.8 5.5 %shard_map.111 = bf16[16,4,192,128]{3,2,1,0:T(8,128)(2,1)} custom-call(s32[1]{0:T(128)} %bitcast.1.turn, bf16[416,4096]{1,0:T(8,128)(2,1)} %bitcast.38, bf16[416,4096]{1,0:T(8,128)(2,1)} %bitcast.40), custom_call_target="tpu_custom_call" | custom-call | bytes 6291456 | tf_op jit(solution)/shard_map/pallas_call | solution.py:61
  17.2 7.5 %all-to-all-start.1 = ((bf16[16,4,192,128]{3,2,1,0:T(8,128)(2,1)}), bf16[16,4,192,128]{3,2,1,0:T(8,128)(2,1)S(1)}, u32[]{:S(2)}, u32[]{:S(2)}) async-start(bf16[16,4,192,128]{3,2,1,0:T(8,128)(2,1)} %shard_map.111), calls=%async_computation.1 | async-start | bytes 6291456 | tf_op jit(solution)/shard_map/all_to_all | solution.py:281
  24.7 3.9 %collective-permute-start = (bf16[6144,128]{1,0:T(8,128)(2,1)}, bf16[6144,128]{1,0:T(8,128)(2,1)}, u32[]{:S(2)}, u32[]{:S(2)}) collective-permute-start(bf16[6144,128]{1,0:T(8,128)(2,1)} %bitcast.47), channel_id=1, source_target_pairs={{0,16},{1,17},{2,18},{3,19},{4,20},{5,21},{6,22},{7,23},{8,24},{9,... | collective-permute-start | bytes 4718600 | tf_op jit(solution)/shard_map/ppermute | solution.py:26
  28.7 3.4 %collective-permute-start.2 = (bf16[6144,128]{1,0:T(8,128)(2,1)}, bf16[6144,128]{1,0:T(8,128)(2,1)}, u32[]{:S(2)}, u32[]{:S(2)}) collective-permute-start(bf16[6144,128]{1,0:T(8,128)(2,1)} %bitcast.51), channel_id=1, source_target_pairs={{0,16},{1,17},{2,18},{3,19},{4,20},{5,21},{6,22},{7,23},{8,24},{9,... | collective-permute-start | bytes 4718600 | tf_op jit(solution)/shard_map/ppermute | solution.py:26
  32.1 1.5 collective-permute-start.3
  34.4 49.8 %collective-permute-done.3 = bf16[128,1536]{1,0:T(8,128)(2,1)} collective-permute-done((bf16[128,1536]{1,0:T(8,128)(2,1)}, bf16[128,1536]{1,0:T(8,128)(2,1)}, u32[]{:S(2)}, u32[]{:S(2)}) %collective-permute-start.3) | collective-permute-done | bytes 393248 | tf_op jit(solution)/shard_map/ppermute | solution.py:26
  84.2 6.2 %shard_map.110 = bf16[16,4,224,128]{3,2,1,0:T(8,128)(2,1)} custom-call(s32[1]{0:T(128)} %bitcast.1.turn, bf16[416,4096]{1,0:T(8,128)(2,1)} %bitcast.39, bf16[416,4096]{1,0:T(8,128)(2,1)} %bitcast.41), custom_call_target="tpu_custom_call" | custom-call | bytes 7340032 | tf_op jit(solution)/shard_map/pallas_call | solution.py:61
  90.4 17.9 %collective-permute-done.5 = bf16[128,1536]{1,0:T(8,128)(2,1)} collective-permute-done((bf16[128,1536]{1,0:T(8,128)(2,1)}, bf16[128,1536]{1,0:T(8,128)(2,1)}, u32[]{:S(2)}, u32[]{:S(2)}) %collective-permute-start.5) | collective-permute-done | bytes 393248 | tf_op jit(solution)/shard_map/ppermute | solution.py:26
  108.3 21.8 %collective-permute-done.2.refs_5_ = bf16[6144,128]{1,0:T(8,128)(2,1)} collective-permute-done((bf16[6144,128]{1,0:T(8,128)(2,1)}, bf16[6144,128]{1,0:T(8,128)(2,1)}, u32[]{:S(2)}, u32[]{:S(2)}) %collective-permute-start.2) | collective-permute-done | bytes 1572896 | tf_op jit(solution)/shard_map/ppermute | solution.py:26
  130.2 1.6 copy-done
  131.8 7.2 %all-to-all-start = ((bf16[16,4,224,128]{3,2,1,0:T(8,128)(2,1)}), bf16[16,4,224,128]{3,2,1,0:T(8,128)(2,1)}, u32[]{:S(2)}, u32[]{:S(2)}) async-start(bf16[16,4,224,128]{3,2,1,0:T(8,128)(2,1)} %shard_map.110), calls=%async_computation | async-start | bytes 7340032 | tf_op jit(solution)/shard_map/all_to_all | solution.py:281
  139.0 1.0 constant_dynamic-update-slice_fusion.2
  140.1 1.0 constant_dynamic-update-slice_fusion.1
  141.1 1.0 constant_dynamic-update-slice_fusion
  142.1 3.3 %collective-permute-start.9 = (bf16[512,1536]{1,0:T(8,128)(2,1)S(1)}, bf16[512,1536]{1,0:T(8,128)(2,1)S(1)}, u32[]{:S(2)}, u32[]{:S(2)}) collective-permute-start(bf16[512,1536]{1,0:T(8,128)(2,1)S(1)} %constant_dynamic-update-slice_fusion), channel_id=1, source_target_pairs={{0,16},{1,17},{2,18},{3,19},{4,20},{5,21},{6,22},{7,23},{8,24},{9,... | collective-permute-start | bytes 4718600 | tf_op jit(solution)/shard_map/ppermute | solution.py:26
  146.8 12.4 %shard_map.109 = (bf16[2,512,128]{2,1,0:T(8,128)(2,1)}, bf16[4,512,128]{2,1,0:T(8,128)(2,1)}) custom-call(s32[4]{0:T(128)} %pad_add_fusion.spot, bf16[512,6144]{1,0:T(8,128)(2,1)} %all-gather.2.cloned.1.call-done.x_hbm, bf16[6144,128]{1,0:T(8,128)(2,1)} %bitcast.48, bf16[6144,128]{1,0:T(8,128)(2,1)} %collective-permute-done.refs_1_, ...), custom_call_target="tpu_custom_call" | custom-call | flops 4831838208 | bytes 16515072 | tf_op jit(solution)/shard_map/pallas_call | solution.py:103
  159.7 21.1 %collective-permute-done.9 = bf16[512,1536]{1,0:T(8,128)(2,1)S(1)} collective-permute-done((bf16[512,1536]{1,0:T(8,128)(2,1)S(1)}, bf16[512,1536]{1,0:T(8,128)(2,1)S(1)}, u32[]{:S(2)}, u32[]{:S(2)}) %collective-permute-start.9) | collective-permute-done | bytes 1572896 | tf_op jit(solution)/shard_map/ppermute | solution.py:26
  180.9 2.8 %collective-permute-done.6.there_ref = bf16[2,512,128]{2,1,0:T(8,128)(2,1)S(1)} collective-permute-done((bf16[2,512,128]{2,1,0:T(8,128)(2,1)}, bf16[2,512,128]{2,1,0:T(8,128)(2,1)S(1)}, u32[]{:S(2)}, u32[]{:S(2)}) %collective-permute-start.6) | collective-permute-done | bytes 262176 | tf_op jit(solution)/shard_map/ppermute | solution.py:26
  184.4 16.0 %shard_map.112 = (f32[2,1024,256]{2,1,0:T(8,128)}, f32[2,1024,128]{2,1,0:T(8,128)}) custom-call(s32[4]{0:T(128)} %pad_add_fusion.spot, bf16[2,512,128]{2,1,0:T(8,128)(2,1)} %get-tuple-element.37.here_ref, bf16[2,512,128]{2,1,0:T(8,128)(2,1)} %copy-done.3, bf16[16,4,192,128]{3,2,1,0:T(8,128)(2,1)} %copy-done, bf16[4,512,128]{2,1,0:T(8,128)(2,1)} %get-tuple-element.47.refs_0_), custom_call_target="tpu_custom_call" | custom-call | flops 7516192768 | bytes 3670016 | tf_op jit(solution)/shard_map/pallas_call | solution.py:235
  200.4 15.8 %shard_map.113 = (f32[2,512,128]{2,1,0:T(8,128)}, f32[2,8,512]{2,1,0:T(8,128)}, bf16[2,512,128]{2,1,0:T(8,128)(2,1)}, f32[2,8,512]{2,1,0:T(8,128)}) custom-call(s32[4]{0:T(128)} %pad_add_fusion.spot, bf16[2,512,128]{2,1,0:T(8,128)(2,1)} %get-tuple-element.37.here_ref, bf16[2,512,128]{2,1,0:T(8,128)(2,1)} %copy-done.3, ...), custom_call_target="tpu_custom_call" | custom-call | flops 7516192768 | bytes 3670016 | tf_op jit(solution)/shard_map/pallas_call | solution.py:235
  216.2 3.1 %collective-permute-start.10 = (f32[2,8,512]{2,1,0:T(8,128)}, f32[2,8,512]{2,1,0:T(8,128)S(1)}, u32[]{:S(2)}, u32[]{:S(2)}) collective-permute-start(f32[2,8,512]{2,1,0:T(8,128)} %get-tuple-element.51), channel_id=1, source_target_pairs={{0,16},{1,17},{2,18},{3,19},{4,20},{5,21},{6,22},{7,23},{8,24},{9,... | collective-permute-start | bytes 98312 | tf_op jit(solution)/shard_map/ppermute | solution.py:26
  219.8 2.5 collective-permute-done.10
  223.0 4.4 %collective-permute-done.11 = bf16[2,512,128]{2,1,0:T(8,128)(2,1)S(1)} collective-permute-done((bf16[2,512,128]{2,1,0:T(8,128)(2,1)}, bf16[2,512,128]{2,1,0:T(8,128)(2,1)S(1)}, u32[]{:S(2)}, u32[]{:S(2)}) %collective-permute-start.11) | collective-permute-done | bytes 262176 | tf_op jit(solution)/shard_map/ppermute | solution.py:26
  227.4 1.4 add_convert_fusion.2
  228.9 1.5 collective-permute-start.12
  230.6 1.1 collective-permute-start.13
  231.7 2.3 collective-permute-start.14
  234.0 1.7 collective-permute-done.12
  235.7 3.1 %collective-permute-done.13 = bf16[512,256]{1,0:T(8,128)(2,1)S(1)} collective-permute-done((bf16[512,256]{1,0:T(8,128)(2,1)S(1)}, bf16[512,256]{1,0:T(8,128)(2,1)S(1)}, u32[]{:S(2)}, u32[]{:S(2)}) %collective-permute-start.13) | collective-permute-done | bytes 262176 | tf_op jit(solution)/shard_map/ppermute | solution.py:26
  238.9 2.2 collective-permute-done.14
  241.4 1.8 fusion.4
  243.3 1.5 collective-permute-start.15
  244.8 2.7 collective-permute-start.16
  247.5 1.5 collective-permute-start.17
  249.0 6.0 %collective-permute-done.15 = bf16[128,1536]{1,0:T(8,128)(2,1)S(1)} collective-permute-done((bf16[128,1536]{1,0:T(8,128)(2,1)S(1)}, bf16[128,1536]{1,0:T(8,128)(2,1)S(1)}, u32[]{:S(2)}, u32[]{:S(2)}) %collective-permute-start.15) | collective-permute-done | bytes 393248 | tf_op jit(solution)/shard_map/ppermute | solution.py:26
  254.9 4.3 %collective-permute-done.16 = bf16[128,1536]{1,0:T(8,128)(2,1)} collective-permute-done((bf16[128,1536]{1,0:T(8,128)(2,1)S(1)}, bf16[128,1536]{1,0:T(8,128)(2,1)}, u32[]{:S(2)}, u32[]{:S(2)}) %collective-permute-start.16) | collective-permute-done | bytes 393248 | tf_op jit(solution)/shard_map/ppermute | solution.py:26
  259.3 1.3 add_convert_fusion.1
  260.8 1.0 collective-permute-start.7
  262.0 1.9 collective-permute-start.19
  263.9 0.9 collective-permute-start.20
  264.8 2.4 collective-permute-start.21
  267.3 4.1 %collective-permute-done.20 = bf16[32,1536]{1,0:T(8,128)(2,1)S(1)} collective-permute-done((bf16[32,1536]{1,0:T(8,128)(2,1)S(1)}, bf16[32,1536]{1,0:T(8,128)(2,1)S(1)}, u32[]{:S(2)}, u32[]{:S(2)}) %collective-permute-start.20) | collective-permute-done | bytes 98336 | tf_op jit(solution)/shard_map/ppermute | solution.py:35
  271.4 1.1 collective-permute-done.21
  272.6 0.9 fusion.11
  (53 shorter events, 5.3 us)
Async XLA Ops:
  6.5 4.2 %copy-start.2 = (bf16[1,128,6144]{2,1,0:T(8,128)(2,1)S(1)}, bf16[1,128,6144]{2,1,0:T(8,128)(2,1)}, u32[]{:S(2)}) copy-start(bf16[1,128,6144]{2,1,0:T(8,128)(2,1)} %param.18) | copy-start | bytes 4718596
  6.5 123.6 %all-gather.2.cloned.1.call-start = ((), (), s32[]{:S(2)}) async-start(), calls=%async_computation.2 | async-start | bytes 6684672 | tf_op jit(solution)/shard_map/all_gather | solution.py:290
  17.2 112.9 %all-to-all-start.1 = ((bf16[16,4,192,128]{3,2,1,0:T(8,128)(2,1)}), bf16[16,4,192,128]{3,2,1,0:T(8,128)(2,1)S(1)}, u32[]{:S(2)}, u32[]{:S(2)}) async-start(bf16[16,4,192,128]{3,2,1,0:T(8,128)(2,1)} %shard_map.111), calls=%async_computation.1 | async-start | bytes 6291456 | tf_op jit(solution)/shard_map/all_to_all | solution.py:281
  24.7 83.6 %collective-permute-start = (bf16[6144,128]{1,0:T(8,128)(2,1)}, bf16[6144,128]{1,0:T(8,128)(2,1)}, u32[]{:S(2)}, u32[]{:S(2)}) collective-permute-start(bf16[6144,128]{1,0:T(8,128)(2,1)} %bitcast.47), channel_id=1, source_target_pairs={{0,16},{1,17},{2,18},{3,19},{4,20},{5,21},{6,22},{7,23},{8,24},{9,... | collective-permute-start | bytes 4718600 | tf_op jit(solution)/shard_map/ppermute | solution.py:26
  28.6 79.7 %collective-permute-start.1 = (bf16[6144,128]{1,0:T(8,128)(2,1)}, bf16[6144,128]{1,0:T(8,128)(2,1)}, u32[]{:S(2)}, u32[]{:S(2)}) collective-permute-start(bf16[6144,128]{1,0:T(8,128)(2,1)} %bitcast.49), channel_id=1, source_target_pairs={{0,16},{1,17},{2,18},{3,19},{4,20},{5,21},{6,22},{7,23},{8,24},{9,... | collective-permute-start | bytes 4718600 | tf_op jit(solution)/shard_map/ppermute | solution.py:26
  28.7 101.5 %collective-permute-start.2 = (bf16[6144,128]{1,0:T(8,128)(2,1)}, bf16[6144,128]{1,0:T(8,128)(2,1)}, u32[]{:S(2)}, u32[]{:S(2)}) collective-permute-start(bf16[6144,128]{1,0:T(8,128)(2,1)} %bitcast.51), channel_id=1, source_target_pairs={{0,16},{1,17},{2,18},{3,19},{4,20},{5,21},{6,22},{7,23},{8,24},{9,... | collective-permute-start | bytes 4718600 | tf_op jit(solution)/shard_map/ppermute | solution.py:26
  32.1 52.1 %collective-permute-start.3 = (bf16[128,1536]{1,0:T(8,128)(2,1)}, bf16[128,1536]{1,0:T(8,128)(2,1)}, u32[]{:S(2)}, u32[]{:S(2)}) collective-permute-start(bf16[128,1536]{1,0:T(8,128)(2,1)} %get-tuple-element.61), channel_id=1, source_target_pairs={{0,1},{1,2},{2,3},{3,0},{4,5},{5,6},{6,7},{7,4},{8,9},{9,10},{10,1... | collective-permute-start | bytes 1179656 | tf_op jit(solution)/shard_map/ppermute | solution.py:26
  33.6 56.8 %collective-permute-start.4 = (bf16[128,1536]{1,0:T(8,128)(2,1)}, bf16[128,1536]{1,0:T(8,128)(2,1)}, u32[]{:S(2)}, u32[]{:S(2)}) collective-permute-start(bf16[128,1536]{1,0:T(8,128)(2,1)} %get-tuple-element.63), channel_id=1, source_target_pairs={{0,2},{1,3},{2,0},{3,1},{4,6},{5,7},{6,4},{7,5},{8,10},{9,11},{10,... | collective-permute-start | bytes 1179656 | tf_op jit(solution)/shard_map/ppermute | solution.py:26
  84.2 24.1 %collective-permute-start.5 = (bf16[128,1536]{1,0:T(8,128)(2,1)}, bf16[128,1536]{1,0:T(8,128)(2,1)}, u32[]{:S(2)}, u32[]{:S(2)}) collective-permute-start(bf16[128,1536]{1,0:T(8,128)(2,1)} %get-tuple-element.60), channel_id=1, source_target_pairs={{0,3},{1,0},{2,1},{3,2},{4,7},{5,4},{6,5},{7,6},{8,11},{9,8},{10,9... | collective-permute-start | bytes 1179656 | tf_op jit(solution)/shard_map/ppermute | solution.py:26
  130.2 1.6 copy-start
  131.8 68.6 %all-to-all-start = ((bf16[16,4,224,128]{3,2,1,0:T(8,128)(2,1)}), bf16[16,4,224,128]{3,2,1,0:T(8,128)(2,1)}, u32[]{:S(2)}, u32[]{:S(2)}) async-start(bf16[16,4,224,128]{3,2,1,0:T(8,128)(2,1)} %shard_map.110), calls=%async_computation | async-start | bytes 7340032 | tf_op jit(solution)/shard_map/all_to_all | solution.py:281
  142.1 38.8 %collective-permute-start.9 = (bf16[512,1536]{1,0:T(8,128)(2,1)S(1)}, bf16[512,1536]{1,0:T(8,128)(2,1)S(1)}, u32[]{:S(2)}, u32[]{:S(2)}) collective-permute-start(bf16[512,1536]{1,0:T(8,128)(2,1)S(1)} %constant_dynamic-update-slice_fusion), channel_id=1, source_target_pairs={{0,16},{1,17},{2,18},{3,19},{4,20},{5,21},{6,22},{7,23},{8,24},{9,... | collective-permute-start | bytes 4718600 | tf_op jit(solution)/shard_map/ppermute | solution.py:26
  159.2 24.5 %collective-permute-start.6 = (bf16[2,512,128]{2,1,0:T(8,128)(2,1)}, bf16[2,512,128]{2,1,0:T(8,128)(2,1)S(1)}, u32[]{:S(2)}, u32[]{:S(2)}) collective-permute-start(bf16[2,512,128]{2,1,0:T(8,128)(2,1)} %get-tuple-element.37.here_ref), channel_id=1, source_target_pairs={{0,16},{1,17},{2,18},{3,19},{4,20},{5,21},{6,22},{7,23},{8,24},{9,... | collective-permute-start | bytes 786440 | tf_op jit(solution)/shard_map/ppermute | solution.py:26
  183.7 0.7 copy-start.3
  216.2 6.0 %collective-permute-start.10 = (f32[2,8,512]{2,1,0:T(8,128)}, f32[2,8,512]{2,1,0:T(8,128)S(1)}, u32[]{:S(2)}, u32[]{:S(2)}) collective-permute-start(f32[2,8,512]{2,1,0:T(8,128)} %get-tuple-element.51), channel_id=1, source_target_pairs={{0,16},{1,17},{2,18},{3,19},{4,20},{5,21},{6,22},{7,23},{8,24},{9,... | collective-permute-start | bytes 98312 | tf_op jit(solution)/shard_map/ppermute | solution.py:26
  219.3 8.1 %collective-permute-start.11 = (bf16[2,512,128]{2,1,0:T(8,128)(2,1)}, bf16[2,512,128]{2,1,0:T(8,128)(2,1)S(1)}, u32[]{:S(2)}, u32[]{:S(2)}) collective-permute-start(bf16[2,512,128]{2,1,0:T(8,128)(2,1)} %get-tuple-element.53), channel_id=1, source_target_pairs={{0,16},{1,17},{2,18},{3,19},{4,20},{5,21},{6,22},{7,23},{8,24},{9,... | collective-permute-start | bytes 786440 | tf_op jit(solution)/shard_map/ppermute | solution.py:26
  228.9 6.8 %collective-permute-start.12 = (bf16[512,256]{1,0:T(8,128)(2,1)S(1)}, bf16[512,256]{1,0:T(8,128)(2,1)S(1)}, u32[]{:S(2)}, u32[]{:S(2)}) collective-permute-start(bf16[512,256]{1,0:T(8,128)(2,1)S(1)} %pad_maximum_fusion), channel_id=1, source_target_pairs={{0,1},{1,2},{2,3},{3,0},{4,5},{5,6},{6,7},{7,4},{8,9},{9,10},{10,1... | collective-permute-start | bytes 786440 | tf_op jit(solution)/shard_map/ppermute | solution.py:26
  230.6 8.2 %collective-permute-start.13 = (bf16[512,256]{1,0:T(8,128)(2,1)S(1)}, bf16[512,256]{1,0:T(8,128)(2,1)S(1)}, u32[]{:S(2)}, u32[]{:S(2)}) collective-permute-start(bf16[512,256]{1,0:T(8,128)(2,1)S(1)} %pad_maximum_fusion), channel_id=1, source_target_pairs={{0,2},{1,3},{2,0},{3,1},{4,6},{5,7},{6,4},{7,5},{8,10},{9,11},{10,... | collective-permute-start | bytes 786440 | tf_op jit(solution)/shard_map/ppermute | solution.py:26
  231.7 9.4 %collective-permute-start.14 = (bf16[512,256]{1,0:T(8,128)(2,1)S(1)}, bf16[512,256]{1,0:T(8,128)(2,1)S(1)}, u32[]{:S(2)}, u32[]{:S(2)}) collective-permute-start(bf16[512,256]{1,0:T(8,128)(2,1)S(1)} %pad_maximum_fusion), channel_id=1, source_target_pairs={{0,3},{1,0},{2,1},{3,2},{4,7},{5,4},{6,5},{7,6},{8,11},{9,8},{10,9... | collective-permute-start | bytes 786440 | tf_op jit(solution)/shard_map/ppermute | solution.py:26
  243.3 17.6 %copy-start.1 = (bf16[1,32,6144]{2,1,0:T(8,128)(2,1)S(1)}, bf16[1,32,6144]{2,1,0:T(8,128)(2,1)}, u32[]{:S(2)}) copy-start(bf16[1,32,6144]{2,1,0:T(8,128)(2,1)} %param.11) | copy-start | bytes 1179652
  243.3 11.7 %collective-permute-start.15 = (bf16[128,1536]{1,0:T(8,128)(2,1)S(1)}, bf16[128,1536]{1,0:T(8,128)(2,1)S(1)}, u32[]{:S(2)}, u32[]{:S(2)}) collective-permute-start(bf16[128,1536]{1,0:T(8,128)(2,1)S(1)} %get-tuple-element.57), channel_id=1, source_target_pairs={{0,4},{1,5},{2,6},{3,7},{4,8},{5,9},{6,10},{7,11},{8,12},{9,13},{1... | collective-permute-start | bytes 1179656 | tf_op jit(solution)/shard_map/ppermute | solution.py:26
  244.8 14.4 %collective-permute-start.16 = (bf16[128,1536]{1,0:T(8,128)(2,1)S(1)}, bf16[128,1536]{1,0:T(8,128)(2,1)}, u32[]{:S(2)}, u32[]{:S(2)}) collective-permute-start(bf16[128,1536]{1,0:T(8,128)(2,1)S(1)} %get-tuple-element.59), channel_id=1, source_target_pairs={{0,8},{1,9},{2,10},{3,11},{4,12},{5,13},{6,14},{7,15},{8,0},{9,1},... | collective-permute-start | bytes 1179656 | tf_op jit(solution)/shard_map/ppermute | solution.py:26
  247.5 11.8 %collective-permute-start.17 = (bf16[128,1536]{1,0:T(8,128)(2,1)S(1)}, bf16[128,1536]{1,0:T(8,128)(2,1)}, u32[]{:S(2)}, u32[]{:S(2)}) collective-permute-start(bf16[128,1536]{1,0:T(8,128)(2,1)S(1)} %get-tuple-element.58), channel_id=1, source_target_pairs={{0,12},{1,13},{2,14},{3,15},{4,0},{5,1},{6,2},{7,3},{8,4},{9,5},{1... | collective-permute-start | bytes 1179656 | tf_op jit(solution)/shard_map/ppermute | solution.py:26
  254.9 6.9 %copy-start.4 = (f32[1,6144]{1,0:T(1,128)S(1)}, f32[1,6144]{1,0:T(1,128)}, u32[]{:S(2)}) copy-start(f32[1,6144]{1,0:T(1,128)} %param.14) | copy-start | bytes 73732
  260.7 4.1 %collective-permute-start.18 = (bf16[32,1536]{1,0:T(8,128)(2,1)S(1)}, bf16[32,1536]{1,0:T(8,128)(2,1)S(1)}, u32[]{:S(2)}, u32[]{:S(2)}) collective-permute-start(bf16[32,1536]{1,0:T(8,128)(2,1)S(1)} %get-tuple-element.67), channel_id=1, source_target_pairs={{0,32},{1,33},{2,34},{3,35},{4,36},{5,37},{6,38},{7,39},{8,40},{9,... | collective-permute-start | bytes 294920 | tf_op jit(solution)/shard_map/ppermute | solution.py:35
  260.8 11.7 %collective-permute-start.7 = (bf16[32,6144]{1,0:T(8,128)(2,1)S(1)}, bf16[32,6144]{1,0:T(8,128)(2,1)S(1)}, u32[]{:S(2)}, u32[]{:S(2)}) collective-permute-start(bf16[32,6144]{1,0:T(8,128)(2,1)S(1)} %bitcast.42), channel_id=1, source_target_pairs={{0,32},{32,64},{64,96},{96,0},{1,33},{33,65},{65,97},{97,1},{2,34}... | collective-permute-start | bytes 1179656 | tf_op jit(solution)/shard_map/ppermute | solution.py:41
  261.8 10.7 %collective-permute-start.8 = (f32[1,6144]{1,0:T(1,128)S(1)}, f32[1,6144]{1,0:T(1,128)S(1)}, u32[]{:S(2)}, u32[]{:S(2)}) collective-permute-start(f32[1,6144]{1,0:T(1,128)S(1)} %copy-done.4), channel_id=1, source_target_pairs={{0,32},{32,64},{64,96},{96,0},{1,33},{33,65},{65,97},{97,1},{2,34}... | collective-permute-start | bytes 73736 | tf_op jit(solution)/shard_map/ppermute | solution.py:41
  262.0 5.3 %collective-permute-start.19 = (bf16[32,1536]{1,0:T(8,128)(2,1)S(1)}, bf16[32,1536]{1,0:T(8,128)(2,1)S(1)}, u32[]{:S(2)}, u32[]{:S(2)}) collective-permute-start(bf16[32,1536]{1,0:T(8,128)(2,1)S(1)} %get-tuple-element.66), channel_id=1, source_target_pairs={{0,33},{1,34},{2,35},{3,32},{4,37},{5,38},{6,39},{7,36},{8,41},{9,... | collective-permute-start | bytes 294920 | tf_op jit(solution)/shard_map/ppermute | solution.py:35
  263.9 7.5 %collective-permute-start.20 = (bf16[32,1536]{1,0:T(8,128)(2,1)S(1)}, bf16[32,1536]{1,0:T(8,128)(2,1)S(1)}, u32[]{:S(2)}, u32[]{:S(2)}) collective-permute-start(bf16[32,1536]{1,0:T(8,128)(2,1)S(1)} %get-tuple-element.65), channel_id=1, source_target_pairs={{0,34},{1,35},{2,32},{3,33},{4,38},{5,39},{6,36},{7,37},{8,42},{9,... | collective-permute-start | bytes 294920 | tf_op jit(solution)/shard_map/ppermute | solution.py:35
  264.8 7.7 %collective-permute-start.21 = (bf16[32,1536]{1,0:T(8,128)(2,1)S(1)}, bf16[32,1536]{1,0:T(8,128)(2,1)S(1)}, u32[]{:S(2)}, u32[]{:S(2)}) collective-permute-start(bf16[32,1536]{1,0:T(8,128)(2,1)S(1)} %get-tuple-element.64), channel_id=1, source_target_pairs={{0,35},{1,32},{2,33},{3,34},{4,39},{5,36},{6,37},{7,38},{8,43},{9,... | collective-permute-start | bytes 294920 | tf_op jit(solution)/shard_map/ppermute | solution.py:35
Sparse Core Ops, SparseCore 0:
  10.7 104.7 all-gather.1

commit v3 on v2

--- a/solution.py
+++ b/solution.py
@@ -69,8 +69,9 @@
     )(turn, keys, values)
 
 
-def project_kernel(spot, x_hbm, *refs):
-    w_hbm, (q_ref, kv_ref, x_ref, w_ref, x_sem, w_sem) = refs[:6], refs[6:]
+def project_kernel(spot, x_hbm, *refs, scale):
+    kinds = (len(refs) - 5) // 2
+    w_hbm, (out_ref, x_ref, w_ref, x_sem, w_sem) = refs[: 2 * kinds], refs[2 * kinds :]
     tile = x_ref.shape[0] // 2
     x_copies, w_copies = [], []
     for t in range(2):
@@ -80,7 +81,7 @@
         w_copies.append(pltpu.make_async_copy(ref, w_ref.at[at // 2, :, pl.ds(at % 2 * HD, HD)], w_sem.at[at]))
     for copy in x_copies[:1] + w_copies[:2] + x_copies[1:] + w_copies[2:]:
         copy.start()
-    for kind in range(3):
+    for kind in range(kinds):
         for copy in w_copies[2 * kind : 2 * kind + 2]:
             copy.wait()
         for t in range(2):
@@ -89,31 +90,27 @@
             some = slice(t * tile, (t + 1) * tile)
             part = jnp.dot(x_ref[some, :], w_ref[kind], preferred_element_type=F32)
             for other in range(NZ):
-                head = lax.rem(spot[0] + other, NZ)
                 one = part[:, other * HD : (other + 1) * HD]
-                if kind == 0:
-                    q_ref[head, some, :] = (one * (LOG2E / HD**0.5)).astype(BF)
-                else:
-                    kv_ref[(kind - 1) * NZ + head, some, :] = one.astype(BF)
-
-
-def project(spot, normed, weights):
+                out_ref[kind * NZ + lax.rem(spot[0] + other, NZ), some, :] = (one * scale).astype(BF)
+
+
+def project(spot, normed, weights, scale):
+    kinds = len(weights) // 2
     patch, depth = normed.shape
-    vmem = pl.BlockSpec(memory_space=pltpu.VMEM)
     return pl.pallas_call(
-        project_kernel,
-        out_shape=(jax.ShapeDtypeStruct((NZ, patch, HD), BF), jax.ShapeDtypeStruct((2 * NZ, patch, HD), BF)),
-        in_specs=[pl.BlockSpec(memory_space=pltpu.SMEM)] + [pl.BlockSpec(memory_space=pl.ANY)] * 7,
-        out_specs=(vmem, vmem),
+        functools.partial(project_kernel, scale=scale),
+        out_shape=jax.ShapeDtypeStruct((kinds * NZ, patch, HD), BF),
+        in_specs=[pl.BlockSpec(memory_space=pltpu.SMEM)] + [pl.BlockSpec(memory_space=pl.ANY)] * (1 + 2 * kinds),
+        out_specs=pl.BlockSpec(memory_space=pltpu.VMEM),
         scratch_shapes=[
             pltpu.VMEM((patch, depth), BF),
-            pltpu.VMEM((3, depth, 2 * HD), BF),
+            pltpu.VMEM((kinds, depth, 2 * HD), BF),
             pltpu.SemaphoreType.DMA((2,)),
-            pltpu.SemaphoreType.DMA((6,)),
+            pltpu.SemaphoreType.DMA((2 * kinds,)),
         ],
         compiler_params=pltpu.CompilerParams(vmem_limit_bytes=58 * 2**20),
         cost_estimate=pl.CostEstimate(
-            flops=12 * patch * depth * HD, bytes_accessed=2 * depth * (patch + 6 * HD) + 12 * patch * HD, transcendentals=0
+            flops=4 * kinds * patch * depth * HD, bytes_accessed=2 * depth * (patch + 2 * kinds * HD) + 4 * patch * HD * kinds, transcendentals=0
         ),
     )(spot, normed, *weights)
 
@@ -301,16 +298,19 @@
     stale_first = stale_share(stale_laid(0, early, *w_slices))
     stale_second = stale_share(stale_laid(early, length - early), normed)
 
-    q, fresh = project(spot, normed, weights)
-    q = (q, moved(q, dz=1))
-    tokens_behind = from_behind(after(tokens[0], q[1]), "section", 1)
-    gate_behind = from_behind(after(mod_gate, q[1]), "section", 1)
-    w_other = moved(w_plane, dz=1)
-    spot, w_other = lax.optimization_barrier((spot, w_other))
-
-    state = attend(spot, q, stale_first, fresh, None, False, 0, length, patch, 4)
+    q = project(spot, normed, weights[:2], LOG2E / HD**0.5)
+    q_there = moved(q, dz=1)
+    spot, q = lax.optimization_barrier((spot, q))
+    fresh = project(spot, normed, weights[2:], 1.0)
+    w_other = moved(after(w_plane, q_there), dz=1)
+    tokens_behind = from_behind(after(tokens[0], q_there), "section", 1)
+    gate_behind = from_behind(after(mod_gate, q_there), "section", 1)
+
+    q = (q, q_there)
+    state = attend(spot, q, stale_first, None, None, False, 0, length, patch, 4)
+    fresh, w_other = lax.optimization_barrier((fresh, w_other))
     w_columns = jnp.concatenate((jnp.where(z == 0, w_plane, w_other), jnp.where(z == 0, w_other, w_plane)), axis=0)
-    o_here, lse_here, o_there, lse_there = attend(spot, q, stale_second, None, state, True, early, length, patch, 4)
+    o_here, lse_here, o_there, lse_there = attend(spot, q, stale_second, fresh, state, True, early, length, patch, 4)
 
     o_got = moved(o_there, dz=1).astype(F32)
     lse_got = moved(lse_there, dz=1)

time: 282 us -> 276 us (0.979)
  waiting for transfers between devices: 143 us -> 130 us
  Pallas kernels: 55.9 us -> 62.8 us
    ppermute x16, waiting for transfers between devices: 138 us -> 123 us  [moved(): return lax.ppermute(value, 'seq', pairs)]
    pallas_call x1 -> x2, Pallas kernels: 12.4 us -> 17.5 us  [project(): pl.pallas_call(functools.partial(project_kernel, scale=scale), out_shape=...]
    ppermute x16, starting transfers between devices: 27.6 us -> 30.7 us  [moved(): return lax.ppermute(value, 'seq', pairs)]
  transfers between devices with their start and end apart: 25 -> 25, of which waited for: 17 -> 16; matrix products, arithmetic and copies ran while one was open for 2% -> 2% of each run, Pallas kernels for 14% -> 16%
where the time goes in v3:
time: 276 us; the launch traced here: 275 us
  waiting for transfers between devices  130 us (47%)
  Pallas kernels  62.8 us (23%)
  starting transfers between devices  50.6 us (18%)
  between operations  14.5 us (5%)
  other arithmetic  9.2 us (3%)
  local copies, waits for them, and re-layouts  6.31 us (2%)
    ppermute x16, waiting for transfers between devices, moved(): return lax.ppermute(value, 'seq', pairs)  123 us
    pallas_call x2, Pallas kernels, attend(): pl.pallas_call(functools.partial(attend_kernel, fresh=fresh is not None,...  33.5 us
    ppermute x16, starting transfers between devices, moved(): return lax.ppermute(value, 'seq', pairs)  30.7 us
    pallas_call x2, Pallas kernels, project(): pl.pallas_call(functools.partial(project_kernel, scale=scale), out_shape=...  17.5 us
    all_to_all x2, starting transfers between devices, stale_share(): lax.all_to_all(laid, 'seq', split_axis=0, concat_axis=0, tiled=True, axis...  14.7 us
    pallas_call x2, Pallas kernels, lay_out(): pl.pallas_call(lay_out_kernel, grid=(length // rows,), out_shape=jax.Shap...  11.8 us
    ppermute x4, waiting for transfers between devices, onward(): return lax.ppermute(value, ('section', 'seq'), pairs)  6.75 us
  transfers between devices with their start and end apart: 25, of which 16 were waited for; matrix products, arithmetic and copies ran while one was open for 2% of the time, Pallas kernels for 16%

profile of v3, /device:TPU:2, one launch (start us, length us, event | category | flops | bytes accessed | tf_op | source)
XLA Modules:
  0.0 274.9 jit_solution(10453443928944930554)
XLA Ops:
  6.5 0.9 broadcast_add_fusion
  7.4 1.2 fusion.7
  8.6 2.0 fusion.10
  10.7 1.1 dynamic-slice_bitcast_fusion
  11.8 5.5 %shard_map.112 = bf16[16,4,192,128]{3,2,1,0:T(8,128)(2,1)} custom-call(s32[1]{0:T(128)} %bitcast.1.turn, bf16[416,4096]{1,0:T(8,128)(2,1)} %bitcast.38, bf16[416,4096]{1,0:T(8,128)(2,1)} %bitcast.40), custom_call_target="tpu_custom_call" | custom-call | bytes 6291456 | tf_op jit(solution)/shard_map/pallas_call | solution.py:61
  17.3 7.5 %all-to-all-start.1 = ((bf16[16,4,192,128]{3,2,1,0:T(8,128)(2,1)}), bf16[16,4,192,128]{3,2,1,0:T(8,128)(2,1)S(1)}, u32[]{:S(2)}, u32[]{:S(2)}) async-start(bf16[16,4,192,128]{3,2,1,0:T(8,128)(2,1)} %shard_map.112), calls=%async_computation.1 | async-start | bytes 6291456 | tf_op jit(solution)/shard_map/all_to_all | solution.py:278
  24.8 3.9 %collective-permute-start = (bf16[6144,128]{1,0:T(8,128)(2,1)}, bf16[6144,128]{1,0:T(8,128)(2,1)}, u32[]{:S(2)}, u32[]{:S(2)}) collective-permute-start(bf16[6144,128]{1,0:T(8,128)(2,1)} %bitcast.42), channel_id=1, source_target_pairs={{0,16},{1,17},{2,18},{3,19},{4,20},{5,21},{6,22},{7,23},{8,24},{9,... | collective-permute-start | bytes 4718600 | tf_op jit(solution)/shard_map/ppermute | solution.py:26
  28.7 3.4 %collective-permute-start.2 = (bf16[6144,128]{1,0:T(8,128)(2,1)}, bf16[6144,128]{1,0:T(8,128)(2,1)}, u32[]{:S(2)}, u32[]{:S(2)}) collective-permute-start(bf16[6144,128]{1,0:T(8,128)(2,1)} %bitcast.46), channel_id=1, source_target_pairs={{0,16},{1,17},{2,18},{3,19},{4,20},{5,21},{6,22},{7,23},{8,24},{9,... | collective-permute-start | bytes 4718600 | tf_op jit(solution)/shard_map/ppermute | solution.py:26
  32.2 1.5 collective-permute-start.3
  34.4 49.8 %collective-permute-done.3 = bf16[128,1536]{1,0:T(8,128)(2,1)} collective-permute-done((bf16[128,1536]{1,0:T(8,128)(2,1)}, bf16[128,1536]{1,0:T(8,128)(2,1)}, u32[]{:S(2)}, u32[]{:S(2)}) %collective-permute-start.3) | collective-permute-done | bytes 393248 | tf_op jit(solution)/shard_map/ppermute | solution.py:26
  84.2 6.3 %shard_map.110 = bf16[16,4,224,128]{3,2,1,0:T(8,128)(2,1)} custom-call(s32[1]{0:T(128)} %bitcast.1.turn, bf16[416,4096]{1,0:T(8,128)(2,1)} %bitcast.39, bf16[416,4096]{1,0:T(8,128)(2,1)} %bitcast.41), custom_call_target="tpu_custom_call" | custom-call | bytes 7340032 | tf_op jit(solution)/shard_map/pallas_call | solution.py:61
  90.5 17.8 %collective-permute-done.5 = bf16[128,1536]{1,0:T(8,128)(2,1)} collective-permute-done((bf16[128,1536]{1,0:T(8,128)(2,1)}, bf16[128,1536]{1,0:T(8,128)(2,1)}, u32[]{:S(2)}, u32[]{:S(2)}) %collective-permute-start.5) | collective-permute-done | bytes 393248 | tf_op jit(solution)/shard_map/ppermute | solution.py:26
  108.3 21.9 %collective-permute-done.2.refs_3_ = bf16[6144,128]{1,0:T(8,128)(2,1)} collective-permute-done((bf16[6144,128]{1,0:T(8,128)(2,1)}, bf16[6144,128]{1,0:T(8,128)(2,1)}, u32[]{:S(2)}, u32[]{:S(2)}) %collective-permute-start.2) | collective-permute-done | bytes 1572896 | tf_op jit(solution)/shard_map/ppermute | solution.py:26
  130.2 1.6 copy-done
  131.8 7.2 %all-to-all-start = ((bf16[16,4,224,128]{3,2,1,0:T(8,128)(2,1)}), bf16[16,4,224,128]{3,2,1,0:T(8,128)(2,1)}, u32[]{:S(2)}, u32[]{:S(2)}) async-start(bf16[16,4,224,128]{3,2,1,0:T(8,128)(2,1)} %shard_map.110), calls=%async_computation | async-start | bytes 7340032 | tf_op jit(solution)/shard_map/all_to_all | solution.py:278
  140.3 7.8 %shard_map.109.here_ref = bf16[2,512,128]{2,1,0:T(8,128)(2,1)} custom-call(s32[4]{0:T(128)} %pad_add_fusion.spot, bf16[512,6144]{1,0:T(8,128)(2,1)} %all-gather.2.cloned.1.call-done.x_hbm, bf16[6144,128]{1,0:T(8,128)(2,1)} %bitcast.43, bf16[6144,128]{1,0:T(8,128)(2,1)} %collective-permute-done.refs_1_), custom_call_target="tpu_custom_call" | custom-call | flops 1610612736 | bytes 9699328 | tf_op jit(solution)/shard_map/pallas_call | solution.py:100
  148.1 3.3 %collective-permute-start.6 = (bf16[2,512,128]{2,1,0:T(8,128)(2,1)}, bf16[2,512,128]{2,1,0:T(8,128)(2,1)S(1)}, u32[]{:S(2)}, u32[]{:S(2)}) collective-permute-start(bf16[2,512,128]{2,1,0:T(8,128)(2,1)} %shard_map.109.here_ref), channel_id=1, source_target_pairs={{0,16},{1,17},{2,18},{3,19},{4,20},{5,21},{6,22},{7,23},{8,24},{9,... | collective-permute-start | bytes 786440 | tf_op jit(solution)/shard_map/ppermute | solution.py:26
  151.4 1.0 constant_dynamic-update-slice_fusion.2
  152.5 1.0 constant_dynamic-update-slice_fusion.1
  153.5 1.0 constant_dynamic-update-slice_fusion
  154.5 1.7 collective-permute-done.6.there_ref
  156.3 3.2 %collective-permute-start.9 = (bf16[512,1536]{1,0:T(8,128)(2,1)S(1)}, bf16[512,1536]{1,0:T(8,128)(2,1)S(1)}, u32[]{:S(2)}, u32[]{:S(2)}) collective-permute-start(bf16[512,1536]{1,0:T(8,128)(2,1)S(1)} %constant_dynamic-update-slice_fusion), channel_id=1, source_target_pairs={{0,16},{1,17},{2,18},{3,19},{4,20},{5,21},{6,22},{7,23},{8,24},{9,... | collective-permute-start | bytes 4718600 | tf_op jit(solution)/shard_map/ppermute | solution.py:26
  159.5 9.7 %shard_map.111.refs_0_ = bf16[4,512,128]{2,1,0:T(8,128)(2,1)} custom-call(s32[4]{0:T(128)} %pad_add_fusion.spot, bf16[512,6144]{1,0:T(8,128)(2,1)} %all-gather.2.cloned.1.call-done.x_hbm, bf16[6144,128]{1,0:T(8,128)(2,1)} %bitcast.45, bf16[6144,128]{1,0:T(8,128)(2,1)} %collective-permute-done.1.refs_1_, bf16[6144,128]{1,0:T(8,128)(2,1)} %bitcast.47, ...), custom_call_target="tpu_custom_call" | custom-call | flops 3221225472 | bytes 13107200 | tf_op jit(solution)/shard_map/pallas_call | solution.py:100
  169.2 13.8 %shard_map.113 = (f32[2,1024,256]{2,1,0:T(8,128)}, f32[2,1024,128]{2,1,0:T(8,128)}) custom-call(s32[4]{0:T(128)} %pad_add_fusion.spot, bf16[2,512,128]{2,1,0:T(8,128)(2,1)} %shard_map.109.here_ref, bf16[2,512,128]{2,1,0:T(8,128)(2,1)} %copy-done.3, bf16[16,4,192,128]{3,2,1,0:T(8,128)(2,1)} %copy-done), custom_call_target="tpu_custom_call" | custom-call | flops 6442450944 | bytes 3145728 | tf_op jit(solution)/shard_map/pallas_call | solution.py:232
  183.0 8.4 %collective-permute-done.9 = bf16[512,1536]{1,0:T(8,128)(2,1)S(1)} collective-permute-done((bf16[512,1536]{1,0:T(8,128)(2,1)S(1)}, bf16[512,1536]{1,0:T(8,128)(2,1)S(1)}, u32[]{:S(2)}, u32[]{:S(2)}) %collective-permute-start.9) | collective-permute-done | bytes 1572896 | tf_op jit(solution)/shard_map/ppermute | solution.py:26
  191.4 19.7 %shard_map.114 = (f32[2,512,128]{2,1,0:T(8,128)}, f32[2,8,512]{2,1,0:T(8,128)}, bf16[2,512,128]{2,1,0:T(8,128)(2,1)}, f32[2,8,512]{2,1,0:T(8,128)}) custom-call(s32[4]{0:T(128)} %pad_add_fusion.spot, bf16[2,512,128]{2,1,0:T(8,128)(2,1)} %shard_map.109.here_ref, bf16[2,512,128]{2,1,0:T(8,128)(2,1)} %copy-done.3, ...), custom_call_target="tpu_custom_call" | custom-call | flops 8589934592 | bytes 4194304 | tf_op jit(solution)/shard_map/pallas_call | solution.py:232
  211.1 2.9 %collective-permute-start.10 = (f32[2,8,512]{2,1,0:T(8,128)}, f32[2,8,512]{2,1,0:T(8,128)S(1)}, u32[]{:S(2)}, u32[]{:S(2)}) collective-permute-start(f32[2,8,512]{2,1,0:T(8,128)} %get-tuple-element.53), channel_id=1, source_target_pairs={{0,16},{1,17},{2,18},{3,19},{4,20},{5,21},{6,22},{7,23},{8,24},{9,... | collective-permute-start | bytes 98312 | tf_op jit(solution)/shard_map/ppermute | solution.py:26
  214.6 2.5 collective-permute-done.10
  217.9 4.2 %collective-permute-done.11 = bf16[2,512,128]{2,1,0:T(8,128)(2,1)S(1)} collective-permute-done((bf16[2,512,128]{2,1,0:T(8,128)(2,1)}, bf16[2,512,128]{2,1,0:T(8,128)(2,1)S(1)}, u32[]{:S(2)}, u32[]{:S(2)}) %collective-permute-start.11) | collective-permute-done | bytes 262176 | tf_op jit(solution)/shard_map/ppermute | solution.py:26
  222.1 1.4 add_convert_fusion.2
  223.6 1.5 collective-permute-start.12
  225.3 1.1 collective-permute-start.13
  226.4 2.5 collective-permute-start.14
  229.0 1.0 collective-permute-done.12
  230.0 3.3 %collective-permute-done.13 = bf16[512,256]{1,0:T(8,128)(2,1)S(1)} collective-permute-done((bf16[512,256]{1,0:T(8,128)(2,1)S(1)}, bf16[512,256]{1,0:T(8,128)(2,1)S(1)}, u32[]{:S(2)}, u32[]{:S(2)}) %collective-permute-start.13) | collective-permute-done | bytes 262176 | tf_op jit(solution)/shard_map/ppermute | solution.py:26
  233.4 2.6 collective-permute-done.14
  236.2 1.8 fusion.4
  238.1 1.6 collective-permute-start.15
  239.8 2.7 collective-permute-start.16
  242.4 1.5 collective-permute-start.17
  243.9 5.5 %collective-permute-done.15 = bf16[128,1536]{1,0:T(8,128)(2,1)S(1)} collective-permute-done((bf16[128,1536]{1,0:T(8,128)(2,1)S(1)}, bf16[128,1536]{1,0:T(8,128)(2,1)S(1)}, u32[]{:S(2)}, u32[]{:S(2)}) %collective-permute-start.15) | collective-permute-done | bytes 393248 | tf_op jit(solution)/shard_map/ppermute | solution.py:26
  249.4 4.3 %collective-permute-done.16 = bf16[128,1536]{1,0:T(8,128)(2,1)} collective-permute-done((bf16[128,1536]{1,0:T(8,128)(2,1)S(1)}, bf16[128,1536]{1,0:T(8,128)(2,1)}, u32[]{:S(2)}, u32[]{:S(2)}) %collective-permute-start.16) | collective-permute-done | bytes 393248 | tf_op jit(solution)/shard_map/ppermute | solution.py:26
  253.7 1.3 add_convert_fusion.1
  255.3 1.0 collective-permute-start.7
  256.4 1.4 collective-permute-start.19
  259.2 1.7 collective-permute-start.21
  261.8 3.6 %collective-permute-done.20 = bf16[32,1536]{1,0:T(8,128)(2,1)S(1)} collective-permute-done((bf16[32,1536]{1,0:T(8,128)(2,1)S(1)}, bf16[32,1536]{1,0:T(8,128)(2,1)S(1)}, u32[]{:S(2)}, u32[]{:S(2)}) %collective-permute-start.20) | collective-permute-done | bytes 98336 | tf_op jit(solution)/shard_map/ppermute | solution.py:35
  265.4 1.8 collective-permute-done.21
  (54 shorter events, 6.9 us)
Async XLA Ops:
  6.5 4.2 %copy-start.2 = (bf16[1,128,6144]{2,1,0:T(8,128)(2,1)S(1)}, bf16[1,128,6144]{2,1,0:T(8,128)(2,1)}, u32[]{:S(2)}) copy-start(bf16[1,128,6144]{2,1,0:T(8,128)(2,1)} %param.18) | copy-start | bytes 4718596
  6.5 123.7 %all-gather.2.cloned.1.call-start = ((), (), s32[]{:S(2)}) async-start(), calls=%async_computation.2 | async-start | bytes 6684672 | tf_op jit(solution)/shard_map/all_gather | solution.py:287
  17.3 112.9 %all-to-all-start.1 = ((bf16[16,4,192,128]{3,2,1,0:T(8,128)(2,1)}), bf16[16,4,192,128]{3,2,1,0:T(8,128)(2,1)S(1)}, u32[]{:S(2)}, u32[]{:S(2)}) async-start(bf16[16,4,192,128]{3,2,1,0:T(8,128)(2,1)} %shard_map.112), calls=%async_computation.1 | async-start | bytes 6291456 | tf_op jit(solution)/shard_map/all_to_all | solution.py:278
  24.8 83.5 %collective-permute-start = (bf16[6144,128]{1,0:T(8,128)(2,1)}, bf16[6144,128]{1,0:T(8,128)(2,1)}, u32[]{:S(2)}, u32[]{:S(2)}) collective-permute-start(bf16[6144,128]{1,0:T(8,128)(2,1)} %bitcast.42), channel_id=1, source_target_pairs={{0,16},{1,17},{2,18},{3,19},{4,20},{5,21},{6,22},{7,23},{8,24},{9,... | collective-permute-start | bytes 4718600 | tf_op jit(solution)/shard_map/ppermute | solution.py:26
  28.6 79.7 %collective-permute-start.1 = (bf16[6144,128]{1,0:T(8,128)(2,1)}, bf16[6144,128]{1,0:T(8,128)(2,1)}, u32[]{:S(2)}, u32[]{:S(2)}) collective-permute-start(bf16[6144,128]{1,0:T(8,128)(2,1)} %bitcast.44), channel_id=1, source_target_pairs={{0,16},{1,17},{2,18},{3,19},{4,20},{5,21},{6,22},{7,23},{8,24},{9,... | collective-permute-start | bytes 4718600 | tf_op jit(solution)/shard_map/ppermute | solution.py:26
  28.7 101.5 %collective-permute-start.2 = (bf16[6144,128]{1,0:T(8,128)(2,1)}, bf16[6144,128]{1,0:T(8,128)(2,1)}, u32[]{:S(2)}, u32[]{:S(2)}) collective-permute-start(bf16[6144,128]{1,0:T(8,128)(2,1)} %bitcast.46), channel_id=1, source_target_pairs={{0,16},{1,17},{2,18},{3,19},{4,20},{5,21},{6,22},{7,23},{8,24},{9,... | collective-permute-start | bytes 4718600 | tf_op jit(solution)/shard_map/ppermute | solution.py:26
  32.2 52.0 %collective-permute-start.3 = (bf16[128,1536]{1,0:T(8,128)(2,1)}, bf16[128,1536]{1,0:T(8,128)(2,1)}, u32[]{:S(2)}, u32[]{:S(2)}) collective-permute-start(bf16[128,1536]{1,0:T(8,128)(2,1)} %get-tuple-element.63), channel_id=1, source_target_pairs={{0,1},{1,2},{2,3},{3,0},{4,5},{5,6},{6,7},{7,4},{8,9},{9,10},{10,1... | collective-permute-start | bytes 1179656 | tf_op jit(solution)/shard_map/ppermute | solution.py:26
  33.6 56.8 %collective-permute-start.4 = (bf16[128,1536]{1,0:T(8,128)(2,1)}, bf16[128,1536]{1,0:T(8,128)(2,1)}, u32[]{:S(2)}, u32[]{:S(2)}) collective-permute-start(bf16[128,1536]{1,0:T(8,128)(2,1)} %get-tuple-element.65), channel_id=1, source_target_pairs={{0,2},{1,3},{2,0},{3,1},{4,6},{5,7},{6,4},{7,5},{8,10},{9,11},{10,... | collective-permute-start | bytes 1179656 | tf_op jit(solution)/shard_map/ppermute | solution.py:26
  84.2 24.1 %collective-permute-start.5 = (bf16[128,1536]{1,0:T(8,128)(2,1)}, bf16[128,1536]{1,0:T(8,128)(2,1)}, u32[]{:S(2)}, u32[]{:S(2)}) collective-permute-start(bf16[128,1536]{1,0:T(8,128)(2,1)} %get-tuple-element.62), channel_id=1, source_target_pairs={{0,3},{1,0},{2,1},{3,2},{4,7},{5,4},{6,5},{7,6},{8,11},{9,8},{10,9... | collective-permute-start | bytes 1179656 | tf_op jit(solution)/shard_map/ppermute | solution.py:26
  130.2 1.6 copy-start
  131.8 59.6 %all-to-all-start = ((bf16[16,4,224,128]{3,2,1,0:T(8,128)(2,1)}), bf16[16,4,224,128]{3,2,1,0:T(8,128)(2,1)}, u32[]{:S(2)}, u32[]{:S(2)}) async-start(bf16[16,4,224,128]{3,2,1,0:T(8,128)(2,1)} %shard_map.110), calls=%async_computation | async-start | bytes 7340032 | tf_op jit(solution)/shard_map/all_to_all | solution.py:278
  148.1 8.2 %collective-permute-start.6 = (bf16[2,512,128]{2,1,0:T(8,128)(2,1)}, bf16[2,512,128]{2,1,0:T(8,128)(2,1)S(1)}, u32[]{:S(2)}, u32[]{:S(2)}) collective-permute-start(bf16[2,512,128]{2,1,0:T(8,128)(2,1)} %shard_map.109.here_ref), channel_id=1, source_target_pairs={{0,16},{1,17},{2,18},{3,19},{4,20},{5,21},{6,22},{7,23},{8,24},{9,... | collective-permute-start | bytes 786440 | tf_op jit(solution)/shard_map/ppermute | solution.py:26
  156.3 12.9 %copy-start.3 = (bf16[2,512,128]{2,1,0:T(8,128)(2,1)}, bf16[2,512,128]{2,1,0:T(8,128)(2,1)S(1)}, u32[]{:S(2)}) copy-start(bf16[2,512,128]{2,1,0:T(8,128)(2,1)S(1)} %collective-permute-done.6.there_ref) | copy-start | bytes 786436
  156.3 35.1 %collective-permute-start.9 = (bf16[512,1536]{1,0:T(8,128)(2,1)S(1)}, bf16[512,1536]{1,0:T(8,128)(2,1)S(1)}, u32[]{:S(2)}, u32[]{:S(2)}) collective-permute-start(bf16[512,1536]{1,0:T(8,128)(2,1)S(1)} %constant_dynamic-update-slice_fusion), channel_id=1, source_target_pairs={{0,16},{1,17},{2,18},{3,19},{4,20},{5,21},{6,22},{7,23},{8,24},{9,... | collective-permute-start | bytes 4718600 | tf_op jit(solution)/shard_map/ppermute | solution.py:26
  211.1 6.0 %collective-permute-start.10 = (f32[2,8,512]{2,1,0:T(8,128)}, f32[2,8,512]{2,1,0:T(8,128)S(1)}, u32[]{:S(2)}, u32[]{:S(2)}) collective-permute-start(f32[2,8,512]{2,1,0:T(8,128)} %get-tuple-element.53), channel_id=1, source_target_pairs={{0,16},{1,17},{2,18},{3,19},{4,20},{5,21},{6,22},{7,23},{8,24},{9,... | collective-permute-start | bytes 98312 | tf_op jit(solution)/shard_map/ppermute | solution.py:26
  214.0 8.1 %collective-permute-start.11 = (bf16[2,512,128]{2,1,0:T(8,128)(2,1)}, bf16[2,512,128]{2,1,0:T(8,128)(2,1)S(1)}, u32[]{:S(2)}, u32[]{:S(2)}) collective-permute-start(bf16[2,512,128]{2,1,0:T(8,128)(2,1)} %get-tuple-element.55), channel_id=1, source_target_pairs={{0,16},{1,17},{2,18},{3,19},{4,20},{5,21},{6,22},{7,23},{8,24},{9,... | collective-permute-start | bytes 786440 | tf_op jit(solution)/shard_map/ppermute | solution.py:26
  223.6 6.4 %collective-permute-start.12 = (bf16[512,256]{1,0:T(8,128)(2,1)S(1)}, bf16[512,256]{1,0:T(8,128)(2,1)S(1)}, u32[]{:S(2)}, u32[]{:S(2)}) collective-permute-start(bf16[512,256]{1,0:T(8,128)(2,1)S(1)} %pad_maximum_fusion), channel_id=1, source_target_pairs={{0,1},{1,2},{2,3},{3,0},{4,5},{5,6},{6,7},{7,4},{8,9},{9,10},{10,1... | collective-permute-start | bytes 786440 | tf_op jit(solution)/shard_map/ppermute | solution.py:26
  225.3 8.1 %collective-permute-start.13 = (bf16[512,256]{1,0:T(8,128)(2,1)S(1)}, bf16[512,256]{1,0:T(8,128)(2,1)S(1)}, u32[]{:S(2)}, u32[]{:S(2)}) collective-permute-start(bf16[512,256]{1,0:T(8,128)(2,1)S(1)} %pad_maximum_fusion), channel_id=1, source_target_pairs={{0,2},{1,3},{2,0},{3,1},{4,6},{5,7},{6,4},{7,5},{8,10},{9,11},{10,... | collective-permute-start | bytes 786440 | tf_op jit(solution)/shard_map/ppermute | solution.py:26
  226.4 9.5 %collective-permute-start.14 = (bf16[512,256]{1,0:T(8,128)(2,1)S(1)}, bf16[512,256]{1,0:T(8,128)(2,1)S(1)}, u32[]{:S(2)}, u32[]{:S(2)}) collective-permute-start(bf16[512,256]{1,0:T(8,128)(2,1)S(1)} %pad_maximum_fusion), channel_id=1, source_target_pairs={{0,3},{1,0},{2,1},{3,2},{4,7},{5,4},{6,5},{7,6},{8,11},{9,8},{10,9... | collective-permute-start | bytes 786440 | tf_op jit(solution)/shard_map/ppermute | solution.py:26
  238.1 17.1 %copy-start.1 = (bf16[1,32,6144]{2,1,0:T(8,128)(2,1)S(1)}, bf16[1,32,6144]{2,1,0:T(8,128)(2,1)}, u32[]{:S(2)}) copy-start(bf16[1,32,6144]{2,1,0:T(8,128)(2,1)} %param.11) | copy-start | bytes 1179652
  238.1 11.3 %collective-permute-start.15 = (bf16[128,1536]{1,0:T(8,128)(2,1)S(1)}, bf16[128,1536]{1,0:T(8,128)(2,1)S(1)}, u32[]{:S(2)}, u32[]{:S(2)}) collective-permute-start(bf16[128,1536]{1,0:T(8,128)(2,1)S(1)} %get-tuple-element.59), channel_id=1, source_target_pairs={{0,4},{1,5},{2,6},{3,7},{4,8},{5,9},{6,10},{7,11},{8,12},{9,13},{1... | collective-permute-start | bytes 1179656 | tf_op jit(solution)/shard_map/ppermute | solution.py:26
  239.8 14.0 %collective-permute-start.16 = (bf16[128,1536]{1,0:T(8,128)(2,1)S(1)}, bf16[128,1536]{1,0:T(8,128)(2,1)}, u32[]{:S(2)}, u32[]{:S(2)}) collective-permute-start(bf16[128,1536]{1,0:T(8,128)(2,1)S(1)} %get-tuple-element.61), channel_id=1, source_target_pairs={{0,8},{1,9},{2,10},{3,11},{4,12},{5,13},{6,14},{7,15},{8,0},{9,1},... | collective-permute-start | bytes 1179656 | tf_op jit(solution)/shard_map/ppermute | solution.py:26
  242.4 11.3 %collective-permute-start.17 = (bf16[128,1536]{1,0:T(8,128)(2,1)S(1)}, bf16[128,1536]{1,0:T(8,128)(2,1)}, u32[]{:S(2)}, u32[]{:S(2)}) collective-permute-start(bf16[128,1536]{1,0:T(8,128)(2,1)S(1)} %get-tuple-element.60), channel_id=1, source_target_pairs={{0,12},{1,13},{2,14},{3,15},{4,0},{5,1},{6,2},{7,3},{8,4},{9,5},{1... | collective-permute-start | bytes 1179656 | tf_op jit(solution)/shard_map/ppermute | solution.py:26
  249.4 6.9 %copy-start.4 = (f32[1,6144]{1,0:T(1,128)S(1)}, f32[1,6144]{1,0:T(1,128)}, u32[]{:S(2)}) copy-start(f32[1,6144]{1,0:T(1,128)} %param.14) | copy-start | bytes 73732
  255.1 4.1 %collective-permute-start.18 = (bf16[32,1536]{1,0:T(8,128)(2,1)S(1)}, bf16[32,1536]{1,0:T(8,128)(2,1)S(1)}, u32[]{:S(2)}, u32[]{:S(2)}) collective-permute-start(bf16[32,1536]{1,0:T(8,128)(2,1)S(1)} %get-tuple-element.69), channel_id=1, source_target_pairs={{0,32},{1,33},{2,34},{3,35},{4,36},{5,37},{6,38},{7,39},{8,40},{9,... | collective-permute-start | bytes 294920 | tf_op jit(solution)/shard_map/ppermute | solution.py:35
  255.3 11.9 %collective-permute-start.7 = (bf16[32,6144]{1,0:T(8,128)(2,1)S(1)}, bf16[32,6144]{1,0:T(8,128)(2,1)S(1)}, u32[]{:S(2)}, u32[]{:S(2)}) collective-permute-start(bf16[32,6144]{1,0:T(8,128)(2,1)S(1)} %bitcast.48), channel_id=1, source_target_pairs={{0,32},{32,64},{64,96},{96,0},{1,33},{33,65},{65,97},{97,1},{2,34}... | collective-permute-start | bytes 1179656 | tf_op jit(solution)/shard_map/ppermute | solution.py:41
  256.3 10.9 %collective-permute-start.8 = (f32[1,6144]{1,0:T(1,128)S(1)}, f32[1,6144]{1,0:T(1,128)S(1)}, u32[]{:S(2)}, u32[]{:S(2)}) collective-permute-start(f32[1,6144]{1,0:T(1,128)S(1)} %copy-done.4), channel_id=1, source_target_pairs={{0,32},{32,64},{64,96},{96,0},{1,33},{33,65},{65,97},{97,1},{2,34}... | collective-permute-start | bytes 73736 | tf_op jit(solution)/shard_map/ppermute | solution.py:41
  256.4 5.3 %collective-permute-start.19 = (bf16[32,1536]{1,0:T(8,128)(2,1)S(1)}, bf16[32,1536]{1,0:T(8,128)(2,1)S(1)}, u32[]{:S(2)}, u32[]{:S(2)}) collective-permute-start(bf16[32,1536]{1,0:T(8,128)(2,1)S(1)} %get-tuple-element.68), channel_id=1, source_target_pairs={{0,33},{1,34},{2,35},{3,32},{4,37},{5,38},{6,39},{7,36},{8,41},{9,... | collective-permute-start | bytes 294920 | tf_op jit(solution)/shard_map/ppermute | solution.py:35
  257.9 7.5 %collective-permute-start.20 = (bf16[32,1536]{1,0:T(8,128)(2,1)S(1)}, bf16[32,1536]{1,0:T(8,128)(2,1)S(1)}, u32[]{:S(2)}, u32[]{:S(2)}) collective-permute-start(bf16[32,1536]{1,0:T(8,128)(2,1)S(1)} %get-tuple-element.67), channel_id=1, source_target_pairs={{0,34},{1,35},{2,32},{3,33},{4,38},{5,39},{6,36},{7,37},{8,42},{9,... | collective-permute-start | bytes 294920 | tf_op jit(solution)/shard_map/ppermute | solution.py:35
  259.2 8.0 %collective-permute-start.21 = (bf16[32,1536]{1,0:T(8,128)(2,1)S(1)}, bf16[32,1536]{1,0:T(8,128)(2,1)S(1)}, u32[]{:S(2)}, u32[]{:S(2)}) collective-permute-start(bf16[32,1536]{1,0:T(8,128)(2,1)S(1)} %get-tuple-element.66), channel_id=1, source_target_pairs={{0,35},{1,32},{2,33},{3,34},{4,39},{5,36},{6,37},{7,38},{8,43},{9,... | collective-permute-start | bytes 294920 | tf_op jit(solution)/shard_map/ppermute | solution.py:35
Sparse Core Ops, SparseCore 0:
  10.7 104.7 all-gather.1

commit v4 on v3

--- a/solution.py
+++ b/solution.py
@@ -291,15 +291,15 @@
     for k in range(NX):
         w_slices.append(lax.dynamic_slice(w_out[0], (0, (x + k) % NX * wide), (HD, wide)))
         w_parts.append(moved(w_slices[k], dx=k) if k else w_slices[k])
+    q = project(spot, normed, weights[:2], LOG2E / HD**0.5)
+    q_there = moved(q, dz=1)
     normed, weights, w_parts = lax.optimization_barrier((normed, weights, w_parts))
     w_plane = jnp.concatenate(w_parts, axis=0)
 
-    early = 6 * rows
+    early = 8 * rows
     stale_first = stale_share(stale_laid(0, early, *w_slices))
     stale_second = stale_share(stale_laid(early, length - early), normed)
 
-    q = project(spot, normed, weights[:2], LOG2E / HD**0.5)
-    q_there = moved(q, dz=1)
     spot, q = lax.optimization_barrier((spot, q))
     fresh = project(spot, normed, weights[2:], 1.0)
     w_other = moved(after(w_plane, q_there), dz=1)

time: 276 us -> 279 us (1.011)
    ppermute x16, waiting for transfers between devices: 123 us -> 67.4 us  [moved(): return lax.ppermute(value, 'seq', pairs)]
    all_gather x1, waiting for transfers between devices: 0.01 us -> 55.1 us  [body(): lax.all_gather(normed, 'seq', axis=0, tiled=True, axis_index_groups=planes)]
  transfers between devices with their start and end apart: 25 -> 25, of which waited for: 16 -> 12; matrix products, arithmetic and copies ran while one was open for 2% -> 2% of each run, Pallas kernels for 16% -> 16%
where the time goes in v4:
time: 279 us; the launch traced here: 276 us
  waiting for transfers between devices  129 us (46%)
  Pallas kernels  62.5 us (22%)
  starting transfers between devices  52 us (19%)
  between operations  14.6 us (5%)
  other arithmetic  10.7 us (4%)
  local copies, waits for them, and re-layouts  6.39 us (2%)
    ppermute x16, waiting for transfers between devices, moved(): return lax.ppermute(value, 'seq', pairs)  67.4 us
    all_gather x1, waiting for transfers between devices, body(): lax.all_gather(normed, 'seq', axis=0, tiled=True, axis_index_groups=planes)  55.1 us
    pallas_call x2, Pallas kernels, attend(): pl.pallas_call(functools.partial(attend_kernel, fresh=fresh is not None,...  33.4 us
    ppermute x16, starting transfers between devices, moved(): return lax.ppermute(value, 'seq', pairs)  29.3 us
    pallas_call x2, Pallas kernels, project(): pl.pallas_call(functools.partial(project_kernel, scale=scale), out_shape=...  17.5 us
    all_to_all x2, starting transfers between devices, stale_share(): lax.all_to_all(laid, 'seq', split_axis=0, concat_axis=0, tiled=True, axis...  16.9 us
    pallas_call x2, Pallas kernels, lay_out(): pl.pallas_call(lay_out_kernel, grid=(length // rows,), out_shape=jax.Shap...  11.7 us
    ppermute x4, waiting for transfers between devices, onward(): return lax.ppermute(value, ('section', 'seq'), pairs)  5.99 us
  transfers between devices with their start and end apart: 25, of which 12 were waited for; matrix products, arithmetic and copies ran while one was open for 2% of the time, Pallas kernels for 16%

profile of v4, /device:TPU:2, one launch (start us, length us, event | category | flops | bytes accessed | tf_op | source)
XLA Modules:
  0.0 276.5 jit_solution(4804246785181002406)
XLA Ops:
  6.5 1.3 fusion.7
  7.8 0.8 broadcast_add_fusion
  8.6 1.9 fusion.10
  10.7 1.1 dynamic-slice_bitcast_fusion
  11.8 6.8 %shard_map.112 = bf16[16,4,256,128]{3,2,1,0:T(8,128)(2,1)} custom-call(s32[1]{0:T(128)} %bitcast.1.turn, bf16[416,4096]{1,0:T(8,128)(2,1)} %bitcast.38, bf16[416,4096]{1,0:T(8,128)(2,1)} %bitcast.40), custom_call_target="tpu_custom_call" | custom-call | bytes 8388608 | tf_op jit(solution)/shard_map/pallas_call | solution.py:61
  18.6 7.7 %all-to-all-start.1 = ((bf16[16,4,256,128]{3,2,1,0:T(8,128)(2,1)}), bf16[16,4,256,128]{3,2,1,0:T(8,128)(2,1)}, u32[]{:S(2)}, u32[]{:S(2)}) async-start(bf16[16,4,256,128]{3,2,1,0:T(8,128)(2,1)} %shard_map.112), calls=%async_computation.1 | async-start | bytes 8388608 | tf_op jit(solution)/shard_map/all_to_all | solution.py:278
  26.4 4.0 %collective-permute-start = (bf16[6144,128]{1,0:T(8,128)(2,1)S(1)}, bf16[6144,128]{1,0:T(8,128)(2,1)S(1)}, u32[]{:S(2)}, u32[]{:S(2)}) collective-permute-start(bf16[6144,128]{1,0:T(8,128)(2,1)S(1)} %bitcast.43), channel_id=1, source_target_pairs={{0,16},{1,17},{2,18},{3,19},{4,20},{5,21},{6,22},{7,23},{8,24},{9,... | collective-permute-start | bytes 4718600 | tf_op jit(solution)/shard_map/ppermute | solution.py:26
  30.4 3.4 %collective-permute-start.5 = (bf16[6144,128]{1,0:T(8,128)(2,1)}, bf16[6144,128]{1,0:T(8,128)(2,1)}, u32[]{:S(2)}, u32[]{:S(2)}) collective-permute-start(bf16[6144,128]{1,0:T(8,128)(2,1)} %bitcast.46), channel_id=1, source_target_pairs={{0,16},{1,17},{2,18},{3,19},{4,20},{5,21},{6,22},{7,23},{8,24},{9,... | collective-permute-start | bytes 4718600 | tf_op jit(solution)/shard_map/ppermute | solution.py:26
  34.0 1.9 collective-permute-start.6
  35.9 29.7 %collective-permute-done.refs_1_ = bf16[6144,128]{1,0:T(8,128)(2,1)S(1)} collective-permute-done((bf16[6144,128]{1,0:T(8,128)(2,1)S(1)}, bf16[6144,128]{1,0:T(8,128)(2,1)S(1)}, u32[]{:S(2)}, u32[]{:S(2)}) %collective-permute-start) | collective-permute-done | bytes 1572896 | tf_op jit(solution)/shard_map/ppermute | solution.py:26
  65.6 1.2 copy-done.5
  66.8 2.1 collective-permute-start.7
  68.9 4.9 %shard_map.110 = bf16[16,4,160,128]{3,2,1,0:T(8,128)(2,1)} custom-call(s32[1]{0:T(128)} %bitcast.1.turn, bf16[416,4096]{1,0:T(8,128)(2,1)} %bitcast.39, bf16[416,4096]{1,0:T(8,128)(2,1)} %bitcast.41), custom_call_target="tpu_custom_call" | custom-call | bytes 5242880 | tf_op jit(solution)/shard_map/pallas_call | solution.py:61
  74.4 0.7 pad_add_fusion.spot
  75.0 55.1 %all-gather.2.cloned.1.call-done.x_hbm = bf16[512,6144]{1,0:T(8,128)(2,1)} async-done(((bf16[32,6144]{1,0:T(8,128)(2,1)}), bf16[512,6144]{1,0:T(8,128)(2,1)}) %all-gather.2.cloned.1.call-update) | async-done | bytes 6291472 | tf_op jit(solution)/shard_map/all_gather | solution.py:287
  130.2 7.8 %shard_map.109.here_ref = bf16[2,512,128]{2,1,0:T(8,128)(2,1)} custom-call(s32[4]{0:T(128)} %pad_add_fusion.spot, bf16[512,6144]{1,0:T(8,128)(2,1)} %all-gather.2.cloned.1.call-done.x_hbm, bf16[6144,128]{1,0:T(8,128)(2,1)} %bitcast.42, bf16[6144,128]{1,0:T(8,128)(2,1)} %copy-done.5), custom_call_target="tpu_custom_call" | custom-call | flops 1610612736 | bytes 9699328 | tf_op jit(solution)/shard_map/pallas_call | solution.py:100
  137.9 4.7 %collective-permute-start.1 = (bf16[2,512,128]{2,1,0:T(8,128)(2,1)}, bf16[2,512,128]{2,1,0:T(8,128)(2,1)}, u32[]{:S(2)}, u32[]{:S(2)}) collective-permute-start(bf16[2,512,128]{2,1,0:T(8,128)(2,1)} %shard_map.109.here_ref), channel_id=1, source_target_pairs={{0,16},{1,17},{2,18},{3,19},{4,20},{5,21},{6,22},{7,23},{8,24},{9,... | collective-permute-start | bytes 786440 | tf_op jit(solution)/shard_map/ppermute | solution.py:26
  142.7 9.1 %all-to-all-start = ((bf16[16,4,160,128]{3,2,1,0:T(8,128)(2,1)}), bf16[16,4,160,128]{3,2,1,0:T(8,128)(2,1)S(1)}, u32[]{:S(2)}, u32[]{:S(2)}) async-start(bf16[16,4,160,128]{3,2,1,0:T(8,128)(2,1)} %shard_map.110), calls=%async_computation | async-start | bytes 5242880 | tf_op jit(solution)/shard_map/all_to_all | solution.py:278
  151.8 1.0 constant_dynamic-update-slice_fusion.2
  152.9 1.0 constant_dynamic-update-slice_fusion
  154.2 9.7 %shard_map.111.refs_0_ = bf16[4,512,128]{2,1,0:T(8,128)(2,1)} custom-call(s32[4]{0:T(128)} %pad_add_fusion.spot, bf16[512,6144]{1,0:T(8,128)(2,1)} %all-gather.2.cloned.1.call-done.x_hbm, bf16[6144,128]{1,0:T(8,128)(2,1)} %bitcast.44, bf16[6144,128]{1,0:T(8,128)(2,1)} %collective-permute-done.4.refs_1_, bf16[6144,128]{1,0:T(8,128)(2,1)} %bitcast.47, ...), custom_call_target="tpu_custom_call" | custom-call | flops 3221225472 | bytes 13107200 | tf_op jit(solution)/shard_map/pallas_call | solution.py:100
  163.9 15.6 %shard_map.113 = (f32[2,1024,256]{2,1,0:T(8,128)}, f32[2,1024,128]{2,1,0:T(8,128)}) custom-call(s32[4]{0:T(128)} %pad_add_fusion.spot, bf16[2,512,128]{2,1,0:T(8,128)(2,1)} %shard_map.109.here_ref, bf16[2,512,128]{2,1,0:T(8,128)(2,1)} %collective-permute-done.1.there_ref, bf16[16,4,256,128]{3,2,1,0:T(8,128)(2,1)} %all-to-all-done.1.kv_ref), custom_call_target="tpu_custom_call" | custom-call | flops 8589934592 | bytes 4194304 | tf_op jit(solution)/shard_map/pallas_call | solution.py:232
  179.6 11.7 %collective-permute-done.9 = bf16[512,1536]{1,0:T(8,128)(2,1)} collective-permute-done((bf16[512,1536]{1,0:T(8,128)(2,1)S(1)}, bf16[512,1536]{1,0:T(8,128)(2,1)}, u32[]{:S(2)}, u32[]{:S(2)}) %collective-permute-start.9) | collective-permute-done | bytes 1572896 | tf_op jit(solution)/shard_map/ppermute | solution.py:26
  191.3 1.5 copy-done
  192.8 17.8 %shard_map.114 = (f32[2,512,128]{2,1,0:T(8,128)}, f32[2,8,512]{2,1,0:T(8,128)}, bf16[2,512,128]{2,1,0:T(8,128)(2,1)}, f32[2,8,512]{2,1,0:T(8,128)}) custom-call(s32[4]{0:T(128)} %pad_add_fusion.spot, bf16[2,512,128]{2,1,0:T(8,128)(2,1)} %shard_map.109.here_ref, bf16[2,512,128]{2,1,0:T(8,128)(2,1)} %collective-permute-done.1.there_ref, ...), custom_call_target="tpu_custom_call" | custom-call | flops 6442450944 | bytes 3145728 | tf_op jit(solution)/shard_map/pallas_call | solution.py:232
  210.8 3.2 %collective-permute-start.11 = (bf16[2,512,128]{2,1,0:T(8,128)(2,1)}, bf16[2,512,128]{2,1,0:T(8,128)(2,1)S(1)}, u32[]{:S(2)}, u32[]{:S(2)}) collective-permute-start(bf16[2,512,128]{2,1,0:T(8,128)(2,1)} %get-tuple-element.51), channel_id=1, source_target_pairs={{0,16},{1,17},{2,18},{3,19},{4,20},{5,21},{6,22},{7,23},{8,24},{9,... | collective-permute-start | bytes 786440 | tf_op jit(solution)/shard_map/ppermute | solution.py:26
  214.1 2.5 collective-permute-done.10
  216.6 0.8 add_divide_fusion
  217.4 2.0 collective-permute-done.11
  219.4 1.4 add_convert_fusion.2
  220.9 1.5 collective-permute-start.12
  222.4 1.6 broadcast_select_fusion.1
  224.6 2.2 collective-permute-start.13
  226.9 2.2 collective-permute-done.12
  229.1 6.7 %collective-permute-done.13 = bf16[512,256]{1,0:T(8,128)(2,1)S(1)} collective-permute-done((bf16[512,256]{1,0:T(8,128)(2,1)S(1)}, bf16[512,256]{1,0:T(8,128)(2,1)S(1)}, u32[]{:S(2)}, u32[]{:S(2)}) %collective-permute-start.13) | collective-permute-done | bytes 262176 | tf_op jit(solution)/shard_map/ppermute | solution.py:26
  236.1 1.8 fusion.4
  238.1 1.3 collective-permute-start.15
  239.3 2.1 collective-permute-start.17
  241.4 1.5 collective-permute-start.16
  242.9 8.1 %collective-permute-done.15 = bf16[128,1536]{1,0:T(8,128)(2,1)S(1)} collective-permute-done((bf16[128,1536]{1,0:T(8,128)(2,1)S(1)}, bf16[128,1536]{1,0:T(8,128)(2,1)S(1)}, u32[]{:S(2)}, u32[]{:S(2)}) %collective-permute-start.15) | collective-permute-done | bytes 393248 | tf_op jit(solution)/shard_map/ppermute | solution.py:26
  251.0 3.0 %collective-permute-done.17 = bf16[128,1536]{1,0:T(8,128)(2,1)} collective-permute-done((bf16[128,1536]{1,0:T(8,128)(2,1)S(1)}, bf16[128,1536]{1,0:T(8,128)(2,1)}, u32[]{:S(2)}, u32[]{:S(2)}) %collective-permute-start.17) | collective-permute-done | bytes 393248 | tf_op jit(solution)/shard_map/ppermute | solution.py:26
  254.1 1.3 collective-permute-done.16
  255.4 1.3 add_convert_fusion.1
  256.9 1.2 collective-permute-start.3
  258.2 2.1 collective-permute-start.21
  260.8 2.3 collective-permute-start.19
  263.2 5.5 %collective-permute-done.19 = bf16[32,1536]{1,0:T(8,128)(2,1)S(1)} collective-permute-done((bf16[32,1536]{1,0:T(8,128)(2,1)S(1)}, bf16[32,1536]{1,0:T(8,128)(2,1)S(1)}, u32[]{:S(2)}, u32[]{:S(2)}) %collective-permute-start.19) | collective-permute-done | bytes 98336 | tf_op jit(solution)/shard_map/ppermute | solution.py:35
  268.8 0.9 fusion.11
  (62 shorter events, 3.0 us)
Async XLA Ops:
  6.5 4.2 %copy-start.7 = (bf16[1,128,6144]{2,1,0:T(8,128)(2,1)S(1)}, bf16[1,128,6144]{2,1,0:T(8,128)(2,1)}, u32[]{:S(2)}) copy-start(bf16[1,128,6144]{2,1,0:T(8,128)(2,1)} %param.18) | copy-start | bytes 4718596
  6.5 123.6 %all-gather.2.cloned.1.call-start = ((), (), s32[]{:S(2)}) async-start(), calls=%async_computation.2 | async-start | bytes 6684672 | tf_op jit(solution)/shard_map/all_gather | solution.py:287
  18.6 7.7 %copy-start.3 = (bf16[1,6144,128]{2,1,0:T(8,128)(2,1)S(1)}, bf16[1,6144,128]{2,1,0:T(8,128)(2,1)}, u32[]{:S(2)}) copy-start(bf16[1,6144,128]{2,1,0:T(8,128)(2,1)} %param.15) | copy-start | bytes 4718596
  18.6 11.7 %copy-start.4 = (bf16[1,6144,128]{2,1,0:T(8,128)(2,1)S(1)}, bf16[1,6144,128]{2,1,0:T(8,128)(2,1)}, u32[]{:S(2)}) copy-start(bf16[1,6144,128]{2,1,0:T(8,128)(2,1)} %param.16) | copy-start | bytes 4718596
  18.6 124.0 %all-to-all-start.1 = ((bf16[16,4,256,128]{3,2,1,0:T(8,128)(2,1)}), bf16[16,4,256,128]{3,2,1,0:T(8,128)(2,1)}, u32[]{:S(2)}, u32[]{:S(2)}) async-start(bf16[16,4,256,128]{3,2,1,0:T(8,128)(2,1)} %shard_map.112), calls=%async_computation.1 | async-start | bytes 8388608 | tf_op jit(solution)/shard_map/all_to_all | solution.py:278
  26.4 39.3 %collective-permute-start = (bf16[6144,128]{1,0:T(8,128)(2,1)S(1)}, bf16[6144,128]{1,0:T(8,128)(2,1)S(1)}, u32[]{:S(2)}, u32[]{:S(2)}) collective-permute-start(bf16[6144,128]{1,0:T(8,128)(2,1)S(1)} %bitcast.43), channel_id=1, source_target_pairs={{0,16},{1,17},{2,18},{3,19},{4,20},{5,21},{6,22},{7,23},{8,24},{9,... | collective-permute-start | bytes 4718600 | tf_op jit(solution)/shard_map/ppermute | solution.py:26
  30.3 112.3 %collective-permute-start.4 = (bf16[6144,128]{1,0:T(8,128)(2,1)S(1)}, bf16[6144,128]{1,0:T(8,128)(2,1)}, u32[]{:S(2)}, u32[]{:S(2)}) collective-permute-start(bf16[6144,128]{1,0:T(8,128)(2,1)S(1)} %bitcast.45), channel_id=1, source_target_pairs={{0,16},{1,17},{2,18},{3,19},{4,20},{5,21},{6,22},{7,23},{8,24},{9,... | collective-permute-start | bytes 4718600 | tf_op jit(solution)/shard_map/ppermute | solution.py:26
  30.4 112.2 %collective-permute-start.5 = (bf16[6144,128]{1,0:T(8,128)(2,1)}, bf16[6144,128]{1,0:T(8,128)(2,1)}, u32[]{:S(2)}, u32[]{:S(2)}) collective-permute-start(bf16[6144,128]{1,0:T(8,128)(2,1)} %bitcast.46), channel_id=1, source_target_pairs={{0,16},{1,17},{2,18},{3,19},{4,20},{5,21},{6,22},{7,23},{8,24},{9,... | collective-permute-start | bytes 4718600 | tf_op jit(solution)/shard_map/ppermute | solution.py:26
  33.8 104.1 %collective-permute-start.8 = (bf16[128,1536]{1,0:T(8,128)(2,1)}, bf16[128,1536]{1,0:T(8,128)(2,1)}, u32[]{:S(2)}, u32[]{:S(2)}) collective-permute-start(bf16[128,1536]{1,0:T(8,128)(2,1)} %get-tuple-element.58), channel_id=1, source_target_pairs={{0,3},{1,0},{2,1},{3,2},{4,7},{5,4},{6,5},{7,6},{8,11},{9,8},{10,9... | collective-permute-start | bytes 1179656 | tf_op jit(solution)/shard_map/ppermute | solution.py:26
  34.0 108.6 %collective-permute-start.6 = (bf16[128,1536]{1,0:T(8,128)(2,1)}, bf16[128,1536]{1,0:T(8,128)(2,1)}, u32[]{:S(2)}, u32[]{:S(2)}) collective-permute-start(bf16[128,1536]{1,0:T(8,128)(2,1)} %get-tuple-element.59), channel_id=1, source_target_pairs={{0,1},{1,2},{2,3},{3,0},{4,5},{5,6},{6,7},{7,4},{8,9},{9,10},{10,1... | collective-permute-start | bytes 1179656 | tf_op jit(solution)/shard_map/ppermute | solution.py:26
  65.6 1.2 copy-start.5
  66.8 75.8 %collective-permute-start.7 = (bf16[128,1536]{1,0:T(8,128)(2,1)}, bf16[128,1536]{1,0:T(8,128)(2,1)S(1)}, u32[]{:S(2)}, u32[]{:S(2)}) collective-permute-start(bf16[128,1536]{1,0:T(8,128)(2,1)} %get-tuple-element.61), channel_id=1, source_target_pairs={{0,2},{1,3},{2,0},{3,1},{4,6},{5,7},{6,4},{7,5},{8,10},{9,11},{10,... | collective-permute-start | bytes 1179656 | tf_op jit(solution)/shard_map/ppermute | solution.py:26
  137.9 16.0 %collective-permute-start.1 = (bf16[2,512,128]{2,1,0:T(8,128)(2,1)}, bf16[2,512,128]{2,1,0:T(8,128)(2,1)}, u32[]{:S(2)}, u32[]{:S(2)}) collective-permute-start(bf16[2,512,128]{2,1,0:T(8,128)(2,1)} %shard_map.109.here_ref), channel_id=1, source_target_pairs={{0,16},{1,17},{2,18},{3,19},{4,20},{5,21},{6,22},{7,23},{8,24},{9,... | collective-permute-start | bytes 786440 | tf_op jit(solution)/shard_map/ppermute | solution.py:26
  142.7 48.6 %all-to-all-start = ((bf16[16,4,160,128]{3,2,1,0:T(8,128)(2,1)}), bf16[16,4,160,128]{3,2,1,0:T(8,128)(2,1)S(1)}, u32[]{:S(2)}, u32[]{:S(2)}) async-start(bf16[16,4,160,128]{3,2,1,0:T(8,128)(2,1)} %shard_map.110), calls=%async_computation | async-start | bytes 5242880 | tf_op jit(solution)/shard_map/all_to_all | solution.py:278
  153.9 10.0 %copy-start.1 = (bf16[512,1536]{1,0:T(8,128)(2,1)}, bf16[512,1536]{1,0:T(8,128)(2,1)S(1)}, u32[]{:S(2)}) copy-start(bf16[512,1536]{1,0:T(8,128)(2,1)S(1)} %constant_dynamic-update-slice_fusion) | copy-start | bytes 4718596
  153.9 37.3 %collective-permute-start.9 = (bf16[512,1536]{1,0:T(8,128)(2,1)S(1)}, bf16[512,1536]{1,0:T(8,128)(2,1)}, u32[]{:S(2)}, u32[]{:S(2)}) collective-permute-start(bf16[512,1536]{1,0:T(8,128)(2,1)S(1)} %constant_dynamic-update-slice_fusion), channel_id=1, source_target_pairs={{0,16},{1,17},{2,18},{3,19},{4,20},{5,21},{6,22},{7,23},{8,24},{9,... | collective-permute-start | bytes 4718600 | tf_op jit(solution)/shard_map/ppermute | solution.py:26
  191.3 1.5 copy-start
  210.5 11.9 %copy-start.2 = (bf16[512,1536]{1,0:T(8,128)(2,1)S(1)}, bf16[512,1536]{1,0:T(8,128)(2,1)}, u32[]{:S(2)}) copy-start(bf16[512,1536]{1,0:T(8,128)(2,1)} %copy-done.1) | copy-start | bytes 4718596
  210.5 6.0 %collective-permute-start.10 = (f32[2,8,512]{2,1,0:T(8,128)}, f32[2,8,512]{2,1,0:T(8,128)S(1)}, u32[]{:S(2)}, u32[]{:S(2)}) collective-permute-start(f32[2,8,512]{2,1,0:T(8,128)} %get-tuple-element.49), channel_id=1, source_target_pairs={{0,16},{1,17},{2,18},{3,19},{4,20},{5,21},{6,22},{7,23},{8,24},{9,... | collective-permute-start | bytes 98312 | tf_op jit(solution)/shard_map/ppermute | solution.py:26
  210.8 8.6 %collective-permute-start.11 = (bf16[2,512,128]{2,1,0:T(8,128)(2,1)}, bf16[2,512,128]{2,1,0:T(8,128)(2,1)S(1)}, u32[]{:S(2)}, u32[]{:S(2)}) collective-permute-start(bf16[2,512,128]{2,1,0:T(8,128)(2,1)} %get-tuple-element.51), channel_id=1, source_target_pairs={{0,16},{1,17},{2,18},{3,19},{4,20},{5,21},{6,22},{7,23},{8,24},{9,... | collective-permute-start | bytes 786440 | tf_op jit(solution)/shard_map/ppermute | solution.py:26
  220.9 8.2 %collective-permute-start.12 = (bf16[512,256]{1,0:T(8,128)(2,1)S(1)}, bf16[512,256]{1,0:T(8,128)(2,1)S(1)}, u32[]{:S(2)}, u32[]{:S(2)}) collective-permute-start(bf16[512,256]{1,0:T(8,128)(2,1)S(1)} %pad_maximum_fusion), channel_id=1, source_target_pairs={{0,1},{1,2},{2,3},{3,0},{4,5},{5,6},{6,7},{7,4},{8,9},{9,10},{10,1... | collective-permute-start | bytes 786440 | tf_op jit(solution)/shard_map/ppermute | solution.py:26
  224.0 11.9 %collective-permute-start.14 = (bf16[512,256]{1,0:T(8,128)(2,1)S(1)}, bf16[512,256]{1,0:T(8,128)(2,1)S(1)}, u32[]{:S(2)}, u32[]{:S(2)}) collective-permute-start(bf16[512,256]{1,0:T(8,128)(2,1)S(1)} %pad_maximum_fusion), channel_id=1, source_target_pairs={{0,3},{1,0},{2,1},{3,2},{4,7},{5,4},{6,5},{7,6},{8,11},{9,8},{10,9... | collective-permute-start | bytes 786440 | tf_op jit(solution)/shard_map/ppermute | solution.py:26
  224.6 11.2 %collective-permute-start.13 = (bf16[512,256]{1,0:T(8,128)(2,1)S(1)}, bf16[512,256]{1,0:T(8,128)(2,1)S(1)}, u32[]{:S(2)}, u32[]{:S(2)}) collective-permute-start(bf16[512,256]{1,0:T(8,128)(2,1)S(1)} %pad_maximum_fusion), channel_id=1, source_target_pairs={{0,2},{1,3},{2,0},{3,1},{4,6},{5,7},{6,4},{7,5},{8,10},{9,11},{10,... | collective-permute-start | bytes 786440 | tf_op jit(solution)/shard_map/ppermute | solution.py:26
  238.1 20.0 %copy-start.6 = (bf16[1,32,6144]{2,1,0:T(8,128)(2,1)S(1)}, bf16[1,32,6144]{2,1,0:T(8,128)(2,1)}, u32[]{:S(2)}) copy-start(bf16[1,32,6144]{2,1,0:T(8,128)(2,1)} %param.11) | copy-start | bytes 1179652
  238.1 13.0 %collective-permute-start.15 = (bf16[128,1536]{1,0:T(8,128)(2,1)S(1)}, bf16[128,1536]{1,0:T(8,128)(2,1)S(1)}, u32[]{:S(2)}, u32[]{:S(2)}) collective-permute-start(bf16[128,1536]{1,0:T(8,128)(2,1)S(1)} %get-tuple-element.55), channel_id=1, source_target_pairs={{0,4},{1,5},{2,6},{3,7},{4,8},{5,9},{6,10},{7,11},{8,12},{9,13},{1... | collective-permute-start | bytes 1179656 | tf_op jit(solution)/shard_map/ppermute | solution.py:26
  239.3 14.7 %collective-permute-start.17 = (bf16[128,1536]{1,0:T(8,128)(2,1)S(1)}, bf16[128,1536]{1,0:T(8,128)(2,1)}, u32[]{:S(2)}, u32[]{:S(2)}) collective-permute-start(bf16[128,1536]{1,0:T(8,128)(2,1)S(1)} %get-tuple-element.56), channel_id=1, source_target_pairs={{0,12},{1,13},{2,14},{3,15},{4,0},{5,1},{6,2},{7,3},{8,4},{9,5},{1... | collective-permute-start | bytes 1179656 | tf_op jit(solution)/shard_map/ppermute | solution.py:26
  241.4 14.0 %collective-permute-start.16 = (bf16[128,1536]{1,0:T(8,128)(2,1)S(1)}, bf16[128,1536]{1,0:T(8,128)(2,1)}, u32[]{:S(2)}, u32[]{:S(2)}) collective-permute-start(bf16[128,1536]{1,0:T(8,128)(2,1)S(1)} %get-tuple-element.57), channel_id=1, source_target_pairs={{0,8},{1,9},{2,10},{3,11},{4,12},{5,13},{6,14},{7,15},{8,0},{9,1},... | collective-permute-start | bytes 1179656 | tf_op jit(solution)/shard_map/ppermute | solution.py:26
  251.0 5.8 %copy-start.8 = (f32[1,6144]{1,0:T(1,128)S(1)}, f32[1,6144]{1,0:T(1,128)}, u32[]{:S(2)}) copy-start(f32[1,6144]{1,0:T(1,128)} %param.14) | copy-start | bytes 73732
  256.7 4.1 %collective-permute-start.18 = (bf16[32,1536]{1,0:T(8,128)(2,1)S(1)}, bf16[32,1536]{1,0:T(8,128)(2,1)S(1)}, u32[]{:S(2)}, u32[]{:S(2)}) collective-permute-start(bf16[32,1536]{1,0:T(8,128)(2,1)S(1)} %get-tuple-element.65), channel_id=1, source_target_pairs={{0,32},{1,33},{2,34},{3,35},{4,36},{5,37},{6,38},{7,39},{8,40},{9,... | collective-permute-start | bytes 294920 | tf_op jit(solution)/shard_map/ppermute | solution.py:35
  256.9 11.9 %collective-permute-start.3 = (f32[1,6144]{1,0:T(1,128)S(1)}, f32[1,6144]{1,0:T(1,128)S(1)}, u32[]{:S(2)}, u32[]{:S(2)}) collective-permute-start(f32[1,6144]{1,0:T(1,128)S(1)} %copy-done.8), channel_id=1, source_target_pairs={{0,32},{32,64},{64,96},{96,0},{1,33},{33,65},{65,97},{97,1},{2,34}... | collective-permute-start | bytes 73736 | tf_op jit(solution)/shard_map/ppermute | solution.py:41
  258.0 10.7 %collective-permute-start.2 = (bf16[32,6144]{1,0:T(8,128)(2,1)S(1)}, bf16[32,6144]{1,0:T(8,128)(2,1)S(1)}, u32[]{:S(2)}, u32[]{:S(2)}) collective-permute-start(bf16[32,6144]{1,0:T(8,128)(2,1)S(1)} %bitcast.48), channel_id=1, source_target_pairs={{0,32},{32,64},{64,96},{96,0},{1,33},{33,65},{65,97},{97,1},{2,34}... | collective-permute-start | bytes 1179656 | tf_op jit(solution)/shard_map/ppermute | solution.py:41
  258.2 10.5 %collective-permute-start.21 = (bf16[32,1536]{1,0:T(8,128)(2,1)S(1)}, bf16[32,1536]{1,0:T(8,128)(2,1)S(1)}, u32[]{:S(2)}, u32[]{:S(2)}) collective-permute-start(bf16[32,1536]{1,0:T(8,128)(2,1)S(1)} %get-tuple-element.62), channel_id=1, source_target_pairs={{0,35},{1,32},{2,33},{3,34},{4,39},{5,36},{6,37},{7,38},{8,43},{9,... | collective-permute-start | bytes 294920 | tf_op jit(solution)/shard_map/ppermute | solution.py:35
  260.3 8.4 %collective-permute-start.20 = (bf16[32,1536]{1,0:T(8,128)(2,1)S(1)}, bf16[32,1536]{1,0:T(8,128)(2,1)S(1)}, u32[]{:S(2)}, u32[]{:S(2)}) collective-permute-start(bf16[32,1536]{1,0:T(8,128)(2,1)S(1)} %get-tuple-element.63), channel_id=1, source_target_pairs={{0,34},{1,35},{2,32},{3,33},{4,38},{5,39},{6,36},{7,37},{8,42},{9,... | collective-permute-start | bytes 294920 | tf_op jit(solution)/shard_map/ppermute | solution.py:35
  260.8 7.9 %collective-permute-start.19 = (bf16[32,1536]{1,0:T(8,128)(2,1)S(1)}, bf16[32,1536]{1,0:T(8,128)(2,1)S(1)}, u32[]{:S(2)}, u32[]{:S(2)}) collective-permute-start(bf16[32,1536]{1,0:T(8,128)(2,1)S(1)} %get-tuple-element.64), channel_id=1, source_target_pairs={{0,33},{1,34},{2,35},{3,32},{4,37},{5,38},{6,39},{7,36},{8,41},{9,... | collective-permute-start | bytes 294920 | tf_op jit(solution)/shard_map/ppermute | solution.py:35
Sparse Core Ops, SparseCore 0:
  10.7 119.3 all-gather.1

commit v5 on v4

--- a/solution.py
+++ b/solution.py
@@ -296,7 +296,7 @@
     normed, weights, w_parts = lax.optimization_barrier((normed, weights, w_parts))
     w_plane = jnp.concatenate(w_parts, axis=0)
 
-    early = 8 * rows
+    early = 6 * rows
     stale_first = stale_share(stale_laid(0, early, *w_slices))
     stale_second = stale_share(stale_laid(early, length - early), normed)
 

time: 279 us -> 276 us (0.989)
    ppermute x16, waiting for transfers between devices: 67.4 us -> 123 us  [moved(): return lax.ppermute(value, 'seq', pairs)]
    all_gather x1, waiting for transfers between devices: 55.1 us -> 0.01 us  [body(): lax.all_gather(normed, 'seq', axis=0, tiled=True, axis_index_groups=planes)]
  transfers between devices with their start and end apart: 25 -> 25, of which waited for: 12 -> 16; matrix products, arithmetic and copies ran while one was open for 2% -> 2% of each run, Pallas kernels for 16% -> 16%
where the time goes in v5:
time: 276 us; the launch traced here: 275 us
  waiting for transfers between devices  130 us (47%)
  Pallas kernels  62.8 us (23%)
  starting transfers between devices  50.6 us (18%)
  between operations  14.5 us (5%)
  other arithmetic  9.2 us (3%)
  local copies, waits for them, and re-layouts  6.31 us (2%)
    ppermute x16, waiting for transfers between devices, moved(): return lax.ppermute(value, 'seq', pairs)  123 us
    pallas_call x2, Pallas kernels, attend(): pl.pallas_call(functools.partial(attend_kernel, fresh=fresh is not None,...  33.5 us
    ppermute x16, starting transfers between devices, moved(): return lax.ppermute(value, 'seq', pairs)  30.7 us
    pallas_call x2, Pallas kernels, project(): pl.pallas_call(functools.partial(project_kernel, scale=scale), out_shape=...  17.4 us
    all_to_all x2, starting transfers between devices, stale_share(): lax.all_to_all(laid, 'seq', split_axis=0, concat_axis=0, tiled=True, axis...  14.7 us
    pallas_call x2, Pallas kernels, lay_out(): pl.pallas_call(lay_out_kernel, grid=(length // rows,), out_shape=jax.Shap...  11.8 us
    ppermute x4, waiting for transfers between devices, onward(): return lax.ppermute(value, ('section', 'seq'), pairs)  6.72 us
  transfers between devices with their start and end apart: 25, of which 16 were waited for; matrix products, arithmetic and copies ran while one was open for 2% of the time, Pallas kernels for 16%

profile of v5, /device:TPU:2, one launch (start us, length us, event | category | flops | bytes accessed | tf_op | source)
XLA Modules:
  0.0 274.9 jit_solution(8026970991167178995)
XLA Ops:
  6.5 0.9 broadcast_add_fusion
  7.4 1.2 fusion.7
  8.6 2.0 fusion.10
  10.7 1.1 dynamic-slice_bitcast_fusion
  11.8 5.5 %shard_map.112 = bf16[16,4,192,128]{3,2,1,0:T(8,128)(2,1)} custom-call(s32[1]{0:T(128)} %bitcast.1.turn, bf16[416,4096]{1,0:T(8,128)(2,1)} %bitcast.38, bf16[416,4096]{1,0:T(8,128)(2,1)} %bitcast.40), custom_call_target="tpu_custom_call" | custom-call | bytes 6291456 | tf_op jit(solution)/shard_map/pallas_call | solution.py:61
  17.3 7.5 %all-to-all-start.1 = ((bf16[16,4,192,128]{3,2,1,0:T(8,128)(2,1)}), bf16[16,4,192,128]{3,2,1,0:T(8,128)(2,1)S(1)}, u32[]{:S(2)}, u32[]{:S(2)}) async-start(bf16[16,4,192,128]{3,2,1,0:T(8,128)(2,1)} %shard_map.112), calls=%async_computation.1 | async-start | bytes 6291456 | tf_op jit(solution)/shard_map/all_to_all | solution.py:278
  24.8 3.9 %collective-permute-start = (bf16[6144,128]{1,0:T(8,128)(2,1)}, bf16[6144,128]{1,0:T(8,128)(2,1)}, u32[]{:S(2)}, u32[]{:S(2)}) collective-permute-start(bf16[6144,128]{1,0:T(8,128)(2,1)} %bitcast.42), channel_id=1, source_target_pairs={{0,16},{1,17},{2,18},{3,19},{4,20},{5,21},{6,22},{7,23},{8,24},{9,... | collective-permute-start | bytes 4718600 | tf_op jit(solution)/shard_map/ppermute | solution.py:26
  28.7 3.4 %collective-permute-start.5 = (bf16[6144,128]{1,0:T(8,128)(2,1)}, bf16[6144,128]{1,0:T(8,128)(2,1)}, u32[]{:S(2)}, u32[]{:S(2)}) collective-permute-start(bf16[6144,128]{1,0:T(8,128)(2,1)} %bitcast.46), channel_id=1, source_target_pairs={{0,16},{1,17},{2,18},{3,19},{4,20},{5,21},{6,22},{7,23},{8,24},{9,... | collective-permute-start | bytes 4718600 | tf_op jit(solution)/shard_map/ppermute | solution.py:26
  32.2 1.5 collective-permute-start.6
  34.4 49.8 %collective-permute-done.6 = bf16[128,1536]{1,0:T(8,128)(2,1)} collective-permute-done((bf16[128,1536]{1,0:T(8,128)(2,1)}, bf16[128,1536]{1,0:T(8,128)(2,1)}, u32[]{:S(2)}, u32[]{:S(2)}) %collective-permute-start.6) | collective-permute-done | bytes 393248 | tf_op jit(solution)/shard_map/ppermute | solution.py:26
  84.2 6.3 %shard_map.110 = bf16[16,4,224,128]{3,2,1,0:T(8,128)(2,1)} custom-call(s32[1]{0:T(128)} %bitcast.1.turn, bf16[416,4096]{1,0:T(8,128)(2,1)} %bitcast.39, bf16[416,4096]{1,0:T(8,128)(2,1)} %bitcast.41), custom_call_target="tpu_custom_call" | custom-call | bytes 7340032 | tf_op jit(solution)/shard_map/pallas_call | solution.py:61
  90.5 17.8 %collective-permute-done.8 = bf16[128,1536]{1,0:T(8,128)(2,1)} collective-permute-done((bf16[128,1536]{1,0:T(8,128)(2,1)}, bf16[128,1536]{1,0:T(8,128)(2,1)}, u32[]{:S(2)}, u32[]{:S(2)}) %collective-permute-start.8) | collective-permute-done | bytes 393248 | tf_op jit(solution)/shard_map/ppermute | solution.py:26
  108.3 21.9 %collective-permute-done.5.refs_3_ = bf16[6144,128]{1,0:T(8,128)(2,1)} collective-permute-done((bf16[6144,128]{1,0:T(8,128)(2,1)}, bf16[6144,128]{1,0:T(8,128)(2,1)}, u32[]{:S(2)}, u32[]{:S(2)}) %collective-permute-start.5) | collective-permute-done | bytes 1572896 | tf_op jit(solution)/shard_map/ppermute | solution.py:26
  130.2 1.6 copy-done
  131.8 7.2 %all-to-all-start = ((bf16[16,4,224,128]{3,2,1,0:T(8,128)(2,1)}), bf16[16,4,224,128]{3,2,1,0:T(8,128)(2,1)}, u32[]{:S(2)}, u32[]{:S(2)}) async-start(bf16[16,4,224,128]{3,2,1,0:T(8,128)(2,1)} %shard_map.110), calls=%async_computation | async-start | bytes 7340032 | tf_op jit(solution)/shard_map/all_to_all | solution.py:278
  140.3 7.8 %shard_map.109.here_ref = bf16[2,512,128]{2,1,0:T(8,128)(2,1)} custom-call(s32[4]{0:T(128)} %pad_add_fusion.spot, bf16[512,6144]{1,0:T(8,128)(2,1)} %all-gather.2.cloned.1.call-done.x_hbm, bf16[6144,128]{1,0:T(8,128)(2,1)} %bitcast.43, bf16[6144,128]{1,0:T(8,128)(2,1)} %collective-permute-done.refs_1_), custom_call_target="tpu_custom_call" | custom-call | flops 1610612736 | bytes 9699328 | tf_op jit(solution)/shard_map/pallas_call | solution.py:100
  148.1 3.3 %collective-permute-start.1 = (bf16[2,512,128]{2,1,0:T(8,128)(2,1)}, bf16[2,512,128]{2,1,0:T(8,128)(2,1)S(1)}, u32[]{:S(2)}, u32[]{:S(2)}) collective-permute-start(bf16[2,512,128]{2,1,0:T(8,128)(2,1)} %shard_map.109.here_ref), channel_id=1, source_target_pairs={{0,16},{1,17},{2,18},{3,19},{4,20},{5,21},{6,22},{7,23},{8,24},{9,... | collective-permute-start | bytes 786440 | tf_op jit(solution)/shard_map/ppermute | solution.py:26
  151.4 1.0 constant_dynamic-update-slice_fusion.2
  152.5 1.0 constant_dynamic-update-slice_fusion.1
  153.5 1.0 constant_dynamic-update-slice_fusion
  154.5 1.7 collective-permute-done.1.there_ref
  156.3 3.2 %collective-permute-start.9 = (bf16[512,1536]{1,0:T(8,128)(2,1)S(1)}, bf16[512,1536]{1,0:T(8,128)(2,1)S(1)}, u32[]{:S(2)}, u32[]{:S(2)}) collective-permute-start(bf16[512,1536]{1,0:T(8,128)(2,1)S(1)} %constant_dynamic-update-slice_fusion), channel_id=1, source_target_pairs={{0,16},{1,17},{2,18},{3,19},{4,20},{5,21},{6,22},{7,23},{8,24},{9,... | collective-permute-start | bytes 4718600 | tf_op jit(solution)/shard_map/ppermute | solution.py:26
  159.5 9.7 %shard_map.111.refs_0_ = bf16[4,512,128]{2,1,0:T(8,128)(2,1)} custom-call(s32[4]{0:T(128)} %pad_add_fusion.spot, bf16[512,6144]{1,0:T(8,128)(2,1)} %all-gather.2.cloned.1.call-done.x_hbm, bf16[6144,128]{1,0:T(8,128)(2,1)} %bitcast.45, bf16[6144,128]{1,0:T(8,128)(2,1)} %collective-permute-done.4.refs_1_, bf16[6144,128]{1,0:T(8,128)(2,1)} %bitcast.47, ...), custom_call_target="tpu_custom_call" | custom-call | flops 3221225472 | bytes 13107200 | tf_op jit(solution)/shard_map/pallas_call | solution.py:100
  169.2 13.8 %shard_map.113 = (f32[2,1024,256]{2,1,0:T(8,128)}, f32[2,1024,128]{2,1,0:T(8,128)}) custom-call(s32[4]{0:T(128)} %pad_add_fusion.spot, bf16[2,512,128]{2,1,0:T(8,128)(2,1)} %shard_map.109.here_ref, bf16[2,512,128]{2,1,0:T(8,128)(2,1)} %copy-done.3, bf16[16,4,192,128]{3,2,1,0:T(8,128)(2,1)} %copy-done), custom_call_target="tpu_custom_call" | custom-call | flops 6442450944 | bytes 3145728 | tf_op jit(solution)/shard_map/pallas_call | solution.py:232
  183.0 8.4 %collective-permute-done.9 = bf16[512,1536]{1,0:T(8,128)(2,1)S(1)} collective-permute-done((bf16[512,1536]{1,0:T(8,128)(2,1)S(1)}, bf16[512,1536]{1,0:T(8,128)(2,1)S(1)}, u32[]{:S(2)}, u32[]{:S(2)}) %collective-permute-start.9) | collective-permute-done | bytes 1572896 | tf_op jit(solution)/shard_map/ppermute | solution.py:26
  191.4 19.7 %shard_map.114 = (f32[2,512,128]{2,1,0:T(8,128)}, f32[2,8,512]{2,1,0:T(8,128)}, bf16[2,512,128]{2,1,0:T(8,128)(2,1)}, f32[2,8,512]{2,1,0:T(8,128)}) custom-call(s32[4]{0:T(128)} %pad_add_fusion.spot, bf16[2,512,128]{2,1,0:T(8,128)(2,1)} %shard_map.109.here_ref, bf16[2,512,128]{2,1,0:T(8,128)(2,1)} %copy-done.3, ...), custom_call_target="tpu_custom_call" | custom-call | flops 8589934592 | bytes 4194304 | tf_op jit(solution)/shard_map/pallas_call | solution.py:232
  211.1 2.9 %collective-permute-start.10 = (f32[2,8,512]{2,1,0:T(8,128)}, f32[2,8,512]{2,1,0:T(8,128)S(1)}, u32[]{:S(2)}, u32[]{:S(2)}) collective-permute-start(f32[2,8,512]{2,1,0:T(8,128)} %get-tuple-element.49), channel_id=1, source_target_pairs={{0,16},{1,17},{2,18},{3,19},{4,20},{5,21},{6,22},{7,23},{8,24},{9,... | collective-permute-start | bytes 98312 | tf_op jit(solution)/shard_map/ppermute | solution.py:26
  214.6 2.5 collective-permute-done.10
  217.9 4.2 %collective-permute-done.11 = bf16[2,512,128]{2,1,0:T(8,128)(2,1)S(1)} collective-permute-done((bf16[2,512,128]{2,1,0:T(8,128)(2,1)}, bf16[2,512,128]{2,1,0:T(8,128)(2,1)S(1)}, u32[]{:S(2)}, u32[]{:S(2)}) %collective-permute-start.11) | collective-permute-done | bytes 262176 | tf_op jit(solution)/shard_map/ppermute | solution.py:26
  222.1 1.4 add_convert_fusion.2
  223.6 1.5 collective-permute-start.12
  225.3 1.1 collective-permute-start.13
  226.4 2.5 collective-permute-start.14
  229.0 1.0 collective-permute-done.12
  230.0 3.3 %collective-permute-done.13 = bf16[512,256]{1,0:T(8,128)(2,1)S(1)} collective-permute-done((bf16[512,256]{1,0:T(8,128)(2,1)S(1)}, bf16[512,256]{1,0:T(8,128)(2,1)S(1)}, u32[]{:S(2)}, u32[]{:S(2)}) %collective-permute-start.13) | collective-permute-done | bytes 262176 | tf_op jit(solution)/shard_map/ppermute | solution.py:26
  233.4 2.6 collective-permute-done.14
  236.2 1.8 fusion.4
  238.1 1.6 collective-permute-start.15
  239.7 2.7 collective-permute-start.16
  242.4 1.5 collective-permute-start.17
  243.9 5.5 %collective-permute-done.15 = bf16[128,1536]{1,0:T(8,128)(2,1)S(1)} collective-permute-done((bf16[128,1536]{1,0:T(8,128)(2,1)S(1)}, bf16[128,1536]{1,0:T(8,128)(2,1)S(1)}, u32[]{:S(2)}, u32[]{:S(2)}) %collective-permute-start.15) | collective-permute-done | bytes 393248 | tf_op jit(solution)/shard_map/ppermute | solution.py:26
  249.4 4.3 %collective-permute-done.16 = bf16[128,1536]{1,0:T(8,128)(2,1)} collective-permute-done((bf16[128,1536]{1,0:T(8,128)(2,1)S(1)}, bf16[128,1536]{1,0:T(8,128)(2,1)}, u32[]{:S(2)}, u32[]{:S(2)}) %collective-permute-start.16) | collective-permute-done | bytes 393248 | tf_op jit(solution)/shard_map/ppermute | solution.py:26
  253.8 1.3 add_convert_fusion.1
  255.3 1.0 collective-permute-start.2
  256.5 1.4 collective-permute-start.19
  259.2 1.8 collective-permute-start.21
  261.8 3.6 %collective-permute-done.20 = bf16[32,1536]{1,0:T(8,128)(2,1)S(1)} collective-permute-done((bf16[32,1536]{1,0:T(8,128)(2,1)S(1)}, bf16[32,1536]{1,0:T(8,128)(2,1)S(1)}, u32[]{:S(2)}, u32[]{:S(2)}) %collective-permute-start.20) | collective-permute-done | bytes 98336 | tf_op jit(solution)/shard_map/ppermute | solution.py:35
  265.4 1.8 collective-permute-done.21
  (54 shorter events, 6.9 us)
Async XLA Ops:
  6.5 4.2 %copy-start.2 = (bf16[1,128,6144]{2,1,0:T(8,128)(2,1)S(1)}, bf16[1,128,6144]{2,1,0:T(8,128)(2,1)}, u32[]{:S(2)}) copy-start(bf16[1,128,6144]{2,1,0:T(8,128)(2,1)} %param.18) | copy-start | bytes 4718596
  6.5 123.7 %all-gather.2.cloned.1.call-start = ((), (), s32[]{:S(2)}) async-start(), calls=%async_computation.2 | async-start | bytes 6684672 | tf_op jit(solution)/shard_map/all_gather | solution.py:287
  17.3 112.9 %all-to-all-start.1 = ((bf16[16,4,192,128]{3,2,1,0:T(8,128)(2,1)}), bf16[16,4,192,128]{3,2,1,0:T(8,128)(2,1)S(1)}, u32[]{:S(2)}, u32[]{:S(2)}) async-start(bf16[16,4,192,128]{3,2,1,0:T(8,128)(2,1)} %shard_map.112), calls=%async_computation.1 | async-start | bytes 6291456 | tf_op jit(solution)/shard_map/all_to_all | solution.py:278
  24.8 83.5 %collective-permute-start = (bf16[6144,128]{1,0:T(8,128)(2,1)}, bf16[6144,128]{1,0:T(8,128)(2,1)}, u32[]{:S(2)}, u32[]{:S(2)}) collective-permute-start(bf16[6144,128]{1,0:T(8,128)(2,1)} %bitcast.42), channel_id=1, source_target_pairs={{0,16},{1,17},{2,18},{3,19},{4,20},{5,21},{6,22},{7,23},{8,24},{9,... | collective-permute-start | bytes 4718600 | tf_op jit(solution)/shard_map/ppermute | solution.py:26
  28.6 79.7 %collective-permute-start.4 = (bf16[6144,128]{1,0:T(8,128)(2,1)}, bf16[6144,128]{1,0:T(8,128)(2,1)}, u32[]{:S(2)}, u32[]{:S(2)}) collective-permute-start(bf16[6144,128]{1,0:T(8,128)(2,1)} %bitcast.44), channel_id=1, source_target_pairs={{0,16},{1,17},{2,18},{3,19},{4,20},{5,21},{6,22},{7,23},{8,24},{9,... | collective-permute-start | bytes 4718600 | tf_op jit(solution)/shard_map/ppermute | solution.py:26
  28.7 101.5 %collective-permute-start.5 = (bf16[6144,128]{1,0:T(8,128)(2,1)}, bf16[6144,128]{1,0:T(8,128)(2,1)}, u32[]{:S(2)}, u32[]{:S(2)}) collective-permute-start(bf16[6144,128]{1,0:T(8,128)(2,1)} %bitcast.46), channel_id=1, source_target_pairs={{0,16},{1,17},{2,18},{3,19},{4,20},{5,21},{6,22},{7,23},{8,24},{9,... | collective-permute-start | bytes 4718600 | tf_op jit(solution)/shard_map/ppermute | solution.py:26
  32.2 52.0 %collective-permute-start.6 = (bf16[128,1536]{1,0:T(8,128)(2,1)}, bf16[128,1536]{1,0:T(8,128)(2,1)}, u32[]{:S(2)}, u32[]{:S(2)}) collective-permute-start(bf16[128,1536]{1,0:T(8,128)(2,1)} %get-tuple-element.59), channel_id=1, source_target_pairs={{0,1},{1,2},{2,3},{3,0},{4,5},{5,6},{6,7},{7,4},{8,9},{9,10},{10,1... | collective-permute-start | bytes 1179656 | tf_op jit(solution)/shard_map/ppermute | solution.py:26
  33.6 56.8 %collective-permute-start.7 = (bf16[128,1536]{1,0:T(8,128)(2,1)}, bf16[128,1536]{1,0:T(8,128)(2,1)}, u32[]{:S(2)}, u32[]{:S(2)}) collective-permute-start(bf16[128,1536]{1,0:T(8,128)(2,1)} %get-tuple-element.61), channel_id=1, source_target_pairs={{0,2},{1,3},{2,0},{3,1},{4,6},{5,7},{6,4},{7,5},{8,10},{9,11},{10,... | collective-permute-start | bytes 1179656 | tf_op jit(solution)/shard_map/ppermute | solution.py:26
  84.2 24.1 %collective-permute-start.8 = (bf16[128,1536]{1,0:T(8,128)(2,1)}, bf16[128,1536]{1,0:T(8,128)(2,1)}, u32[]{:S(2)}, u32[]{:S(2)}) collective-permute-start(bf16[128,1536]{1,0:T(8,128)(2,1)} %get-tuple-element.58), channel_id=1, source_target_pairs={{0,3},{1,0},{2,1},{3,2},{4,7},{5,4},{6,5},{7,6},{8,11},{9,8},{10,9... | collective-permute-start | bytes 1179656 | tf_op jit(solution)/shard_map/ppermute | solution.py:26
  130.2 1.6 copy-start
  131.8 59.6 %all-to-all-start = ((bf16[16,4,224,128]{3,2,1,0:T(8,128)(2,1)}), bf16[16,4,224,128]{3,2,1,0:T(8,128)(2,1)}, u32[]{:S(2)}, u32[]{:S(2)}) async-start(bf16[16,4,224,128]{3,2,1,0:T(8,128)(2,1)} %shard_map.110), calls=%async_computation | async-start | bytes 7340032 | tf_op jit(solution)/shard_map/all_to_all | solution.py:278
  148.1 8.2 %collective-permute-start.1 = (bf16[2,512,128]{2,1,0:T(8,128)(2,1)}, bf16[2,512,128]{2,1,0:T(8,128)(2,1)S(1)}, u32[]{:S(2)}, u32[]{:S(2)}) collective-permute-start(bf16[2,512,128]{2,1,0:T(8,128)(2,1)} %shard_map.109.here_ref), channel_id=1, source_target_pairs={{0,16},{1,17},{2,18},{3,19},{4,20},{5,21},{6,22},{7,23},{8,24},{9,... | collective-permute-start | bytes 786440 | tf_op jit(solution)/shard_map/ppermute | solution.py:26
  156.3 12.9 %copy-start.3 = (bf16[2,512,128]{2,1,0:T(8,128)(2,1)}, bf16[2,512,128]{2,1,0:T(8,128)(2,1)S(1)}, u32[]{:S(2)}) copy-start(bf16[2,512,128]{2,1,0:T(8,128)(2,1)S(1)} %collective-permute-done.1.there_ref) | copy-start | bytes 786436
  156.3 35.1 %collective-permute-start.9 = (bf16[512,1536]{1,0:T(8,128)(2,1)S(1)}, bf16[512,1536]{1,0:T(8,128)(2,1)S(1)}, u32[]{:S(2)}, u32[]{:S(2)}) collective-permute-start(bf16[512,1536]{1,0:T(8,128)(2,1)S(1)} %constant_dynamic-update-slice_fusion), channel_id=1, source_target_pairs={{0,16},{1,17},{2,18},{3,19},{4,20},{5,21},{6,22},{7,23},{8,24},{9,... | collective-permute-start | bytes 4718600 | tf_op jit(solution)/shard_map/ppermute | solution.py:26
  211.1 6.0 %collective-permute-start.10 = (f32[2,8,512]{2,1,0:T(8,128)}, f32[2,8,512]{2,1,0:T(8,128)S(1)}, u32[]{:S(2)}, u32[]{:S(2)}) collective-permute-start(f32[2,8,512]{2,1,0:T(8,128)} %get-tuple-element.49), channel_id=1, source_target_pairs={{0,16},{1,17},{2,18},{3,19},{4,20},{5,21},{6,22},{7,23},{8,24},{9,... | collective-permute-start | bytes 98312 | tf_op jit(solution)/shard_map/ppermute | solution.py:26
  214.0 8.1 %collective-permute-start.11 = (bf16[2,512,128]{2,1,0:T(8,128)(2,1)}, bf16[2,512,128]{2,1,0:T(8,128)(2,1)S(1)}, u32[]{:S(2)}, u32[]{:S(2)}) collective-permute-start(bf16[2,512,128]{2,1,0:T(8,128)(2,1)} %get-tuple-element.51), channel_id=1, source_target_pairs={{0,16},{1,17},{2,18},{3,19},{4,20},{5,21},{6,22},{7,23},{8,24},{9,... | collective-permute-start | bytes 786440 | tf_op jit(solution)/shard_map/ppermute | solution.py:26
  223.6 6.4 %collective-permute-start.12 = (bf16[512,256]{1,0:T(8,128)(2,1)S(1)}, bf16[512,256]{1,0:T(8,128)(2,1)S(1)}, u32[]{:S(2)}, u32[]{:S(2)}) collective-permute-start(bf16[512,256]{1,0:T(8,128)(2,1)S(1)} %pad_maximum_fusion), channel_id=1, source_target_pairs={{0,1},{1,2},{2,3},{3,0},{4,5},{5,6},{6,7},{7,4},{8,9},{9,10},{10,1... | collective-permute-start | bytes 786440 | tf_op jit(solution)/shard_map/ppermute | solution.py:26
  225.3 8.1 %collective-permute-start.13 = (bf16[512,256]{1,0:T(8,128)(2,1)S(1)}, bf16[512,256]{1,0:T(8,128)(2,1)S(1)}, u32[]{:S(2)}, u32[]{:S(2)}) collective-permute-start(bf16[512,256]{1,0:T(8,128)(2,1)S(1)} %pad_maximum_fusion), channel_id=1, source_target_pairs={{0,2},{1,3},{2,0},{3,1},{4,6},{5,7},{6,4},{7,5},{8,10},{9,11},{10,... | collective-permute-start | bytes 786440 | tf_op jit(solution)/shard_map/ppermute | solution.py:26
  226.4 9.5 %collective-permute-start.14 = (bf16[512,256]{1,0:T(8,128)(2,1)S(1)}, bf16[512,256]{1,0:T(8,128)(2,1)S(1)}, u32[]{:S(2)}, u32[]{:S(2)}) collective-permute-start(bf16[512,256]{1,0:T(8,128)(2,1)S(1)} %pad_maximum_fusion), channel_id=1, source_target_pairs={{0,3},{1,0},{2,1},{3,2},{4,7},{5,4},{6,5},{7,6},{8,11},{9,8},{10,9... | collective-permute-start | bytes 786440 | tf_op jit(solution)/shard_map/ppermute | solution.py:26
  238.1 17.2 %copy-start.1 = (bf16[1,32,6144]{2,1,0:T(8,128)(2,1)S(1)}, bf16[1,32,6144]{2,1,0:T(8,128)(2,1)}, u32[]{:S(2)}) copy-start(bf16[1,32,6144]{2,1,0:T(8,128)(2,1)} %param.11) | copy-start | bytes 1179652
  238.1 11.3 %collective-permute-start.15 = (bf16[128,1536]{1,0:T(8,128)(2,1)S(1)}, bf16[128,1536]{1,0:T(8,128)(2,1)S(1)}, u32[]{:S(2)}, u32[]{:S(2)}) collective-permute-start(bf16[128,1536]{1,0:T(8,128)(2,1)S(1)} %get-tuple-element.55), channel_id=1, source_target_pairs={{0,4},{1,5},{2,6},{3,7},{4,8},{5,9},{6,10},{7,11},{8,12},{9,13},{1... | collective-permute-start | bytes 1179656 | tf_op jit(solution)/shard_map/ppermute | solution.py:26
  239.7 14.0 %collective-permute-start.16 = (bf16[128,1536]{1,0:T(8,128)(2,1)S(1)}, bf16[128,1536]{1,0:T(8,128)(2,1)}, u32[]{:S(2)}, u32[]{:S(2)}) collective-permute-start(bf16[128,1536]{1,0:T(8,128)(2,1)S(1)} %get-tuple-element.57), channel_id=1, source_target_pairs={{0,8},{1,9},{2,10},{3,11},{4,12},{5,13},{6,14},{7,15},{8,0},{9,1},... | collective-permute-start | bytes 1179656 | tf_op jit(solution)/shard_map/ppermute | solution.py:26
  242.4 11.3 %collective-permute-start.17 = (bf16[128,1536]{1,0:T(8,128)(2,1)S(1)}, bf16[128,1536]{1,0:T(8,128)(2,1)}, u32[]{:S(2)}, u32[]{:S(2)}) collective-permute-start(bf16[128,1536]{1,0:T(8,128)(2,1)S(1)} %get-tuple-element.56), channel_id=1, source_target_pairs={{0,12},{1,13},{2,14},{3,15},{4,0},{5,1},{6,2},{7,3},{8,4},{9,5},{1... | collective-permute-start | bytes 1179656 | tf_op jit(solution)/shard_map/ppermute | solution.py:26
  249.4 6.9 %copy-start.4 = (f32[1,6144]{1,0:T(1,128)S(1)}, f32[1,6144]{1,0:T(1,128)}, u32[]{:S(2)}) copy-start(f32[1,6144]{1,0:T(1,128)} %param.14) | copy-start | bytes 73732
  255.1 4.1 %collective-permute-start.18 = (bf16[32,1536]{1,0:T(8,128)(2,1)S(1)}, bf16[32,1536]{1,0:T(8,128)(2,1)S(1)}, u32[]{:S(2)}, u32[]{:S(2)}) collective-permute-start(bf16[32,1536]{1,0:T(8,128)(2,1)S(1)} %get-tuple-element.65), channel_id=1, source_target_pairs={{0,32},{1,33},{2,34},{3,35},{4,36},{5,37},{6,38},{7,39},{8,40},{9,... | collective-permute-start | bytes 294920 | tf_op jit(solution)/shard_map/ppermute | solution.py:35
  255.3 11.9 %collective-permute-start.2 = (bf16[32,6144]{1,0:T(8,128)(2,1)S(1)}, bf16[32,6144]{1,0:T(8,128)(2,1)S(1)}, u32[]{:S(2)}, u32[]{:S(2)}) collective-permute-start(bf16[32,6144]{1,0:T(8,128)(2,1)S(1)} %bitcast.48), channel_id=1, source_target_pairs={{0,32},{32,64},{64,96},{96,0},{1,33},{33,65},{65,97},{97,1},{2,34}... | collective-permute-start | bytes 1179656 | tf_op jit(solution)/shard_map/ppermute | solution.py:41
  256.3 10.9 %collective-permute-start.3 = (f32[1,6144]{1,0:T(1,128)S(1)}, f32[1,6144]{1,0:T(1,128)S(1)}, u32[]{:S(2)}, u32[]{:S(2)}) collective-permute-start(f32[1,6144]{1,0:T(1,128)S(1)} %copy-done.4), channel_id=1, source_target_pairs={{0,32},{32,64},{64,96},{96,0},{1,33},{33,65},{65,97},{97,1},{2,34}... | collective-permute-start | bytes 73736 | tf_op jit(solution)/shard_map/ppermute | solution.py:41
  256.5 5.3 %collective-permute-start.19 = (bf16[32,1536]{1,0:T(8,128)(2,1)S(1)}, bf16[32,1536]{1,0:T(8,128)(2,1)S(1)}, u32[]{:S(2)}, u32[]{:S(2)}) collective-permute-start(bf16[32,1536]{1,0:T(8,128)(2,1)S(1)} %get-tuple-element.64), channel_id=1, source_target_pairs={{0,33},{1,34},{2,35},{3,32},{4,37},{5,38},{6,39},{7,36},{8,41},{9,... | collective-permute-start | bytes 294920 | tf_op jit(solution)/shard_map/ppermute | solution.py:35
  257.9 7.5 %collective-permute-start.20 = (bf16[32,1536]{1,0:T(8,128)(2,1)S(1)}, bf16[32,1536]{1,0:T(8,128)(2,1)S(1)}, u32[]{:S(2)}, u32[]{:S(2)}) collective-permute-start(bf16[32,1536]{1,0:T(8,128)(2,1)S(1)} %get-tuple-element.63), channel_id=1, source_target_pairs={{0,34},{1,35},{2,32},{3,33},{4,38},{5,39},{6,36},{7,37},{8,42},{9,... | collective-permute-start | bytes 294920 | tf_op jit(solution)/shard_map/ppermute | solution.py:35
  259.2 8.0 %collective-permute-start.21 = (bf16[32,1536]{1,0:T(8,128)(2,1)S(1)}, bf16[32,1536]{1,0:T(8,128)(2,1)S(1)}, u32[]{:S(2)}, u32[]{:S(2)}) collective-permute-start(bf16[32,1536]{1,0:T(8,128)(2,1)S(1)} %get-tuple-element.62), channel_id=1, source_target_pairs={{0,35},{1,32},{2,33},{3,34},{4,39},{5,36},{6,37},{7,38},{8,43},{9,... | collective-permute-start | bytes 294920 | tf_op jit(solution)/shard_map/ppermute | solution.py:35
Sparse Core Ops, SparseCore 0:
  10.7 104.7 all-gather.1
